TPU v7x, 32 devices: a whole 2x2x4 slice. The times are simulated.
32 devices in a mesh: seq: 16 (over z, y, core), head: 2 (over x).
Axes of the slice: x: 2, y: 2, z: 4, core: 2. Of those that a mesh axis runs over, the one named last changes fastest.
Arguments:
- query: bfloat16 [4096, 2048], P('seq', 'head'), may hold values from -40 to 40
- key_in: bfloat16 [4096, 2048], P('seq', 'head'), may hold values from -6 to 6
- value: bfloat16 [4096, 2048], P('seq', 'head'), may hold values from -40 to 40
- cotangent: bfloat16 [4096, 2048], P('seq', 'head'), may hold values from -6 to 6
Outputs:
- output: bfloat16 [4096, 2048], P('seq', 'head')
- grad_query: bfloat16 [4096, 2048], P('seq', 'head')
- grad_key: bfloat16 [4096, 2048], P('seq', 'head')
- grad_value: bfloat16 [4096, 2048], P('seq', 'head')
All inputs are finite; a program needn't handle non-finite values.
Results may differ from a plain program's by a relative error of at most 0.0059.
Values sent between devices are 32-bit elements; how exact they have to be, the bound alone decides.
No kernel may reach another device: no remote copies, remote signals or barrier semaphores. Data moves between devices by JAX's collectives and lax.ppermute only.
A program may use at most 128 MiB of HBM per device.

v0:
```python
import jax
import jax.numpy as jnp
from jax import lax
from jax.sharding import PartitionSpec as P

HEADS = 16
HEAD_DIM = 128


def entering(part, axis, combine, identity, reverse):
    count = lax.axis_size(axis)
    place = lax.axis_index(axis)
    ahead = count - 1 - place if reverse else place
    gathered = lax.all_gather(part, axis)
    state = jnp.zeros_like(part) + jnp.asarray(identity, part.dtype)

    def one(hop, state):
        source = count - 1 - hop if reverse else hop
        return combine(state, lax.dynamic_index_in_dim(gathered, source, 0, False))

    return lax.fori_loop(0, ahead, one, state)


def add_states(earlier, later):
    return earlier + later


def local(query, key_in, value, cotangent):
    tok_rows = query.shape[0]
    heads = query.shape[1] // HEAD_DIM
    width = HEADS * HEAD_DIM
    queries = query.reshape(tok_rows, heads, HEAD_DIM)
    keys = key_in.reshape(tok_rows, heads, HEAD_DIM)
    values = value.reshape(tok_rows, heads, HEAD_DIM)
    cot_rows = cotangent.reshape(tok_rows, heads, HEAD_DIM)
    local_state = jnp.einsum("thd,the->hde", keys, values, preferred_element_type=jnp.float32)
    zero_state = jnp.zeros_like(local_state)
    prefix = entering(local_state, "seq", add_states, zero_state, False)
    prefix_b = prefix.astype(jnp.bfloat16)
    positions = lax.broadcasted_iota(jnp.int32, (tok_rows, tok_rows), 0)
    sources = lax.broadcasted_iota(jnp.int32, (tok_rows, tok_rows), 1)
    causal = (positions >= sources)[None]
    raw = jnp.einsum("thd,shd->hts", queries, keys, preferred_element_type=jnp.float32)
    scores = jnp.where(causal, raw, 0.0).astype(jnp.bfloat16)
    mixed = jnp.einsum("hts,she->the", scores, values, preferred_element_type=jnp.float32)
    mixed = mixed + jnp.einsum(
        "thd,hde->the", queries, prefix_b, preferred_element_type=jnp.float32
    )
    local_square = jnp.sum(mixed * mixed, axis=(1, 2))
    local_dot = jnp.sum(cot_rows * mixed, axis=(1, 2))
    square = lax.psum(local_square, "head")
    dot_sum = lax.psum(local_dot, "head")
    rstd = lax.rsqrt(square / width + 1e-06)
    output = (mixed * rstd[:, None, None]).astype(jnp.bfloat16)
    mean_dot = dot_sum / width
    d_mixed = (
        rstd[:, None, None] * (cot_rows - mixed * (rstd * rstd * mean_dot)[:, None, None])
    ).astype(jnp.bfloat16)
    grad_state = jnp.einsum("thd,the->hde", queries, d_mixed, preferred_element_type=jnp.float32)
    suffix = entering(grad_state, "seq", add_states, zero_state, True)
    suffix_b = suffix.astype(jnp.bfloat16)
    d_raw = jnp.einsum("the,she->hts", d_mixed, values, preferred_element_type=jnp.float32)
    d_scores = jnp.where(causal, d_raw, 0.0).astype(jnp.bfloat16)
    grad_q = jnp.einsum("hts,shd->thd", d_scores, keys, preferred_element_type=jnp.float32)
    grad_q = grad_q + jnp.einsum(
        "the,hde->thd", d_mixed, prefix_b, preferred_element_type=jnp.float32
    )
    grad_k = jnp.einsum("hts,thd->shd", d_scores, queries, preferred_element_type=jnp.float32)
    grad_k = grad_k + jnp.einsum(
        "she,hde->shd", values, suffix_b, preferred_element_type=jnp.float32
    )
    grad_v = jnp.einsum("hts,the->she", scores, d_mixed, preferred_element_type=jnp.float32)
    grad_v = grad_v + jnp.einsum("shd,hde->she", keys, suffix_b, preferred_element_type=jnp.float32)
    flat = heads * HEAD_DIM
    return (
        output.reshape(tok_rows, flat),
        grad_q.astype(jnp.bfloat16).reshape(tok_rows, flat),
        grad_k.astype(jnp.bfloat16).reshape(tok_rows, flat),
        grad_v.astype(jnp.bfloat16).reshape(tok_rows, flat),
    )


def solution(mesh):
    return jax.shard_map(
        local,
        mesh=mesh,
        in_specs=(P("seq", "head"), P("seq", "head"), P("seq", "head"), P("seq", "head")),
        out_specs=(P("seq", "head"), P("seq", "head"), P("seq", "head"), P("seq", "head")),
        check_vma=False,
    )
```

profile of v0, /device:TPU:0, one launch (start us, length us, event | category | flops | bytes accessed | tf_op | source)
XLA Modules:
  0.0 220.0 jit_solution(4778391744788379662)
XLA Ops:
  7.2 1.2 copy.59
  10.0 1.2 copy.37
  12.8 1.5 convolution_bitcast_fusion.5
  14.3 74.1 %all-gather.5.cloned.1.call-done = f32[128,128,128]{2,1,0:T(8,128)} async-done(((f32[8,128,128]{2,1,0:T(8,128)}), f32[128,128,128]{2,1,0:T(8,128)}) %all-gather.5.cloned.1.call-update) | async-done | bytes 8388624 | tf_op jit(solution)/shard_map/all_gather | solution.py:14
  88.4 2.6 %multiply_reduce_fusion = (f32[256]{0:T(256)S(1)}, f32[256]{0:T(256)S(1)}, f32[256,8,128]{0,2,1:T(8,128)}) fusion(f32[256,1024]{0,1:T(8,128)S(1)} %copy.37, f32[256,8,128]{0,2,1:T(8,128)} %convolution_bitcast_fusion.5, f32[8,128,128]{2,1,0:T(8,128)S(1)} %get-tuple-element.83, bf16[256,1024]{1,0:T(8,128)(2,1)S(1)} %copy-done), kind=kOutput, calls=%fused_computation.19 | convolution fusion | flops 68550144 | bytes 4196352 | tf_op jit(solution)/shard_map/thd,hde->the/dot_general | solution.py:46
  91.0 4.9 %all-reduce = (f32[256]{0:T(256)S(1)}, f32[256]{0:T(256)S(1)}) all-reduce(f32[256]{0:T(256)S(1)} %get-tuple-element.98, f32[256]{0:T(256)S(1)} %get-tuple-element.97), channel_id=1, replica_groups=mesh['seq'=16,'head'=2] {'head'}, use_global_device_ids=true, to_apply=%region_3.4 | all-reduce | flops 512 | bytes 4096 | tf_op jit(solution)/shard_map/psum | solution.py:51
  96.0 2.3 %multiply_convert_fusion = (bf16[256,8,128]{0,2,1:T(8,128)(2,1)S(1)}, bf16[256,8,128]{0,2,1:T(8,128)(2,1)}) fusion(f32[256,8,128]{0,2,1:T(8,128)} %get-tuple-element.121, f32[256]{0:T(256)S(1)} %get-tuple-element.119, f32[256]{0:T(256)S(1)} %get-tuple-element.120, f32[256,1024]{0,1:T(8,128)S(1)} %copy.37), kind=kLoop, calls=%fused_computation.18 | loop fusion | flops 1572864 | bytes 3147776 | tf_op jit(solution)/shard_map/convert_element_type | solution.py:58
  102.6 2.0 copy.49
  104.7 1.4 fusion.31
  106.4 83.1 %all-gather.7.cloned.1.call-done = f32[128,128,128]{2,1,0:T(8,128)} async-done(((f32[8,128,128]{2,1,0:T(8,128)}), f32[128,128,128]{2,1,0:T(8,128)}) %all-gather.7.cloned.1.call-update) | async-done | bytes 8388624 | tf_op jit(solution)/shard_map/all_gather | solution.py:14
  189.5 17.9 %while.23 = (s32[]{:T(128)}, f32[8,128,128]{2,1,0:T(8,128)S(1)}, s32[]{:T(128)}, f32[16,8,128,128]{3,2,1,0:T(8,128)}, s32[]{:T(128)}, /*index=5*/s32[]{:T(128)}, s32[]{:T(128)}, s32[]{:T(128)}) while((s32[]{:T(128)}, f32[8,128,128]{2,1,0:T(8,128)S(1)}, s32[]{:T(128)}, f32[16,8,128,128]{3,2,1,0:T(8,128)}, s32[]{:T(128)}, /*index=5*/s32[]{:T(128)}, ...), condition=%wide.region_7.8_spmd, body=%wide.region_6.7_spmd.sunk | while | flops 131078 | bytes 1573007 | solution.py:21
  189.5 1.2 bitcast_add_fusion.5
  190.8 1.2 bitcast_add_fusion.5
  192.0 1.2 bitcast_add_fusion.5
  193.2 1.2 bitcast_add_fusion.5
  194.4 1.2 bitcast_add_fusion.5
  195.5 1.2 bitcast_add_fusion.5
  196.7 1.2 bitcast_add_fusion.5
  202.7 1.2 bitcast_add_fusion.5
  203.9 1.2 bitcast_add_fusion.5
  205.1 1.2 bitcast_add_fusion.5
  206.3 1.2 bitcast_add_fusion.5
  207.5 2.4 %fusion.5 = bf16[8,128,256]{2,1,0:T(8,128)(2,1)} fusion(f32[8,128,256]{2,1,0:T(8,128)} %fusion.31, f32[8,128,128]{2,1,0:T(8,128)S(1)} %get-tuple-element.84, bf16[256,1024]{1,0:T(8,128)(2,1)S(1)} %copy-done.9), kind=kOutput, calls=%fused_computation.16 | convolution fusion | flops 67764224 | bytes 2621440 | tf_op jit(solution)/shard_map/shd,hde->she/dot_general | solution.py:73
  209.8 2.0 copy.51
  (47 shorter events, 13.8 us)
Async XLA Ops:
  7.2 4.1 %copy-start = (bf16[256,1024]{1,0:T(8,128)(2,1)S(1)}, bf16[256,1024]{1,0:T(8,128)(2,1)}, u32[]{:S(2)}) copy-start(bf16[256,1024]{1,0:T(8,128)(2,1)} %param.8) | copy-start | bytes 1572868
  7.2 1.6 copy-start.1
  7.2 81.2 %all-gather.5.cloned.1.call-start = ((), (), s32[]{:S(2)}) async-start(), calls=%async_computation | async-start | bytes 8912896 | tf_op jit(solution)/shard_map/all_gather | solution.py:14
  8.8 2.9 %copy-start.2 = (bf16[256,8,128]{0,2,1:T(8,128)(2,1)}, bf16[256,8,128]{0,2,1:T(8,128)(2,1)S(1)}, u32[]{:S(2)}) copy-start(bf16[256,8,128]{0,2,1:T(8,128)(2,1)S(1)} %copy.33) | copy-start | bytes 1572868
  8.8 2.5 %copy-start.8 = (bf16[256,1024]{1,0:T(8,128)(2,1)S(1)}, bf16[256,1024]{1,0:T(8,128)(2,1)}, u32[]{:S(2)}) copy-start(bf16[256,1024]{1,0:T(8,128)(2,1)} %param.9) | copy-start | bytes 1572868
  9.9 179.5 %all-gather.7.cloned.1.call-start = ((), (), s32[]{:S(2)}) async-start(), calls=%async_computation.1 | async-start | bytes 8912896 | tf_op jit(solution)/shard_map/all_gather | solution.py:14
  11.8 1.1 copy-start.4
  98.2 1.3 copy-start.10
  99.5 1.5 copy-start.3
  101.0 1.6 copy-start.6
  101.5 3.1 %copy-start.5 = (bf16[8,256,256]{2,1,0:T(8,128)(2,1)S(1)}, bf16[8,256,256]{2,1,0:T(8,128)(2,1)}, u32[]{:S(2)}) copy-start(bf16[8,256,256]{2,1,0:T(8,128)(2,1)} %copy-done.4) | copy-start | bytes 3145732
  104.7 1.4 copy-start.7
  189.5 18.0 %copy-start.9 = (bf16[256,1024]{1,0:T(8,128)(2,1)S(1)}, bf16[256,1024]{1,0:T(8,128)(2,1)}, u32[]{:S(2)}) copy-start(bf16[256,1024]{1,0:T(8,128)(2,1)} %param.9) | copy-start | bytes 1572868
Sparse Core Ops, SparseCore 0:
  10.8 77.5 all-gather.4
  99.6 89.7 all-gather.6
where the time goes:
time: 221 us; the launch traced here: 220 us
  waiting for transfers between devices  157 us (71%)
  other arithmetic  19.9 us (9%)
  between operations  14.3 us (6%)
  matrix products  12.3 us (6%)
  local copies, waits for them, and re-layouts  11.1 us (5%)
  blocking collectives  4.92 us (2%)
    all_gather x2, waiting for transfers between devices, entering(): gathered = lax.all_gather(part, axis)  157 us
    add x15, other arithmetic, add_states(): return earlier + later  17.6 us
    unnamed x27, local copies, waits for them, and re-layouts  8.42 us
    psum x1, blocking collectives, local(): square = lax.psum(local_square, 'head')  4.92 us
  transfers between devices with their start and end apart: 2, of which 2 were waited for; matrix products, arithmetic and copies ran while one was open for 5% of the time, Pallas kernels for 0%

commit v1 on v0

v1 whole, which is shorter than its diff:
```python
import jax
import jax.numpy as jnp
from jax import lax
from jax.experimental import pallas as pl
from jax.experimental.pallas import tpu as pltpu
from jax.sharding import PartitionSpec as P

HEAD_DIM = 128
EPS = 1e-06
F32 = jnp.float32
BF16 = jnp.bfloat16


def first_head(quarter, per):
    block = lax.axis_index("seq")
    core = block % 2
    pair = (block // 2) % 2
    if quarter >= 2:
        core = 1 - core
    if quarter % 2:
        pair = 1 - pair
    return (2 * core + pair) * per


def head_columns(quarter, sub, per):
    return pl.ds(pl.multiple_of((first_head(quarter, per) + sub) * HEAD_DIM, HEAD_DIM), HEAD_DIM)


def spots(per, quarters=range(4)):
    return [(quarter, sub, (quarter % 2) * per + sub) for quarter in quarters for sub in range(per)]


def dot(a, b, contract):
    return lax.dot_general(a, b, (contract, ((), ())), preferred_element_type=F32)


def causal(rows):
    return lax.broadcasted_iota(jnp.int32, (rows, rows), 0) >= lax.broadcasted_iota(jnp.int32, (rows, rows), 1)


def call(kernel, outs, args, flops, scratch=()):
    moved = sum(a.size * a.dtype.itemsize for a in (*args, *outs))
    return pl.pallas_call(
        kernel,
        out_shape=outs,
        in_specs=[pl.BlockSpec(memory_space=pltpu.VMEM)] * len(args),
        out_specs=[pl.BlockSpec(memory_space=pltpu.VMEM)] * len(outs),
        scratch_shapes=list(scratch),
        cost_estimate=pl.CostEstimate(flops=int(flops), bytes_accessed=int(moved), transcendentals=0),
        compiler_params=pltpu.CompilerParams(vmem_limit_bytes=16 * 1024 * 1024),
    )(*args)


def like(shape, dtype=F32):
    return jax.ShapeDtypeStruct(tuple(shape), dtype)


def exchange(axis, pairs_of, array):
    count = lax.axis_size(axis)
    return lax.ppermute(array, axis, [(i, pairs_of(i)) for i in range(count)])


def far_scan(total, reverse):
    count = lax.axis_size("seq")
    steps = count // 4
    far = lax.axis_index("seq") // 4
    if reverse:
        far = steps - 1 - far
    before = jnp.zeros_like(total)
    hop = 1
    if steps & (steps - 1) == 0:
        while hop < steps:
            got = exchange("seq", lambda i: i ^ (4 * hop), total)
            before = before + jnp.where((far // hop) % 2 == 1, got, 0.0)
            total = total + got
            hop *= 2
        return before
    while hop < steps:
        up = [(i, i + 4 * hop) for i in range(count - 4 * hop)]
        got = lax.ppermute(total, "seq", [(d, s) for s, d in up] if reverse else up)
        before = before + got
        total = total + got
        hop *= 2
    return before


def scan(keep, send, reverse):
    block = lax.axis_index("seq")
    core, pair = block % 2, (block // 2) % 2
    if reverse:
        core, pair = 1 - core, 1 - pair
    got = exchange("seq", lambda i: i ^ 1, send)
    chip = keep + got
    other = exchange("seq", lambda i: i ^ 2, chip[1])
    before = far_scan(chip[0] + other, reverse)
    theirs = before + jnp.where(pair == 0, chip[0], 0.0)
    mine = before + jnp.where(pair == 1, other, 0.0)
    back = exchange("seq", lambda i: i ^ 2, theirs)
    base = jnp.stack([mine, back])
    away = exchange("seq", lambda i: i ^ 1, base + jnp.where(core == 0, keep, 0.0))
    return base + jnp.where(core == 1, got, 0.0), away


def local(query, key_in, value, cotangent):
    rows, width = query.shape
    heads = width // HEAD_DIM
    per = heads // 4
    features = width * lax.axis_size("head")
    half = (2, per * HEAD_DIM, HEAD_DIM)
    state_flops = heads * rows * HEAD_DIM * HEAD_DIM

    def states_of(quarters):
        def kernel(a_ref, b_ref, out_ref):
            for quarter, sub, _ in spots(per, quarters):
                cols = head_columns(quarter, sub, per)
                out_ref[quarter % 2, sub * HEAD_DIM : (sub + 1) * HEAD_DIM, :] = dot(a_ref[:, cols], b_ref[:, cols], ((0,), (0,)))

        return kernel

    (send,) = call(states_of((2, 3)), [like(half)], (key_in, value), state_flops)
    (keep,) = call(states_of((0, 1)), [like(half)], (key_in, value), state_flops)

    def inner(q_ref, k_ref, v_ref, scores_ref, near_ref):
        mask = causal(rows)
        for head in range(heads):
            cols = slice(head * HEAD_DIM, (head + 1) * HEAD_DIM)
            raw = dot(q_ref[:, cols], k_ref[:, cols], ((1,), (1,)))
            scores = jnp.where(mask, raw, 0.0).astype(BF16)
            scores_ref[head] = scores
            near_ref[:, cols] = dot(scores, v_ref[:, cols], ((1,), (0,)))

    scores, near = call(
        inner,
        [like((heads, rows, rows), BF16), like((rows, width))],
        (query, key_in, value),
        4 * heads * rows * rows * HEAD_DIM,
    )

    own, away = scan(keep, send, False)

    def mix(q_ref, c_ref, near_ref, own_ref, away_ref, mixed_ref, stats_ref):
        square = jnp.zeros((rows, HEAD_DIM), F32)
        along = jnp.zeros((rows, HEAD_DIM), F32)
        for quarter, sub, _ in spots(per):
            cols = head_columns(quarter, sub, per)
            prefix_ref = own_ref if quarter < 2 else away_ref
            prefix = prefix_ref[quarter % 2, sub * HEAD_DIM : (sub + 1) * HEAD_DIM, :].astype(BF16)
            mixed = near_ref[:, cols] + dot(q_ref[:, cols], prefix, ((1,), (0,)))
            mixed_ref[:, cols] = mixed
            square += mixed * mixed
            along += c_ref[:, cols].astype(F32) * mixed
        stats_ref[0:1, :] = jnp.sum(square.T, axis=0, keepdims=True)
        stats_ref[1:2, :] = jnp.sum(along.T, axis=0, keepdims=True)

    mixed, stats = call(
        mix, [like((rows, width)), like((2, rows))], (query, cotangent, near, own, away), 2 * state_flops
    )
    if lax.axis_size("head") == 2:
        stats = stats + exchange("head", lambda i: 1 - i, stats)
    else:
        stats = lax.psum(stats, "head")

    def token_scales(stats_ref):
        rstd = lax.rsqrt(stats_ref[0:1, :] / features + EPS)
        slope = rstd * rstd * (stats_ref[1:2, :] / features)
        return (
            jnp.broadcast_to(rstd, (HEAD_DIM, rows)).T,
            jnp.broadcast_to(slope, (HEAD_DIM, rows)).T,
        )

    def grads_of(quarters):
        def kernel(q_ref, c_ref, mixed_ref, stats_ref, d_ref, out_ref):
            rstd, slope = token_scales(stats_ref)
            for quarter, sub, spot in spots(per, quarters):
                cols = head_columns(quarter, sub, per)
                d_mixed = (rstd * (c_ref[:, cols].astype(F32) - mixed_ref[:, cols] * slope)).astype(BF16)
                d_ref[:, spot * HEAD_DIM : (spot + 1) * HEAD_DIM] = d_mixed
                out_ref[quarter % 2, sub * HEAD_DIM : (sub + 1) * HEAD_DIM, :] = dot(q_ref[:, cols], d_mixed, ((0,), (0,)))

        return kernel

    d_half = like((rows, width // 2), BF16)
    d_send, g_send = call(grads_of((2, 3)), [d_half, like(half)], (query, cotangent, mixed, stats), state_flops)
    d_keep, g_keep = call(grads_of((0, 1)), [d_half, like(half)], (query, cotangent, mixed, stats), state_flops)

    def middle(
        q_ref, k_ref, v_ref, scores_ref, mixed_ref, stats_ref, d_keep_ref, d_send_ref, own_ref, away_ref,
        out_ref, gq_ref, gk_ref, gv_ref,
    ):
        mask = causal(rows)
        rstd, _ = token_scales(stats_ref)
        for quarter, sub, spot in spots(per):
            cols = head_columns(quarter, sub, per)
            d_ref, prefix_ref = (d_keep_ref, own_ref) if quarter < 2 else (d_send_ref, away_ref)
            out_ref[:, cols] = (mixed_ref[:, cols] * rstd).astype(BF16)
            d_mixed = d_ref[:, spot * HEAD_DIM : (spot + 1) * HEAD_DIM]
            prefix = prefix_ref[quarter % 2, sub * HEAD_DIM : (sub + 1) * HEAD_DIM, :].astype(BF16)
            raw = dot(d_mixed, v_ref[:, cols], ((1,), (1,)))
            d_scores = jnp.where(mask, raw, 0.0).astype(BF16)
            gq = dot(d_scores, k_ref[:, cols], ((1,), (0,))) + dot(d_mixed, prefix, ((1,), (1,)))
            gq_ref[:, cols] = gq.astype(BF16)
            gk_ref[:, cols] = dot(d_scores, q_ref[:, cols], ((0,), (0,)))
            gv_ref[:, cols] = dot(scores_ref[first_head(quarter, per) + sub], d_mixed, ((0,), (0,)))

    whole = like((rows, width), BF16)
    output, grad_q, near_k, near_v = call(
        middle,
        [whole, whole, like((rows, width)), like((rows, width))],
        (query, key_in, value, scores, mixed, stats, d_keep, d_send, own, away),
        8 * heads * rows * rows * HEAD_DIM,
    )

    g_own, g_away = scan(g_keep, g_send, True)

    def last(k_ref, v_ref, near_k_ref, near_v_ref, own_ref, away_ref, gk_ref, gv_ref):
        for quarter, sub, _ in spots(per):
            cols = head_columns(quarter, sub, per)
            suffix_ref = own_ref if quarter < 2 else away_ref
            suffix = suffix_ref[quarter % 2, sub * HEAD_DIM : (sub + 1) * HEAD_DIM, :].astype(BF16)
            gk_ref[:, cols] = (near_k_ref[:, cols] + dot(v_ref[:, cols], suffix, ((1,), (1,)))).astype(BF16)
            gv_ref[:, cols] = (near_v_ref[:, cols] + dot(k_ref[:, cols], suffix, ((1,), (0,)))).astype(BF16)

    grad_k, grad_v = call(last, [whole, whole], (key_in, value, near_k, near_v, g_own, g_away), 4 * state_flops)
    return output, grad_q, grad_k, grad_v


def solution(mesh):
    spec = P("seq", "head")
    return jax.shard_map(local, mesh=mesh, in_specs=(spec,) * 4, out_specs=(spec,) * 4, check_vma=False)
```

time: 221 us -> 73.4 us (0.33)
  waiting for transfers between devices: 157 us -> 39.4 us
  other arithmetic: 19.9 us -> 3.78 us
  starting transfers between devices: 0.08 us -> 14.9 us
  between operations: 14.3 us -> 0.84 us
  matrix products: 12.3 us -> 0 us
  Pallas kernels: 0 us -> 8.33 us
  local copies, waits for them, and re-layouts: 11.1 us -> 5.79 us
  blocking collectives: 4.92 us -> 0 us
    all_gather x2 -> x0, waiting for transfers between devices: 157 us -> none  [entering(): gathered = lax.all_gather(part, axis)]
    ppermute x0 -> x13, waiting for transfers between devices: none -> 39.4 us  [exchange(): return lax.ppermute(array, axis, [(i, pairs_of(i)) for i in range(count)])]
    add x15 -> x9, other arithmetic: 17.6 us -> 1.98 us  [the longest x2 1.16 us: scan(): base + jnp.where(core == 0, keep, 0.0)]
    ppermute x0 -> x13, starting transfers between devices: none -> 14.9 us  [exchange(): return lax.ppermute(array, axis, [(i, pairs_of(i)) for i in range(count)])]
    dot_general x12 -> x0, matrix products: 12.3 us -> none  [the longest x1 2.57 us: local(): jnp.einsum('thd,hde->the', queries, prefix_b, preferred_element_type=jnp....]
    pallas_call x0 -> x8, Pallas kernels: none -> 8.33 us  [call(): pl.pallas_call(kernel, out_shape=outs, in_specs=[pl.BlockSpec(memory_spac...]
    psum x1 -> x0, blocking collectives: 4.92 us -> none  [local(): square = lax.psum(local_square, 'head')]
    unnamed x27 -> x30, local copies, waits for them, and re-layouts: 8.42 us -> 5.77 us
  transfers between devices with their start and end apart: 2 -> 13, of which waited for: 2 -> 11; matrix products, arithmetic and copies ran while one was open for 5% -> 0% of each run, Pallas kernels for 0% -> 7%
where the time goes in v1:
time: 73.4 us; the launch traced here: 73.1 us
  waiting for transfers between devices  39.4 us (54%)
  starting transfers between devices  14.9 us (20%)
  Pallas kernels  8.33 us (11%)
  local copies, waits for them, and re-layouts  5.79 us (8%)
  other arithmetic  3.78 us (5%)
  between operations  0.84 us (1%)
    ppermute x13, waiting for transfers between devices, exchange(): return lax.ppermute(array, axis, [(i, pairs_of(i)) for i in range(count)])  39.4 us
    ppermute x13, starting transfers between devices, exchange(): return lax.ppermute(array, axis, [(i, pairs_of(i)) for i in range(count)])  14.9 us
    pallas_call x8, Pallas kernels, call(): pl.pallas_call(kernel, out_shape=outs, in_specs=[pl.BlockSpec(memory_spac...  8.33 us
    unnamed x30, local copies, waits for them, and re-layouts  5.77 us
    another operation x2, other arithmetic, scan(): base = jnp.stack([mine, back])  1.8 us
  transfers between devices with their start and end apart: 13, of which 11 were waited for; matrix products, arithmetic and copies ran while one was open for 0% of the time, Pallas kernels for 7%

profile of v1, /device:TPU:0, one launch (start us, length us, event | category | flops | bytes accessed | tf_op | source)
XLA Modules:
  0.0 73.1 jit_solution(8201541806635274943)
XLA Ops:
  0.6 1.0 %copy-done.1 = bf16[256,1024]{1,0:T(8,128)(2,1)S(1)} copy-done((bf16[256,1024]{1,0:T(8,128)(2,1)S(1)}, bf16[256,1024]{1,0:T(8,128)(2,1)}, u32[]{:S(2)}) %copy-start.1) | copy-done | bytes 524312
  1.7 1.0 %copy-done.3 = bf16[256,1024]{1,0:T(8,128)(2,1)S(1)} copy-done((bf16[256,1024]{1,0:T(8,128)(2,1)S(1)}, bf16[256,1024]{1,0:T(8,128)(2,1)}, u32[]{:S(2)}) %copy-start.3) | copy-done | bytes 524312
  4.8 3.0 %collective-permute-start.1 = (f32[256,128]{1,0:T(8,128)S(1)}, f32[256,128]{1,0:T(8,128)S(1)}, u32[]{:S(2)}, u32[]{:S(2)}) collective-permute-start(f32[256,128]{1,0:T(8,128)S(1)} %slice_bitcast_fusion.2), channel_id=1, source_target_pairs={{0,4},{2,6},{4,0},{6,2},{8,12},{10,14},{12,8},{14,10},{16,20},{18,... | collective-permute-start | bytes 393224 | tf_op jit(solution)/shard_map/ppermute | solution.py:60
  7.7 3.8 %collective-permute-done.1 = f32[256,128]{1,0:T(8,128)S(1)} collective-permute-done((f32[256,128]{1,0:T(8,128)S(1)}, f32[256,128]{1,0:T(8,128)S(1)}, u32[]{:S(2)}, u32[]{:S(2)}) %collective-permute-start.1) | collective-permute-done | bytes 131104 | tf_op jit(solution)/shard_map/ppermute | solution.py:60
  11.5 1.9 %collective-permute-start.2 = (f32[256,128]{1,0:T(8,128)S(1)}, f32[256,128]{1,0:T(8,128)S(1)}, u32[]{:S(2)}, u32[]{:S(2)}) collective-permute-start(f32[256,128]{1,0:T(8,128)S(1)} %fusion), channel_id=1, source_target_pairs={{0,8},{2,10},{4,12},{6,14},{8,0},{10,2},{12,4},{14,6},{16,24},{18,... | collective-permute-start | bytes 393224 | tf_op jit(solution)/shard_map/ppermute | solution.py:60
  13.4 3.2 %collective-permute-done.2 = f32[256,128]{1,0:T(8,128)S(1)} collective-permute-done((f32[256,128]{1,0:T(8,128)S(1)}, f32[256,128]{1,0:T(8,128)S(1)}, u32[]{:S(2)}, u32[]{:S(2)}) %collective-permute-start.2) | collective-permute-done | bytes 131104 | tf_op jit(solution)/shard_map/ppermute | solution.py:60
  16.7 2.8 %collective-permute-start.3 = (f32[256,128]{1,0:T(8,128)S(1)}, f32[256,128]{1,0:T(8,128)S(1)}, u32[]{:S(2)}, u32[]{:S(2)}) collective-permute-start(f32[256,128]{1,0:T(8,128)S(1)} %add.83), channel_id=1, source_target_pairs={{0,16},{2,18},{4,20},{6,22},{8,24},{10,26},{12,28},{14,30},{16,0},... | collective-permute-start | bytes 393224 | tf_op jit(solution)/shard_map/ppermute | solution.py:60
  19.5 5.1 %collective-permute-done.3 = f32[256,128]{1,0:T(8,128)S(1)} collective-permute-done((f32[256,128]{1,0:T(8,128)S(1)}, f32[256,128]{1,0:T(8,128)S(1)}, u32[]{:S(2)}, u32[]{:S(2)}) %collective-permute-start.3) | collective-permute-done | bytes 131104 | tf_op jit(solution)/shard_map/ppermute | solution.py:60
  24.6 1.2 %collective-permute-start.4 = (f32[256,128]{1,0:T(8,128)S(1)}, f32[256,128]{1,0:T(8,128)S(1)}, u32[]{:S(2)}, u32[]{:S(2)}) collective-permute-start(f32[256,128]{1,0:T(8,128)S(1)} %get-tuple-element.39), channel_id=1, source_target_pairs={{0,4},{2,6},{4,0},{6,2},{8,12},{10,14},{12,8},{14,10},{16,20},{18,... | collective-permute-start | bytes 393224 | tf_op jit(solution)/shard_map/ppermute | solution.py:60
  25.8 3.9 %collective-permute-done.4 = f32[256,128]{1,0:T(8,128)S(1)} collective-permute-done((f32[256,128]{1,0:T(8,128)S(1)}, f32[256,128]{1,0:T(8,128)S(1)}, u32[]{:S(2)}, u32[]{:S(2)}) %collective-permute-start.4) | collective-permute-done | bytes 131104 | tf_op jit(solution)/shard_map/ppermute | solution.py:60
  33.4 1.1 %collective-permute-start.6 = (f32[2,256]{1,0:T(2,128)S(1)}, f32[2,256]{1,0:T(2,128)S(1)}, u32[]{:S(2)}, u32[]{:S(2)}) collective-permute-start(f32[2,256]{1,0:T(2,128)S(1)} %get-tuple-element.21), channel_id=1, source_target_pairs={{0,1},{1,0},{2,3},{3,2},{4,5},{5,4},{6,7},{7,6},{8,9},{9,8},{10,11... | collective-permute-start | bytes 6152 | tf_op jit(solution)/shard_map/ppermute | solution.py:60
  34.6 2.5 %collective-permute-done.6 = f32[2,256]{1,0:T(2,128)S(1)} collective-permute-done((f32[2,256]{1,0:T(2,128)S(1)}, f32[2,256]{1,0:T(2,128)S(1)}, u32[]{:S(2)}, u32[]{:S(2)}) %collective-permute-start.6) | collective-permute-done | bytes 2080 | tf_op jit(solution)/shard_map/ppermute | solution.py:60
  38.8 1.0 %collective-permute-done.7 = f32[2,256,128]{2,1,0:T(8,128)S(1)} collective-permute-done((f32[2,256,128]{2,1,0:T(8,128)S(1)}, f32[2,256,128]{2,1,0:T(8,128)S(1)}, u32[]{:S(2)}, u32[]{:S(2)}) %collective-permute-start.7) | collective-permute-done | bytes 262176 | tf_op jit(solution)/shard_map/ppermute | solution.py:60
  39.9 1.2 %collective-permute-start.8 = (f32[256,128]{1,0:T(8,128)S(1)}, f32[256,128]{1,0:T(8,128)S(1)}, u32[]{:S(2)}, u32[]{:S(2)}) collective-permute-start(f32[256,128]{1,0:T(8,128)S(1)} %slice_bitcast_fusion), channel_id=1, source_target_pairs={{0,4},{2,6},{4,0},{6,2},{8,12},{10,14},{12,8},{14,10},{16,20},{18,... | collective-permute-start | bytes 393224 | tf_op jit(solution)/shard_map/ppermute | solution.py:60
  41.1 4.4 %collective-permute-done.8 = f32[256,128]{1,0:T(8,128)S(1)} collective-permute-done((f32[256,128]{1,0:T(8,128)S(1)}, f32[256,128]{1,0:T(8,128)S(1)}, u32[]{:S(2)}, u32[]{:S(2)}) %collective-permute-start.8) | collective-permute-done | bytes 131104 | tf_op jit(solution)/shard_map/ppermute | solution.py:60
  45.9 4.7 %collective-permute-done.9 = f32[256,128]{1,0:T(8,128)S(1)} collective-permute-done((f32[256,128]{1,0:T(8,128)S(1)}, f32[256,128]{1,0:T(8,128)S(1)}, u32[]{:S(2)}, u32[]{:S(2)}) %collective-permute-start.9) | collective-permute-done | bytes 131104 | tf_op jit(solution)/shard_map/ppermute | solution.py:60
  51.3 1.6 %collective-permute-start.10 = (f32[256,128]{1,0:T(8,128)}, f32[256,128]{1,0:T(8,128)}, u32[]{:S(2)}, u32[]{:S(2)}) collective-permute-start(f32[256,128]{1,0:T(8,128)} %add.96), channel_id=1, source_target_pairs={{0,16},{2,18},{4,20},{6,22},{8,24},{10,26},{12,28},{14,30},{16,0},... | collective-permute-start | bytes 393224 | tf_op jit(solution)/shard_map/ppermute | solution.py:60
  53.0 5.9 %collective-permute-done.10 = f32[256,128]{1,0:T(8,128)} collective-permute-done((f32[256,128]{1,0:T(8,128)}, f32[256,128]{1,0:T(8,128)}, u32[]{:S(2)}, u32[]{:S(2)}) %collective-permute-start.10) | collective-permute-done | bytes 131104 | tf_op jit(solution)/shard_map/ppermute | solution.py:60
  58.9 1.8 %add_bitcast_fusion = (f32[1,256,128]{2,1,0:T(8,128)}, f32[256,128]{1,0:T(8,128)}) fusion(f32[256,128]{1,0:T(8,128)S(1)} %collective-permute-done.8, pred[]{:T(512)S(6)} %eq.53, f32[256,128]{1,0:T(8,128)} %collective-permute-done.10, pred[]{:T(512)S(6)} %eq.52, f32[256,128]{1,0:T(8,128)} %copy-done.14, pred[]{:T(512)S(6)} %eq.51, ...), kind=kLoop, calls=%fused_computation.11 | loop fusion | flops 229376 | bytes 786436 | tf_op jit(solution)/shard_map/stack | solution.py:99
  60.7 1.1 %collective-permute-start.11 = (f32[256,128]{1,0:T(8,128)}, f32[256,128]{1,0:T(8,128)S(1)}, u32[]{:S(2)}, u32[]{:S(2)}) collective-permute-start(f32[256,128]{1,0:T(8,128)} %get-tuple-element.35), channel_id=1, source_target_pairs={{0,4},{2,6},{4,0},{6,2},{8,12},{10,14},{12,8},{14,10},{16,20},{18,... | collective-permute-start | bytes 393224 | tf_op jit(solution)/shard_map/ppermute | solution.py:60
  61.8 4.1 %collective-permute-done.11 = f32[256,128]{1,0:T(8,128)S(1)} collective-permute-done((f32[256,128]{1,0:T(8,128)}, f32[256,128]{1,0:T(8,128)S(1)}, u32[]{:S(2)}, u32[]{:S(2)}) %collective-permute-start.11) | collective-permute-done | bytes 131104 | tf_op jit(solution)/shard_map/ppermute | solution.py:60
  65.8 1.1 %select_add_fusion = (f32[2,256,128]{2,1,0:T(8,128)S(1)}, f32[2,256,128]{2,1,0:T(8,128)S(1)}) fusion(f32[2,256,128]{2,1,0:T(8,128)S(1)} %get-tuple-element.28, f32[1,256,128]{2,1,0:T(8,128)S(1)} %bitcast.23, f32[1,256,128]{2,1,0:T(8,128)} %get-tuple-element.34, pred[]{:T(512)S(6)} %eq.56, f32[2,256,128]{2,1,0:T(8,128)} %copy-done.13, pred[]{:T(512)S(6)} %eq.55), kind=kLoop, calls=%fused_computation.2 | loop fusion | flops 327680 | bytes 1310722 | tf_op jit(solution)/shard_map/add | solution.py:100
  68.0 3.5 %shard_map.81 = (bf16[256,1024]{1,0:T(8,128)(2,1)}, bf16[256,1024]{1,0:T(8,128)(2,1)}, f32[256,1024]{1,0:T(8,128)S(1)}, f32[256,1024]{1,0:T(8,128)S(1)}) custom-call(bf16[256,1024]{1,0:T(8,128)(2,1)S(1)} %copy-done, bf16[256,1024]{1,0:T(8,128)(2,1)S(1)} %copy-done.2, bf16[256,1024]{1,0:T(8,128)(2,1)S(1)} %copy-done.4, bf16[8,256,256]{2,1,0:T(8,128)(2,1)S(1)} %copy-done.7, ...), custom_call_target="tpu_custom_call" | custom-call | flops 536870912 | bytes 7866368 | tf_op jit(solution)/shard_map/pallas_call | solution.py:43
  71.5 1.6 %shard_map.82 = (bf16[256,1024]{1,0:T(8,128)(2,1)}, bf16[256,1024]{1,0:T(8,128)(2,1)}) custom-call(bf16[256,1024]{1,0:T(8,128)(2,1)S(1)} %copy-done.2, bf16[256,1024]{1,0:T(8,128)(2,1)S(1)} %copy-done.4, f32[256,1024]{1,0:T(8,128)S(1)} %get-tuple-element.26.near_k_ref, f32[256,1024]{1,0:T(8,128)S(1)} %get-tuple-element.27.near_v_ref, ...), custom_call_target="tpu_custom_call" | custom-call | flops 134217728 | bytes 4718592 | tf_op jit(solution)/shard_map/pallas_call | solution.py:43
  (53 shorter events, 9.7 us)
Async XLA Ops:
  0.6 1.0 %copy-start.1 = (bf16[256,1024]{1,0:T(8,128)(2,1)S(1)}, bf16[256,1024]{1,0:T(8,128)(2,1)}, u32[]{:S(2)}) copy-start(bf16[256,1024]{1,0:T(8,128)(2,1)} %k_ref.5) | copy-start | bytes 1572868
  1.7 1.0 %copy-start.3 = (bf16[256,1024]{1,0:T(8,128)(2,1)S(1)}, bf16[256,1024]{1,0:T(8,128)(2,1)}, u32[]{:S(2)}) copy-start(bf16[256,1024]{1,0:T(8,128)(2,1)} %v_ref.5) | copy-start | bytes 1572868
  3.0 1.7 %collective-permute-start = (f32[2,256,128]{2,1,0:T(8,128)S(1)}, f32[2,256,128]{2,1,0:T(8,128)S(1)}, u32[]{:S(2)}, u32[]{:S(2)}) collective-permute-start(f32[2,256,128]{2,1,0:T(8,128)S(1)} %shard_map.77), channel_id=1, source_target_pairs={{0,2},{2,0},{4,6},{6,4},{8,10},{10,8},{12,14},{14,12},{16,18},{18,... | collective-permute-start | bytes 786440 | tf_op jit(solution)/shard_map/ppermute | solution.py:60
  4.8 6.7 %collective-permute-start.1 = (f32[256,128]{1,0:T(8,128)S(1)}, f32[256,128]{1,0:T(8,128)S(1)}, u32[]{:S(2)}, u32[]{:S(2)}) collective-permute-start(f32[256,128]{1,0:T(8,128)S(1)} %slice_bitcast_fusion.2), channel_id=1, source_target_pairs={{0,4},{2,6},{4,0},{6,2},{8,12},{10,14},{12,8},{14,10},{16,20},{18,... | collective-permute-start | bytes 393224 | tf_op jit(solution)/shard_map/ppermute | solution.py:60
  11.5 5.1 %collective-permute-start.2 = (f32[256,128]{1,0:T(8,128)S(1)}, f32[256,128]{1,0:T(8,128)S(1)}, u32[]{:S(2)}, u32[]{:S(2)}) collective-permute-start(f32[256,128]{1,0:T(8,128)S(1)} %fusion), channel_id=1, source_target_pairs={{0,8},{2,10},{4,12},{6,14},{8,0},{10,2},{12,4},{14,6},{16,24},{18,... | collective-permute-start | bytes 393224 | tf_op jit(solution)/shard_map/ppermute | solution.py:60
  16.7 7.9 %collective-permute-start.3 = (f32[256,128]{1,0:T(8,128)S(1)}, f32[256,128]{1,0:T(8,128)S(1)}, u32[]{:S(2)}, u32[]{:S(2)}) collective-permute-start(f32[256,128]{1,0:T(8,128)S(1)} %add.83), channel_id=1, source_target_pairs={{0,16},{2,18},{4,20},{6,22},{8,24},{10,26},{12,28},{14,30},{16,0},... | collective-permute-start | bytes 393224 | tf_op jit(solution)/shard_map/ppermute | solution.py:60
  24.6 5.2 %copy-start.4 = (bf16[256,1024]{1,0:T(8,128)(2,1)S(1)}, bf16[256,1024]{1,0:T(8,128)(2,1)}, u32[]{:S(2)}) copy-start(bf16[256,1024]{1,0:T(8,128)(2,1)} %v_ref.5) | copy-start | bytes 1572868
  24.6 5.0 %collective-permute-start.4 = (f32[256,128]{1,0:T(8,128)S(1)}, f32[256,128]{1,0:T(8,128)S(1)}, u32[]{:S(2)}, u32[]{:S(2)}) collective-permute-start(f32[256,128]{1,0:T(8,128)S(1)} %get-tuple-element.39), channel_id=1, source_target_pairs={{0,4},{2,6},{4,0},{6,2},{8,12},{10,14},{12,8},{14,10},{16,20},{18,... | collective-permute-start | bytes 393224 | tf_op jit(solution)/shard_map/ppermute | solution.py:60
  29.6 1.0 %copy-start = (bf16[256,1024]{1,0:T(8,128)(2,1)S(1)}, bf16[256,1024]{1,0:T(8,128)(2,1)}, u32[]{:S(2)}) copy-start(bf16[256,1024]{1,0:T(8,128)(2,1)} %q_ref.9) | copy-start | bytes 1572868
  29.6 1.2 %copy-start.2 = (bf16[256,1024]{1,0:T(8,128)(2,1)S(1)}, bf16[256,1024]{1,0:T(8,128)(2,1)}, u32[]{:S(2)}) copy-start(bf16[256,1024]{1,0:T(8,128)(2,1)} %k_ref.5) | copy-start | bytes 1572868
  29.7 3.1 %copy-start.5 = (bf16[256,1024]{1,0:T(8,128)(2,1)S(1)}, bf16[256,1024]{1,0:T(8,128)(2,1)}, u32[]{:S(2)}) copy-start(bf16[256,1024]{1,0:T(8,128)(2,1)} %c_ref.5) | copy-start | bytes 1572868
  29.7 3.0 %collective-permute-start.5 = (f32[2,256,128]{2,1,0:T(8,128)S(1)}, f32[2,256,128]{2,1,0:T(8,128)S(1)}, u32[]{:S(2)}, u32[]{:S(2)}) collective-permute-start(f32[2,256,128]{2,1,0:T(8,128)S(1)} %get-tuple-element.36), channel_id=1, source_target_pairs={{0,2},{2,0},{4,6},{6,4},{8,10},{10,8},{12,14},{14,12},{16,18},{18,... | collective-permute-start | bytes 786440 | tf_op jit(solution)/shard_map/ppermute | solution.py:60
  33.4 3.6 %collective-permute-start.6 = (f32[2,256]{1,0:T(2,128)S(1)}, f32[2,256]{1,0:T(2,128)S(1)}, u32[]{:S(2)}, u32[]{:S(2)}) collective-permute-start(f32[2,256]{1,0:T(2,128)S(1)} %get-tuple-element.21), channel_id=1, source_target_pairs={{0,1},{1,0},{2,3},{3,2},{4,5},{5,4},{6,7},{7,6},{8,9},{9,8},{10,11... | collective-permute-start | bytes 6152 | tf_op jit(solution)/shard_map/ppermute | solution.py:60
  38.3 1.5 %collective-permute-start.7 = (f32[2,256,128]{2,1,0:T(8,128)S(1)}, f32[2,256,128]{2,1,0:T(8,128)S(1)}, u32[]{:S(2)}, u32[]{:S(2)}) collective-permute-start(f32[2,256,128]{2,1,0:T(8,128)S(1)} %get-tuple-element.29), channel_id=1, source_target_pairs={{0,2},{2,0},{4,6},{6,4},{8,10},{10,8},{12,14},{14,12},{16,18},{18,... | collective-permute-start | bytes 786440 | tf_op jit(solution)/shard_map/ppermute | solution.py:60
  38.8 1.1 %copy-start.10 = (bf16[256,512]{1,0:T(8,128)(2,1)}, bf16[256,512]{1,0:T(8,128)(2,1)S(1)}, u32[]{:S(2)}) copy-start(bf16[256,512]{1,0:T(8,128)(2,1)S(1)} %get-tuple-element.22.d_keep_ref) | copy-start | bytes 786436
  39.8 11.5 %copy-start.13 = (f32[2,256,128]{2,1,0:T(8,128)}, f32[2,256,128]{2,1,0:T(8,128)S(1)}, u32[]{:S(2)}) copy-start(f32[2,256,128]{2,1,0:T(8,128)S(1)} %collective-permute-done.7) | copy-start | bytes 786436
  39.9 5.7 %copy-start.12 = (f32[2,256,128]{2,1,0:T(8,128)}, f32[2,256,128]{2,1,0:T(8,128)S(1)}, u32[]{:S(2)}) copy-start(f32[2,256,128]{2,1,0:T(8,128)S(1)} %add.93) | copy-start | bytes 786436
  39.9 5.6 %collective-permute-start.8 = (f32[256,128]{1,0:T(8,128)S(1)}, f32[256,128]{1,0:T(8,128)S(1)}, u32[]{:S(2)}, u32[]{:S(2)}) collective-permute-start(f32[256,128]{1,0:T(8,128)S(1)} %slice_bitcast_fusion), channel_id=1, source_target_pairs={{0,4},{2,6},{4,0},{6,2},{8,12},{10,14},{12,8},{14,10},{16,20},{18,... | collective-permute-start | bytes 393224 | tf_op jit(solution)/shard_map/ppermute | solution.py:60
  45.6 5.0 %collective-permute-start.9 = (f32[256,128]{1,0:T(8,128)S(1)}, f32[256,128]{1,0:T(8,128)S(1)}, u32[]{:S(2)}, u32[]{:S(2)}) collective-permute-start(f32[256,128]{1,0:T(8,128)S(1)} %fusion.1), channel_id=1, source_target_pairs={{0,8},{2,10},{4,12},{6,14},{8,0},{10,2},{12,4},{14,6},{16,24},{18,... | collective-permute-start | bytes 393224 | tf_op jit(solution)/shard_map/ppermute | solution.py:60
  51.3 7.6 %collective-permute-start.10 = (f32[256,128]{1,0:T(8,128)}, f32[256,128]{1,0:T(8,128)}, u32[]{:S(2)}, u32[]{:S(2)}) collective-permute-start(f32[256,128]{1,0:T(8,128)} %add.96), channel_id=1, source_target_pairs={{0,16},{2,18},{4,20},{6,22},{8,24},{10,26},{12,28},{14,30},{16,0},... | collective-permute-start | bytes 393224 | tf_op jit(solution)/shard_map/ppermute | solution.py:60
  60.7 5.2 %collective-permute-start.11 = (f32[256,128]{1,0:T(8,128)}, f32[256,128]{1,0:T(8,128)S(1)}, u32[]{:S(2)}, u32[]{:S(2)}) collective-permute-start(f32[256,128]{1,0:T(8,128)} %get-tuple-element.35), channel_id=1, source_target_pairs={{0,4},{2,6},{4,0},{6,2},{8,12},{10,14},{12,8},{14,10},{16,20},{18,... | collective-permute-start | bytes 393224 | tf_op jit(solution)/shard_map/ppermute | solution.py:60
  61.8 5.3 %copy-start.7 = (bf16[8,256,256]{2,1,0:T(8,128)(2,1)S(1)}, bf16[8,256,256]{2,1,0:T(8,128)(2,1)}, u32[]{:S(2)}) copy-start(bf16[8,256,256]{2,1,0:T(8,128)(2,1)} %copy-done.6) | copy-start | bytes 3145732
  65.8 1.2 %copy-start.9 = (bf16[256,512]{1,0:T(8,128)(2,1)S(1)}, bf16[256,512]{1,0:T(8,128)(2,1)}, u32[]{:S(2)}) copy-start(bf16[256,512]{1,0:T(8,128)(2,1)} %copy-done.8) | copy-start | bytes 786436
  67.0 4.5 %collective-permute-start.12 = (f32[2,256,128]{2,1,0:T(8,128)S(1)}, f32[2,256,128]{2,1,0:T(8,128)S(1)}, u32[]{:S(2)}, u32[]{:S(2)}) collective-permute-start(f32[2,256,128]{2,1,0:T(8,128)S(1)} %get-tuple-element.32), channel_id=1, source_target_pairs={{0,2},{2,0},{4,6},{6,4},{8,10},{10,8},{12,14},{14,12},{16,18},{18,... | collective-permute-start | bytes 786440 | tf_op jit(solution)/shard_map/ppermute | solution.py:60
  (4 other events, 3.3 us)

commit v2 on v0

v2 whole, which is shorter than its diff:
```python
import jax
import jax.numpy as jnp
from jax import lax
from jax.experimental import pallas as pl
from jax.experimental.pallas import tpu as pltpu
from jax.sharding import PartitionSpec as P

HEAD_DIM = 128
EPS = 1e-06
CHUNKS = 2
F32 = jnp.float32
BF16 = jnp.bfloat16
VMEM = pl.BlockSpec(memory_space=pltpu.VMEM)
HBM = pl.BlockSpec(memory_space=pltpu.HBM)

OWN, AWAY = 0, 1


class Layout:
    def __init__(self, rows, heads):
        self.rows = rows
        self.per = heads // 4
        self.chunks = CHUNKS if self.per % CHUNKS == 0 else 1
        self.hc = self.per // self.chunks
        self.half = jax.ShapeDtypeStruct((2, self.hc * HEAD_DIM, HEAD_DIM), F32)

    def heads(self, half):
        block = lax.axis_index("seq")
        core, pair = block & 1, (block >> 1) & 1
        if half == AWAY:
            core = 1 - core
        out = []
        for sub in range(self.per):
            for second in range(2):
                head = (2 * core + (1 - pair if second else pair)) * self.per + sub
                chunk, slot = divmod(sub, self.hc)
                spot = second * self.per + sub
                out.append((head, chunk, (second, pl.ds(slot * HEAD_DIM, HEAD_DIM)), pl.ds(spot * HEAD_DIM, HEAD_DIM)))
        return out


    def quarters(self, half):
        block = lax.axis_index("seq")
        core, pair = block & 1, (block >> 1) & 1
        if half == AWAY:
            core = 1 - core
        size = self.per * HEAD_DIM
        return [
            (pl.ds(pl.multiple_of((2 * core + (1 - pair if second else pair)) * size, HEAD_DIM), size), pl.ds(second * size, size))
            for second in range(2)
        ]


def columns(head):
    return pl.ds(pl.multiple_of(head * HEAD_DIM, HEAD_DIM), HEAD_DIM)


def dot(a, b, contract):
    return lax.dot_general(a, b, (contract, ((), ())), preferred_element_type=F32)


def causal(rows):
    return lax.broadcasted_iota(jnp.int32, (rows, rows), 0) >= lax.broadcasted_iota(jnp.int32, (rows, rows), 1)


def like(shape, dtype=F32):
    return jax.ShapeDtypeStruct(tuple(shape), dtype)


def call(kernel, outs, args, flops, in_hbm=(), out_hbm=(), scratch=(), alias=None):
    moved = sum(a.size * a.dtype.itemsize for a in (*args, *outs))
    return pl.pallas_call(
        kernel,
        out_shape=outs,
        in_specs=[HBM if i in in_hbm else VMEM for i in range(len(args))],
        out_specs=[HBM if i in out_hbm else VMEM for i in range(len(outs))],
        scratch_shapes=list(scratch),
        input_output_aliases=alias or {},
        cost_estimate=pl.CostEstimate(flops=int(flops), bytes_accessed=int(moved), transcendentals=0),
        compiler_params=pltpu.CompilerParams(vmem_limit_bytes=16 * 1024 * 1024),
    )(*[pltpu.with_memory_space_constraint(a, pltpu.HBM) if i in in_hbm else a for i, a in enumerate(args)])


def exchange(axis, partner, array):
    return lax.ppermute(array, axis, [(i, partner(i)) for i in range(lax.axis_size(axis))])


def hops(count):
    steps = count // 4
    by_xor = steps & (steps - 1) == 0
    out, hop = [], 1
    while hop < steps:
        out.append(hop)
        hop *= 2
    return out, by_xor


def scan(keep, send, reverse, beside):
    count = lax.axis_size("seq")
    block = lax.axis_index("seq")
    core, pair, far = block & 1, (block >> 1) & 1, block >> 2
    if reverse:
        core, pair, far = 1 - core, 1 - pair, count // 4 - 1 - far
    each = range(len(keep))
    extra = {}

    def beside_of(name, ready, come):
        if name not in beside:
            return come
        come, extra[name] = lax.optimization_barrier((come, beside[name](ready, extra)))
        return come

    got = [exchange("seq", lambda i: i ^ 1, s) for s in send]
    chip = [keep[c] + got[c] for c in each]
    edge = [jnp.where(core == 0, keep[c], got[c]) for c in each]
    other = [exchange("seq", lambda i: i ^ 2, chip[c][1]) for c in each]
    other = beside_of("pair", chip, other)
    total = [chip[c][0] + other[c] for c in each]
    pair_edge = [jnp.where(pair == 0, chip[c][0], other[c]) for c in each]
    before = [jnp.zeros_like(t) for t in total]
    steps, by_xor = hops(count)
    for hop in steps:
        if by_xor:
            come = [exchange("seq", lambda i: i ^ (4 * hop), t) for t in total]
        else:
            up = [(i, i + 4 * hop) for i in range(count - 4 * hop)]
            if reverse:
                up = [(d, s) for s, d in up]
            come = [lax.ppermute(t, "seq", up) for t in total]
        if hop == steps[0]:
            come = beside_of("first", total, come)
        if hop == steps[-1]:
            come = beside_of("last", total, come)
        if by_xor:
            before = [b + jnp.where(far & hop != 0, g, 0.0) for b, g in zip(before, come)]
        else:
            before = [b + g for b, g in zip(before, come)]
        total = [t + g for t, g in zip(total, come)]
    theirs = [before[c] + jnp.where(pair == 0, pair_edge[c], 0.0) for c in each]
    mine = [before[c] + jnp.where(pair == 1, pair_edge[c], 0.0) for c in each]
    back = [exchange("seq", lambda i: i ^ 2, t) for t in theirs]
    base = [jnp.stack([mine[c], back[c]]) for c in each]
    away = [exchange("seq", lambda i: i ^ 1, base[c] + jnp.where(core == 0, edge[c], 0.0)) for c in each]
    own = [base[c] + jnp.where(core == 1, edge[c], 0.0) for c in each]
    return own, away, extra


def after(early, *arrays):
    return lax.optimization_barrier((early, arrays))[1]


def local(query, key_in, value, cotangent):
    rows, width = query.shape
    heads = width // HEAD_DIM
    lay = Layout(rows, heads)
    n = lay.chunks
    features = width * lax.axis_size("head")
    half_wide = width // 2
    state_flops = heads * rows * HEAD_DIM * HEAD_DIM
    block_flops = heads * rows * rows * HEAD_DIM
    whole = like((rows, width), BF16)
    wide = like((rows, half_wide))

    def loads(half, sources, targets, sems):
        return [
            [
                pltpu.make_async_copy(a.at[:, there], b.at[:, here], sems.at[second, j])
                for j, (a, b) in enumerate(zip(sources, targets))
            ]
            for second, (there, here) in enumerate(lay.quarters(half))
        ]

    def start(copies):
        for copy in copies:
            copy.start()

    def wait(copies):
        for copy in copies:
            copy.wait()

    packed = like((rows, half_wide), BF16)

    def first_states(k_any, v_any, k_own_ref, v_own_ref, k_ref, v_ref, *refs):
        outs, (own_sems, sems) = refs[:n], refs[n:]
        near = loads(OWN, (k_any, v_any), (k_own_ref, v_own_ref), own_sems)
        copies = loads(AWAY, (k_any, v_any), (k_ref, v_ref), sems)
        for part in copies + near:
            start(part)
        arrived = set()
        for head, chunk, place, spot in sorted(lay.heads(AWAY), key=lambda h: h[2][0]):
            if place[0] not in arrived:
                arrived.add(place[0])
                wait(copies[place[0]])
            outs[chunk][place] = dot(k_ref[:, spot], v_ref[:, spot], ((0,), (0,)))
        for part in near:
            wait(part)

    k_own, v_own, k_away, v_away, *send = call(
        first_states,
        [packed] * 4 + [lay.half] * n,
        (key_in, value),
        state_flops,
        (0, 1),
        (),
        [pltpu.SemaphoreType.DMA((2, 2))] * 2,
    )

    def second_states(k_ref, v_ref, *outs):
        for _, chunk, place, spot in lay.heads(OWN):
            outs[chunk][place] = dot(k_ref[:, spot], v_ref[:, spot], ((0,), (0,)))

    keep = call(second_states, [lay.half] * n, (k_own, v_own), state_flops)

    def inner(ready, _):
        def kernel(q_ref, *refs):
            mask = causal(rows)
            for half in (OWN, AWAY):
                k_ref, v_ref, near_ref = refs[half], refs[2 + half], refs[4 + half]
                for head, _, _, spot in lay.heads(half):
                    scores = jnp.where(mask, dot(q_ref[:, columns(head)], k_ref[:, spot], ((1,), (1,))), 0.0).astype(BF16)
                    near_ref[:, spot] = dot(scores, v_ref[:, spot], ((1,), (0,)))

        args = after(ready, query, k_own, k_away, v_own, v_away)
        return call(kernel, [wide] * 2, args, 4 * block_flops)

    own, away, extra = scan(keep, send, False, {"pair": inner})
    near = extra["pair"]

    def mix(half, prefix):
        def kernel(q_ref, c_ref, near_ref, *refs):
            prefix_refs, (mixed_ref, stats_ref, rounded_ref) = refs[:n], refs[n:]
            square = jnp.zeros((rows, HEAD_DIM), F32)
            along = jnp.zeros((rows, HEAD_DIM), F32)
            for head, chunk, place, spot in lay.heads(half):
                cols = columns(head)
                prefix_b = prefix_refs[chunk][place].astype(BF16)
                rounded_ref[spot, :] = prefix_b
                mixed = near_ref[:, spot] + dot(q_ref[:, cols], prefix_b, ((1,), (0,)))
                mixed_ref[:, spot] = mixed
                square += mixed * mixed
                along += c_ref[:, cols].astype(F32) * mixed
            stats_ref[0:1, :] = jnp.sum(square.T, axis=0, keepdims=True)
            stats_ref[1:2, :] = jnp.sum(along.T, axis=0, keepdims=True)

        args = (query, cotangent, near[half], *prefix)
        outs = [wide, like((2, rows)), like((half_wide, HEAD_DIM), BF16)]
        return call(kernel, outs, args, state_flops, alias={2: 0})

    mixed_own, stats_own, prefix_own = mix(OWN, own)
    mixed_away, stats_away, prefix_away = mix(AWAY, away)
    mixed = (mixed_own, mixed_away)
    stats = stats_own + stats_away
    if lax.axis_size("head") == 2:
        stats = stats + exchange("head", lambda i: 1 - i, stats)
    else:
        stats = lax.psum(stats, "head")

    def token_scales(stats_ref):
        rstd = lax.rsqrt(stats_ref[0:1, :] / features + EPS)
        slope = rstd * rstd * (stats_ref[1:2, :] / features)
        return (
            jnp.broadcast_to(rstd, (HEAD_DIM, rows)).T,
            jnp.broadcast_to(slope, (HEAD_DIM, rows)).T,
        )

    def grads(half):
        def kernel(q_ref, c_ref, mixed_ref, stats_ref, d_ref, *outs):
            rstd, slope = token_scales(stats_ref)
            for head, chunk, place, spot in lay.heads(half):
                cols = columns(head)
                d_mixed = (rstd * (c_ref[:, cols].astype(F32) - mixed_ref[:, spot] * slope)).astype(BF16)
                d_ref[:, spot] = d_mixed
                outs[chunk][place] = dot(q_ref[:, cols], d_mixed, ((0,), (0,)))

        out = call(
            kernel,
            [like((rows, half_wide), BF16)] + [lay.half] * n,
            (query, cotangent, mixed[half], stats),
            state_flops,
        )
        return out[0], out[1:]

    d_away, g_send = grads(AWAY)
    d_own, g_keep = grads(OWN)

    def emit(ready, _):
        def kernel(stats_ref, own_ref, away_ref, q_any, k_any, v_any, out_any, q_ref, k_ref, v_ref, *scratch):
            in_sems, out_ref, out_sems = scratch
            copies = loads(OWN, (q_any, k_any, v_any), (q_ref, k_ref, v_ref), in_sems)
            for part in copies:
                start(part)
            rstd, _ = token_scales(stats_ref)
            for half, mixed_ref in ((OWN, own_ref), (AWAY, away_ref)):
                for second, (there, here) in enumerate(lay.quarters(half)):
                    i = 2 * half + second
                    for sub in range(lay.per):
                        part = pl.ds(sub * HEAD_DIM, HEAD_DIM)
                        spot = pl.ds((second * lay.per + sub) * HEAD_DIM, HEAD_DIM)
                        out_ref[i, :, part] = (mixed_ref[:, spot] * rstd).astype(BF16)
                    copy = pltpu.make_async_copy(out_ref.at[i], out_any.at[:, there], out_sems.at[i])
                    copy.start()
                    copies.append([copy])
            for part in copies:
                wait(part)

        args = after(ready, stats, *mixed, query, key_in, value)
        scratch = [
            pltpu.SemaphoreType.DMA((2, 3)),
            pltpu.VMEM((4, rows, lay.per * HEAD_DIM), BF16),
            pltpu.SemaphoreType.DMA((4,)),
        ]
        return call(kernel, [whole, packed, packed, packed], args, width * rows, (3, 4, 5), (0,), scratch)

    def middle_head(q, k, v, d, prefix, mask, spot, gq_ref, gk_ref, gv_ref):
        scores = jnp.where(mask, dot(q, k, ((1,), (1,))), 0.0).astype(BF16)
        d_scores = jnp.where(mask, dot(d, v, ((1,), (1,))), 0.0).astype(BF16)
        gq_ref[:, spot] = (dot(d_scores, k, ((1,), (0,))) + dot(d, prefix, ((1,), (1,)))).astype(BF16)
        gk_ref[:, spot] = dot(d_scores, q, ((0,), (0,)))
        gv_ref[:, spot] = dot(scores, d, ((0,), (0,)))

    def middle_own(ready, extra):
        def kernel(q_ref, k_ref, v_ref, d_ref, prefix_ref, *outs):
            mask = causal(rows)
            for _, _, _, spot in lay.heads(OWN):
                middle_head(
                    q_ref[:, spot], k_ref[:, spot], v_ref[:, spot], d_ref[:, spot], prefix_ref[spot, :], mask, spot, *outs
                )

        args = after(ready, *extra["pair"][1:], d_own, prefix_own)
        return call(kernel, [packed, wide, wide], args, 5 * block_flops)

    def middle_away(ready, extra):
        def kernel(q_any, k_any, v_any, d_ref, prefix_ref, gq_own_ref, gq_any, gk_ref, gv_ref, *scratch):
            q_ref, k_ref, v_ref, in_sems, gq_ref, out_sems = scratch
            copies = loads(AWAY, (q_any, k_any, v_any), (q_ref, k_ref, v_ref), in_sems)
            for part in copies:
                start(part)
            outs = []

            def give(half, second, source):
                there, here = lay.quarters(half)[second]
                outs.append(pltpu.make_async_copy(source.at[:, here], gq_any.at[:, there], out_sems.at[half, second]))
                outs[-1].start()

            give(OWN, 0, gq_own_ref)
            give(OWN, 1, gq_own_ref)
            mask = causal(rows)
            for second in range(2):
                wait(copies[second])
                for _, _, place, spot in lay.heads(AWAY):
                    if place[0] == second:
                        middle_head(
                            q_ref[:, spot], k_ref[:, spot], v_ref[:, spot], d_ref[:, spot], prefix_ref[spot, :], mask, spot,
                            gq_ref, gk_ref, gv_ref,
                        )
                give(AWAY, second, gq_ref)
            wait(outs)

        args = after(ready, query, key_in, value, d_away, prefix_away, extra["first"][0])
        half_room = pltpu.VMEM((rows, half_wide), BF16)
        scratch = [half_room] * 3 + [pltpu.SemaphoreType.DMA((2, 3)), half_room, pltpu.SemaphoreType.DMA((2, 2))]
        return call(kernel, [whole, wide, wide], args, 5 * block_flops, (0, 1, 2), (0,), scratch)

    beside = {"pair": emit, "first": middle_own, "last": middle_away}
    g_own, g_away, extra = scan(g_keep, g_send, True, beside)
    output = extra["pair"][0]
    grad_q = extra["last"][0]
    near_k = (extra["first"][1], extra["last"][1])
    near_v = (extra["first"][2], extra["last"][2])

    def last(half, suffix, so_far):
        count = 2 * lay.per

        def kernel(k_ref, v_ref, near_k_ref, near_v_ref, *refs):
            suffix_refs = refs[:n]
            gk_any, gv_any, gk_ref, gv_ref, sems = refs[n + len(so_far) :]
            copies = []
            for i, (head, chunk, place, spot) in enumerate(lay.heads(half)):
                cols = columns(head)
                state = suffix_refs[chunk][place].astype(BF16)
                gk_ref[i] = (near_k_ref[:, spot] + dot(v_ref[:, cols], state, ((1,), (1,)))).astype(BF16)
                copies.append(pltpu.make_async_copy(gk_ref.at[i], gk_any.at[:, cols], sems.at[i, 0]))
                copies[-1].start()
                gv_ref[i] = (near_v_ref[:, spot] + dot(k_ref[:, cols], state, ((1,), (0,)))).astype(BF16)
                copies.append(pltpu.make_async_copy(gv_ref.at[i], gv_any.at[:, cols], sems.at[i, 1]))
                copies[-1].start()
            for copy in copies:
                copy.wait()

        args = (key_in, value, near_k[half], near_v[half], *suffix, *so_far)
        first = 4 + n
        return call(
            kernel,
            [whole, whole],
            args,
            2 * state_flops,
            tuple(first + i for i in range(len(so_far))),
            (0, 1),
            [pltpu.VMEM((count, rows, HEAD_DIM), BF16)] * 2 + [pltpu.SemaphoreType.DMA((count, 2))],
            {first + i: i for i in range(len(so_far))},
        )

    grad_k, grad_v = last(AWAY, g_away, tuple(last(OWN, g_own, ())))
    return output, grad_q, grad_k, grad_v


def solution(mesh):
    spec = P("seq", "head")
    return jax.shard_map(local, mesh=mesh, in_specs=(spec,) * 4, out_specs=(spec,) * 4, check_vma=False)
```

time: 221 us -> 62.9 us (0.28)
  waiting for transfers between devices: 157 us -> 22.3 us
  starting transfers between devices: 0.08 us -> 25.7 us
  other arithmetic: 19.9 us -> 0.34 us
  between operations: 14.3 us -> 0.91 us
  Pallas kernels: 0 us -> 13.2 us
  matrix products: 12.3 us -> 0 us
  local copies, waits for them, and re-layouts: 11.1 us -> 0.13 us
  blocking collectives: 4.92 us -> 0 us
    all_gather x2 -> x0, waiting for transfers between devices: 157 us -> none  [entering(): gathered = lax.all_gather(part, axis)]
    ppermute x0 -> x25, starting transfers between devices: none -> 25.7 us  [exchange(): lax.ppermute(array, axis, [(i, partner(i)) for i in range(lax.axis_size(a...]
    ppermute x0 -> x25, waiting for transfers between devices: none -> 22.3 us  [exchange(): lax.ppermute(array, axis, [(i, partner(i)) for i in range(lax.axis_size(a...]
    add x15 -> x18, other arithmetic: 17.6 us -> 0.25 us  [the longest x4 0.06 us: scan(): chip = [keep[c] + got[c] for c in each]]
    pallas_call x0 -> x12, Pallas kernels: none -> 13.2 us  [call(): pl.pallas_call(kernel, out_shape=outs, in_specs=[HBM if i in in_hbm else...]
    dot_general x12 -> x0, matrix products: 12.3 us -> none  [the longest x1 2.57 us: local(): jnp.einsum('thd,hde->the', queries, prefix_b, preferred_element_type=jnp....]
    unnamed x27 -> x8, local copies, waits for them, and re-layouts: 8.42 us -> 0.1 us
    psum x1 -> x0, blocking collectives: 4.92 us -> none  [local(): square = lax.psum(local_square, 'head')]
  transfers between devices with their start and end apart: 2 -> 25, of which waited for: 2 -> 18; matrix products, arithmetic and copies ran while one was open for 5% -> 0% of each run, Pallas kernels for 0% -> 15%
where the time goes in v2:
time: 62.9 us; the launch traced here: 62.6 us
  starting transfers between devices  25.7 us (41%)
  waiting for transfers between devices  22.3 us (35%)
  Pallas kernels  13.2 us (21%)
  between operations  0.91 us (1%)
    ppermute x25, starting transfers between devices, exchange(): lax.ppermute(array, axis, [(i, partner(i)) for i in range(lax.axis_size(a...  25.7 us
    ppermute x25, waiting for transfers between devices, exchange(): lax.ppermute(array, axis, [(i, partner(i)) for i in range(lax.axis_size(a...  22.3 us
    pallas_call x12, Pallas kernels, call(): pl.pallas_call(kernel, out_shape=outs, in_specs=[HBM if i in in_hbm else...  13.2 us
  transfers between devices with their start and end apart: 25, of which 18 were waited for; matrix products, arithmetic and copies ran while one was open for 0% of the time, Pallas kernels for 15%

profile of v2, /device:TPU:0, one launch (start us, length us, event | category | flops | bytes accessed | tf_op | source)
XLA Modules:
  0.0 62.6 jit_solution(3780924528201955002)
XLA Ops:
  0.6 1.6 %shard_map.75 = (bf16[256,512]{1,0:T(8,128)(2,1)S(1)}, bf16[256,512]{1,0:T(8,128)(2,1)S(1)}, bf16[256,512]{1,0:T(8,128)(2,1)S(1)}, bf16[256,512]{1,0:T(8,128)(2,...) custom-call(bf16[256,1024]{1,0:T(8,128)(2,1)} %k_ref.3, bf16[256,1024]{1,0:T(8,128)(2,1)} %v_ref.3), custom_call_target="tpu_custom_call" | custom-call | flops 33554432 | bytes 2359296 | tf_op jit(solution)/shard_map/pallas_call | solution.py:72
  3.8 2.9 %collective-permute-start.1 = (f32[128,128]{1,0:T(8,128)S(1)}, f32[128,128]{1,0:T(8,128)S(1)}, u32[]{:S(2)}, u32[]{:S(2)}) collective-permute-start(f32[128,128]{1,0:T(8,128)S(1)} %slice_bitcast_fusion.7), channel_id=1, source_target_pairs={{0,4},{2,6},{4,0},{6,2},{8,12},{10,14},{12,8},{14,10},{16,20},{18,... | collective-permute-start | bytes 196616 | tf_op jit(solution)/shard_map/ppermute | solution.py:85
  7.8 1.3 %collective-permute-done.1 = f32[128,128]{1,0:T(8,128)S(1)} collective-permute-done((f32[128,128]{1,0:T(8,128)S(1)}, f32[128,128]{1,0:T(8,128)S(1)}, u32[]{:S(2)}, u32[]{:S(2)}) %collective-permute-start.1) | collective-permute-done | bytes 65568 | tf_op jit(solution)/shard_map/ppermute | solution.py:85
  9.1 2.0 %collective-permute-done.3 = f32[128,128]{1,0:T(8,128)S(1)} collective-permute-done((f32[128,128]{1,0:T(8,128)S(1)}, f32[128,128]{1,0:T(8,128)S(1)}, u32[]{:S(2)}, u32[]{:S(2)}) %collective-permute-start.3) | collective-permute-done | bytes 65568 | tf_op jit(solution)/shard_map/ppermute | solution.py:85
  11.1 1.6 %collective-permute-start.4 = (f32[128,128]{1,0:T(8,128)S(1)}, f32[128,128]{1,0:T(8,128)S(1)}, u32[]{:S(2)}, u32[]{:S(2)}) collective-permute-start(f32[128,128]{1,0:T(8,128)S(1)} %fusion.1), channel_id=1, source_target_pairs={{0,8},{2,10},{4,12},{6,14},{8,0},{10,2},{12,4},{14,6},{16,24},{18,... | collective-permute-start | bytes 196616 | tf_op jit(solution)/shard_map/ppermute | solution.py:85
  13.3 2.2 %collective-permute-done.4 = f32[128,128]{1,0:T(8,128)S(1)} collective-permute-done((f32[128,128]{1,0:T(8,128)S(1)}, f32[128,128]{1,0:T(8,128)S(1)}, u32[]{:S(2)}, u32[]{:S(2)}) %collective-permute-start.4) | collective-permute-done | bytes 65568 | tf_op jit(solution)/shard_map/ppermute | solution.py:85
  15.4 2.7 %collective-permute-start.5 = (f32[128,128]{1,0:T(8,128)S(1)}, f32[128,128]{1,0:T(8,128)S(1)}, u32[]{:S(2)}, u32[]{:S(2)}) collective-permute-start(f32[128,128]{1,0:T(8,128)S(1)} %add.105), channel_id=1, source_target_pairs={{0,16},{2,18},{4,20},{6,22},{8,24},{10,26},{12,28},{14,30},{16,0},... | collective-permute-start | bytes 196616 | tf_op jit(solution)/shard_map/ppermute | solution.py:85
  18.1 1.7 %collective-permute-start.8 = (f32[128,128]{1,0:T(8,128)S(1)}, f32[128,128]{1,0:T(8,128)S(1)}, u32[]{:S(2)}, u32[]{:S(2)}) collective-permute-start(f32[128,128]{1,0:T(8,128)S(1)} %add.111), channel_id=1, source_target_pairs={{0,16},{2,18},{4,20},{6,22},{8,24},{10,26},{12,28},{14,30},{16,0},... | collective-permute-start | bytes 196616 | tf_op jit(solution)/shard_map/ppermute | solution.py:85
  19.8 2.3 %collective-permute-done.5 = f32[128,128]{1,0:T(8,128)S(1)} collective-permute-done((f32[128,128]{1,0:T(8,128)S(1)}, f32[128,128]{1,0:T(8,128)S(1)}, u32[]{:S(2)}, u32[]{:S(2)}) %collective-permute-start.5) | collective-permute-done | bytes 65568 | tf_op jit(solution)/shard_map/ppermute | solution.py:85
  22.1 1.7 %collective-permute-start.6 = (f32[128,128]{1,0:T(8,128)S(1)}, f32[128,128]{1,0:T(8,128)S(1)}, u32[]{:S(2)}, u32[]{:S(2)}) collective-permute-start(f32[128,128]{1,0:T(8,128)S(1)} %get-tuple-element.175), channel_id=1, source_target_pairs={{0,4},{2,6},{4,0},{6,2},{8,12},{10,14},{12,8},{14,10},{16,20},{18,... | collective-permute-start | bytes 196616 | tf_op jit(solution)/shard_map/ppermute | solution.py:85
  23.8 1.9 %collective-permute-start.9 = (f32[128,128]{1,0:T(8,128)S(1)}, f32[128,128]{1,0:T(8,128)S(1)}, u32[]{:S(2)}, u32[]{:S(2)}) collective-permute-start(f32[128,128]{1,0:T(8,128)S(1)} %get-tuple-element.173), channel_id=1, source_target_pairs={{0,4},{2,6},{4,0},{6,2},{8,12},{10,14},{12,8},{14,10},{16,20},{18,... | collective-permute-start | bytes 196616 | tf_op jit(solution)/shard_map/ppermute | solution.py:85
  26.5 1.6 %collective-permute-done.9 = f32[128,128]{1,0:T(8,128)S(1)} collective-permute-done((f32[128,128]{1,0:T(8,128)S(1)}, f32[128,128]{1,0:T(8,128)S(1)}, u32[]{:S(2)}, u32[]{:S(2)}) %collective-permute-start.9) | collective-permute-done | bytes 65568 | tf_op jit(solution)/shard_map/ppermute | solution.py:85
  30.1 1.6 %collective-permute-start.12 = (f32[2,256]{1,0:T(2,128)S(1)}, f32[2,256]{1,0:T(2,128)S(1)}, u32[]{:S(2)}, u32[]{:S(2)}) collective-permute-start(f32[2,256]{1,0:T(2,128)S(1)} %add.118), channel_id=1, source_target_pairs={{0,1},{1,0},{2,3},{3,2},{4,5},{5,4},{6,7},{7,6},{8,9},{9,8},{10,11... | collective-permute-start | bytes 6152 | tf_op jit(solution)/shard_map/ppermute | solution.py:85
  31.7 2.1 %collective-permute-done.12 = f32[2,256]{1,0:T(2,128)S(1)} collective-permute-done((f32[2,256]{1,0:T(2,128)S(1)}, f32[2,256]{1,0:T(2,128)S(1)}, u32[]{:S(2)}, u32[]{:S(2)}) %collective-permute-start.12) | collective-permute-done | bytes 2080 | tf_op jit(solution)/shard_map/ppermute | solution.py:85
  35.7 1.9 %collective-permute-start.14 = (f32[128,128]{1,0:T(8,128)S(1)}, f32[128,128]{1,0:T(8,128)S(1)}, u32[]{:S(2)}, u32[]{:S(2)}) collective-permute-start(f32[128,128]{1,0:T(8,128)S(1)} %slice_bitcast_fusion.3), channel_id=1, source_target_pairs={{0,4},{2,6},{4,0},{6,2},{8,12},{10,14},{12,8},{14,10},{16,20},{18,... | collective-permute-start | bytes 196616 | tf_op jit(solution)/shard_map/ppermute | solution.py:85
  37.9 1.5 %shard_map.82 = (bf16[256,1024]{1,0:T(8,128)(2,1)}, bf16[256,512]{1,0:T(8,128)(2,1)S(1)}, bf16[256,512]{1,0:T(8,128)(2,1)S(1)}, bf16[256,512]{1,0:T(8,128)(2,1)S(1)}) custom-call(f32[2,256]{1,0:T(2,128)S(1)} %add.119.stats_ref, f32[256,512]{1,0:T(8,128)S(1)} %get-tuple-element.110.mixed_ref.own_ref, f32[256,512]{1,0:T(8,128)S(1)} %get-tuple-element.111.mixed_ref.away_ref, ...), custom_call_target="tpu_custom_call" | custom-call | flops 262144 | bytes 3934208 | tf_op jit(solution)/shard_map/pallas_call | solution.py:72
  40.0 2.0 %collective-permute-done.16 = f32[128,128]{1,0:T(8,128)S(1)} collective-permute-done((f32[128,128]{1,0:T(8,128)S(1)}, f32[128,128]{1,0:T(8,128)S(1)}, u32[]{:S(2)}, u32[]{:S(2)}) %collective-permute-start.16) | collective-permute-done | bytes 65568 | tf_op jit(solution)/shard_map/ppermute | solution.py:85
  42.6 1.5 %collective-permute-start.18 = (f32[128,128]{1,0:T(8,128)S(1)}, f32[128,128]{1,0:T(8,128)S(1)}, u32[]{:S(2)}, u32[]{:S(2)}) collective-permute-start(f32[128,128]{1,0:T(8,128)S(1)} %fusion.7), channel_id=1, source_target_pairs={{0,8},{2,10},{4,12},{6,14},{8,0},{10,2},{12,4},{14,6},{16,24},{18,... | collective-permute-start | bytes 196616 | tf_op jit(solution)/shard_map/ppermute | solution.py:85
  44.2 1.4 %shard_map.83 = (bf16[256,512]{1,0:T(8,128)(2,1)S(1)}, f32[256,512]{1,0:T(8,128)S(1)}, f32[256,512]{1,0:T(8,128)S(1)}) custom-call(bf16[256,512]{1,0:T(8,128)(2,1)S(1)} %get-tuple-element.127.q_ref, bf16[256,512]{1,0:T(8,128)(2,1)S(1)} %get-tuple-element.128.k_ref, bf16[256,512]{1,0:T(8,128)(2,1)S(1)} %get-tuple-element.129.v_ref, ...), custom_call_target="tpu_custom_call" | custom-call | flops 335544320 | bytes 2490368 | tf_op jit(solution)/shard_map/pallas_call | solution.py:72
  47.0 1.8 %collective-permute-start.19 = (f32[128,128]{1,0:T(8,128)S(1)}, f32[128,128]{1,0:T(8,128)S(1)}, u32[]{:S(2)}, u32[]{:S(2)}) collective-permute-start(f32[128,128]{1,0:T(8,128)S(1)} %add.124), channel_id=1, source_target_pairs={{0,16},{2,18},{4,20},{6,22},{8,24},{10,26},{12,28},{14,30},{16,0},... | collective-permute-start | bytes 196616 | tf_op jit(solution)/shard_map/ppermute | solution.py:85
  48.9 1.2 %collective-permute-start.20 = (f32[128,128]{1,0:T(8,128)S(1)}, f32[128,128]{1,0:T(8,128)S(1)}, u32[]{:S(2)}, u32[]{:S(2)}) collective-permute-start(f32[128,128]{1,0:T(8,128)S(1)} %add.125), channel_id=1, source_target_pairs={{0,16},{2,18},{4,20},{6,22},{8,24},{10,26},{12,28},{14,30},{16,0},... | collective-permute-start | bytes 196616 | tf_op jit(solution)/shard_map/ppermute | solution.py:85
  50.1 3.4 %shard_map.84 = (bf16[256,1024]{1,0:T(8,128)(2,1)}, f32[256,512]{1,0:T(8,128)S(1)}, f32[256,512]{1,0:T(8,128)S(1)}) custom-call(bf16[256,1024]{1,0:T(8,128)(2,1)} %q_any.1, bf16[256,1024]{1,0:T(8,128)(2,1)} %k_ref.3, bf16[256,1024]{1,0:T(8,128)(2,1)} %v_ref.3, bf16[256,512]{1,0:T(8,128)(2,1)S(1)} %get-tuple-element.143.d_ref, ...), custom_call_target="tpu_custom_call" | custom-call | flops 335544320 | bytes 3801088 | tf_op jit(solution)/shard_map/pallas_call | solution.py:72
  53.5 1.3 %collective-permute-done.20 = f32[128,128]{1,0:T(8,128)S(1)} collective-permute-done((f32[128,128]{1,0:T(8,128)S(1)}, f32[128,128]{1,0:T(8,128)S(1)}, u32[]{:S(2)}, u32[]{:S(2)}) %collective-permute-start.20) | collective-permute-done | bytes 65568 | tf_op jit(solution)/shard_map/ppermute | solution.py:85
  57.0 2.1 %collective-permute-done.21 = f32[128,128]{1,0:T(8,128)S(1)} collective-permute-done((f32[128,128]{1,0:T(8,128)S(1)}, f32[128,128]{1,0:T(8,128)S(1)}, u32[]{:S(2)}, u32[]{:S(2)}) %collective-permute-start.21) | collective-permute-done | bytes 65568 | tf_op jit(solution)/shard_map/ppermute | solution.py:85
  (72 shorter events, 16.5 us)
Async XLA Ops:
  2.2 1.5 %collective-permute-start = (f32[2,128,128]{2,1,0:T(8,128)S(1)}, f32[2,128,128]{2,1,0:T(8,128)S(1)}, u32[]{:S(2)}, u32[]{:S(2)}) collective-permute-start(f32[2,128,128]{2,1,0:T(8,128)S(1)} %get-tuple-element.85), channel_id=1, source_target_pairs={{0,2},{2,0},{4,6},{6,4},{8,10},{10,8},{12,14},{14,12},{16,18},{18,... | collective-permute-start | bytes 393224 | tf_op jit(solution)/shard_map/ppermute | solution.py:85
  2.7 4.0 %collective-permute-start.2 = (f32[2,128,128]{2,1,0:T(8,128)S(1)}, f32[2,128,128]{2,1,0:T(8,128)S(1)}, u32[]{:S(2)}, u32[]{:S(2)}) collective-permute-start(f32[2,128,128]{2,1,0:T(8,128)S(1)} %get-tuple-element.87), channel_id=1, source_target_pairs={{0,2},{2,0},{4,6},{6,4},{8,10},{10,8},{12,14},{14,12},{16,18},{18,... | collective-permute-start | bytes 393224 | tf_op jit(solution)/shard_map/ppermute | solution.py:85
  3.8 5.3 %collective-permute-start.1 = (f32[128,128]{1,0:T(8,128)S(1)}, f32[128,128]{1,0:T(8,128)S(1)}, u32[]{:S(2)}, u32[]{:S(2)}) collective-permute-start(f32[128,128]{1,0:T(8,128)S(1)} %slice_bitcast_fusion.7), channel_id=1, source_target_pairs={{0,4},{2,6},{4,0},{6,2},{8,12},{10,14},{12,8},{14,10},{16,20},{18,... | collective-permute-start | bytes 196616 | tf_op jit(solution)/shard_map/ppermute | solution.py:85
  6.7 4.3 %collective-permute-start.3 = (f32[128,128]{1,0:T(8,128)S(1)}, f32[128,128]{1,0:T(8,128)S(1)}, u32[]{:S(2)}, u32[]{:S(2)}) collective-permute-start(f32[128,128]{1,0:T(8,128)S(1)} %slice_bitcast_fusion.6), channel_id=1, source_target_pairs={{0,4},{2,6},{4,0},{6,2},{8,12},{10,14},{12,8},{14,10},{16,20},{18,... | collective-permute-start | bytes 196616 | tf_op jit(solution)/shard_map/ppermute | solution.py:85
  11.1 4.3 %collective-permute-start.4 = (f32[128,128]{1,0:T(8,128)S(1)}, f32[128,128]{1,0:T(8,128)S(1)}, u32[]{:S(2)}, u32[]{:S(2)}) collective-permute-start(f32[128,128]{1,0:T(8,128)S(1)} %fusion.1), channel_id=1, source_target_pairs={{0,8},{2,10},{4,12},{6,14},{8,0},{10,2},{12,4},{14,6},{16,24},{18,... | collective-permute-start | bytes 196616 | tf_op jit(solution)/shard_map/ppermute | solution.py:85
  12.7 5.4 %collective-permute-start.7 = (f32[128,128]{1,0:T(8,128)S(1)}, f32[128,128]{1,0:T(8,128)S(1)}, u32[]{:S(2)}, u32[]{:S(2)}) collective-permute-start(f32[128,128]{1,0:T(8,128)S(1)} %fusion.3), channel_id=1, source_target_pairs={{0,8},{2,10},{4,12},{6,14},{8,0},{10,2},{12,4},{14,6},{16,24},{18,... | collective-permute-start | bytes 196616 | tf_op jit(solution)/shard_map/ppermute | solution.py:85
  15.4 6.6 %collective-permute-start.5 = (f32[128,128]{1,0:T(8,128)S(1)}, f32[128,128]{1,0:T(8,128)S(1)}, u32[]{:S(2)}, u32[]{:S(2)}) collective-permute-start(f32[128,128]{1,0:T(8,128)S(1)} %add.105), channel_id=1, source_target_pairs={{0,16},{2,18},{4,20},{6,22},{8,24},{10,26},{12,28},{14,30},{16,0},... | collective-permute-start | bytes 196616 | tf_op jit(solution)/shard_map/ppermute | solution.py:85
  18.1 5.7 %collective-permute-start.8 = (f32[128,128]{1,0:T(8,128)S(1)}, f32[128,128]{1,0:T(8,128)S(1)}, u32[]{:S(2)}, u32[]{:S(2)}) collective-permute-start(f32[128,128]{1,0:T(8,128)S(1)} %add.111), channel_id=1, source_target_pairs={{0,16},{2,18},{4,20},{6,22},{8,24},{10,26},{12,28},{14,30},{16,0},... | collective-permute-start | bytes 196616 | tf_op jit(solution)/shard_map/ppermute | solution.py:85
  22.1 4.3 %collective-permute-start.6 = (f32[128,128]{1,0:T(8,128)S(1)}, f32[128,128]{1,0:T(8,128)S(1)}, u32[]{:S(2)}, u32[]{:S(2)}) collective-permute-start(f32[128,128]{1,0:T(8,128)S(1)} %get-tuple-element.175), channel_id=1, source_target_pairs={{0,4},{2,6},{4,0},{6,2},{8,12},{10,14},{12,8},{14,10},{16,20},{18,... | collective-permute-start | bytes 196616 | tf_op jit(solution)/shard_map/ppermute | solution.py:85
  23.8 4.3 %collective-permute-start.9 = (f32[128,128]{1,0:T(8,128)S(1)}, f32[128,128]{1,0:T(8,128)S(1)}, u32[]{:S(2)}, u32[]{:S(2)}) collective-permute-start(f32[128,128]{1,0:T(8,128)S(1)} %get-tuple-element.173), channel_id=1, source_target_pairs={{0,4},{2,6},{4,0},{6,2},{8,12},{10,14},{12,8},{14,10},{16,20},{18,... | collective-permute-start | bytes 196616 | tf_op jit(solution)/shard_map/ppermute | solution.py:85
  26.5 2.3 %collective-permute-start.10 = (f32[2,128,128]{2,1,0:T(8,128)S(1)}, f32[2,128,128]{2,1,0:T(8,128)S(1)}, u32[]{:S(2)}, u32[]{:S(2)}) collective-permute-start(f32[2,128,128]{2,1,0:T(8,128)S(1)} %get-tuple-element.166), channel_id=1, source_target_pairs={{0,2},{2,0},{4,6},{6,4},{8,10},{10,8},{12,14},{14,12},{16,18},{18,... | collective-permute-start | bytes 393224 | tf_op jit(solution)/shard_map/ppermute | solution.py:85
  28.1 1.4 %collective-permute-start.11 = (f32[2,128,128]{2,1,0:T(8,128)S(1)}, f32[2,128,128]{2,1,0:T(8,128)S(1)}, u32[]{:S(2)}, u32[]{:S(2)}) collective-permute-start(f32[2,128,128]{2,1,0:T(8,128)S(1)} %get-tuple-element.164), channel_id=1, source_target_pairs={{0,2},{2,0},{4,6},{6,4},{8,10},{10,8},{12,14},{14,12},{16,18},{18,... | collective-permute-start | bytes 393224 | tf_op jit(solution)/shard_map/ppermute | solution.py:85
  30.1 3.7 %collective-permute-start.12 = (f32[2,256]{1,0:T(2,128)S(1)}, f32[2,256]{1,0:T(2,128)S(1)}, u32[]{:S(2)}, u32[]{:S(2)}) collective-permute-start(f32[2,256]{1,0:T(2,128)S(1)} %add.118), channel_id=1, source_target_pairs={{0,1},{1,0},{2,3},{3,2},{4,5},{5,4},{6,7},{7,6},{8,9},{9,8},{10,11... | collective-permute-start | bytes 6152 | tf_op jit(solution)/shard_map/ppermute | solution.py:85
  34.2 1.4 %collective-permute-start.13 = (f32[2,128,128]{2,1,0:T(8,128)S(1)}, f32[2,128,128]{2,1,0:T(8,128)S(1)}, u32[]{:S(2)}, u32[]{:S(2)}) collective-permute-start(f32[2,128,128]{2,1,0:T(8,128)S(1)} %get-tuple-element.106), channel_id=1, source_target_pairs={{0,2},{2,0},{4,6},{6,4},{8,10},{10,8},{12,14},{14,12},{16,18},{18,... | collective-permute-start | bytes 393224 | tf_op jit(solution)/shard_map/ppermute | solution.py:85
  34.3 3.3 %collective-permute-start.15 = (f32[2,128,128]{2,1,0:T(8,128)S(1)}, f32[2,128,128]{2,1,0:T(8,128)S(1)}, u32[]{:S(2)}, u32[]{:S(2)}) collective-permute-start(f32[2,128,128]{2,1,0:T(8,128)S(1)} %get-tuple-element.108), channel_id=1, source_target_pairs={{0,2},{2,0},{4,6},{6,4},{8,10},{10,8},{12,14},{14,12},{16,18},{18,... | collective-permute-start | bytes 393224 | tf_op jit(solution)/shard_map/ppermute | solution.py:85
  35.7 4.3 %collective-permute-start.14 = (f32[128,128]{1,0:T(8,128)S(1)}, f32[128,128]{1,0:T(8,128)S(1)}, u32[]{:S(2)}, u32[]{:S(2)}) collective-permute-start(f32[128,128]{1,0:T(8,128)S(1)} %slice_bitcast_fusion.3), channel_id=1, source_target_pairs={{0,4},{2,6},{4,0},{6,2},{8,12},{10,14},{12,8},{14,10},{16,20},{18,... | collective-permute-start | bytes 196616 | tf_op jit(solution)/shard_map/ppermute | solution.py:85
  37.7 4.3 %collective-permute-start.16 = (f32[128,128]{1,0:T(8,128)S(1)}, f32[128,128]{1,0:T(8,128)S(1)}, u32[]{:S(2)}, u32[]{:S(2)}) collective-permute-start(f32[128,128]{1,0:T(8,128)S(1)} %slice_bitcast_fusion.2), channel_id=1, source_target_pairs={{0,4},{2,6},{4,0},{6,2},{8,12},{10,14},{12,8},{14,10},{16,20},{18,... | collective-permute-start | bytes 196616 | tf_op jit(solution)/shard_map/ppermute | solution.py:85
  42.0 4.3 %collective-permute-start.17 = (f32[128,128]{1,0:T(8,128)S(1)}, f32[128,128]{1,0:T(8,128)S(1)}, u32[]{:S(2)}, u32[]{:S(2)}) collective-permute-start(f32[128,128]{1,0:T(8,128)S(1)} %fusion.5), channel_id=1, source_target_pairs={{0,8},{2,10},{4,12},{6,14},{8,0},{10,2},{12,4},{14,6},{16,24},{18,... | collective-permute-start | bytes 196616 | tf_op jit(solution)/shard_map/ppermute | solution.py:85
  42.6 4.4 %collective-permute-start.18 = (f32[128,128]{1,0:T(8,128)S(1)}, f32[128,128]{1,0:T(8,128)S(1)}, u32[]{:S(2)}, u32[]{:S(2)}) collective-permute-start(f32[128,128]{1,0:T(8,128)S(1)} %fusion.7), channel_id=1, source_target_pairs={{0,8},{2,10},{4,12},{6,14},{8,0},{10,2},{12,4},{14,6},{16,24},{18,... | collective-permute-start | bytes 196616 | tf_op jit(solution)/shard_map/ppermute | solution.py:85
  47.0 6.5 %collective-permute-start.19 = (f32[128,128]{1,0:T(8,128)S(1)}, f32[128,128]{1,0:T(8,128)S(1)}, u32[]{:S(2)}, u32[]{:S(2)}) collective-permute-start(f32[128,128]{1,0:T(8,128)S(1)} %add.124), channel_id=1, source_target_pairs={{0,16},{2,18},{4,20},{6,22},{8,24},{10,26},{12,28},{14,30},{16,0},... | collective-permute-start | bytes 196616 | tf_op jit(solution)/shard_map/ppermute | solution.py:85
  48.9 5.9 %collective-permute-start.20 = (f32[128,128]{1,0:T(8,128)S(1)}, f32[128,128]{1,0:T(8,128)S(1)}, u32[]{:S(2)}, u32[]{:S(2)}) collective-permute-start(f32[128,128]{1,0:T(8,128)S(1)} %add.125), channel_id=1, source_target_pairs={{0,16},{2,18},{4,20},{6,22},{8,24},{10,26},{12,28},{14,30},{16,0},... | collective-permute-start | bytes 196616 | tf_op jit(solution)/shard_map/ppermute | solution.py:85
  54.8 4.3 %collective-permute-start.21 = (f32[128,128]{1,0:T(8,128)S(1)}, f32[128,128]{1,0:T(8,128)S(1)}, u32[]{:S(2)}, u32[]{:S(2)}) collective-permute-start(f32[128,128]{1,0:T(8,128)S(1)} %get-tuple-element.171), channel_id=1, source_target_pairs={{0,4},{2,6},{4,0},{6,2},{8,12},{10,14},{12,8},{14,10},{16,20},{18,... | collective-permute-start | bytes 196616 | tf_op jit(solution)/shard_map/ppermute | solution.py:85
  55.8 4.3 %collective-permute-start.23 = (f32[128,128]{1,0:T(8,128)S(1)}, f32[128,128]{1,0:T(8,128)S(1)}, u32[]{:S(2)}, u32[]{:S(2)}) collective-permute-start(f32[128,128]{1,0:T(8,128)S(1)} %get-tuple-element.169), channel_id=1, source_target_pairs={{0,4},{2,6},{4,0},{6,2},{8,12},{10,14},{12,8},{14,10},{16,20},{18,... | collective-permute-start | bytes 196616 | tf_op jit(solution)/shard_map/ppermute | solution.py:85
  59.2 2.2 %collective-permute-start.22 = (f32[2,128,128]{2,1,0:T(8,128)S(1)}, f32[2,128,128]{2,1,0:T(8,128)S(1)}, u32[]{:S(2)}, u32[]{:S(2)}) collective-permute-start(f32[2,128,128]{2,1,0:T(8,128)S(1)} %get-tuple-element.163), channel_id=1, source_target_pairs={{0,2},{2,0},{4,6},{6,4},{8,10},{10,8},{12,14},{14,12},{16,18},{18,... | collective-permute-start | bytes 393224 | tf_op jit(solution)/shard_map/ppermute | solution.py:85
  (5 other events, 8.7 us)

commit v3 on v0

v3 whole, which is shorter than its diff:
```python
import jax
import jax.numpy as jnp
from jax import lax
from jax.experimental import pallas as pl
from jax.experimental.pallas import tpu as pltpu
from jax.sharding import PartitionSpec as P

HEAD_DIM = 128
EPS = 1e-06
F32 = jnp.float32
BF16 = jnp.bfloat16
VMEM = pl.BlockSpec(memory_space=pltpu.VMEM)
HBM = pl.BlockSpec(memory_space=pltpu.HBM)
OWN, AWAY = 0, 1

PIECES = 4


def split(block):
    return block & 1, (block >> 1) & (PIECES - 1), block >> 3


class Half:
    def __init__(self, which, heads):
        core, self.team, _ = split(lax.axis_index("seq"))
        number = core if which == OWN else 1 - core
        self.heads = heads // 2
        self.base = number * (self.heads * HEAD_DIM)
        self.piece_rows = self.heads * HEAD_DIM // PIECES

    def columns(self, start=0, size=None):
        size = self.heads * HEAD_DIM if size is None else size
        return pl.ds(pl.multiple_of(self.base + start, HEAD_DIM), size)

    def state_parts(self, head):
        step = min(self.piece_rows, HEAD_DIM)
        return [
            ((head * HEAD_DIM + row) // self.piece_rows ^ self.team, (head * HEAD_DIM + row) % self.piece_rows, row, step)
            for row in range(0, HEAD_DIM, step)
        ]

    def put(self, ref, head, state):
        for place, there, here, step in self.state_parts(head):
            ref[place, there : there + step, :] = state[here : here + step, :]

    def get(self, ref, head):
        parts = [ref[place, there : there + step, :] for place, there, _, step in self.state_parts(head)]
        return (parts[0] if len(parts) == 1 else jnp.concatenate(parts, axis=0)).astype(BF16)


def dot(a, b, contract):
    return lax.dot_general(a, b, (contract, ((), ())), preferred_element_type=F32)


def causal(rows):
    return lax.broadcasted_iota(jnp.int32, (rows, rows), 0) >= lax.broadcasted_iota(jnp.int32, (rows, rows), 1)


def like(shape, dtype=F32):
    return jax.ShapeDtypeStruct(tuple(shape), dtype)


def call(kernel, outs, args, flops, in_hbm=(), out_hbm=(), scratch=(), alias=None):
    moved = sum(a.size * a.dtype.itemsize for a in (*args, *outs))
    return pl.pallas_call(
        kernel,
        out_shape=outs,
        in_specs=[HBM if i in in_hbm else VMEM for i in range(len(args))],
        out_specs=[HBM if i in out_hbm else VMEM for i in range(len(outs))],
        scratch_shapes=list(scratch),
        input_output_aliases=alias or {},
        cost_estimate=pl.CostEstimate(flops=int(flops), bytes_accessed=int(moved), transcendentals=0),
        compiler_params=pltpu.CompilerParams(vmem_limit_bytes=16 * 1024 * 1024),
    )(*[pltpu.with_memory_space_constraint(a, pltpu.HBM) if i in in_hbm else a for i, a in enumerate(args)])


def exchange(axis, partner, array):
    return lax.ppermute(array, axis, [(i, partner(i)) for i in range(lax.axis_size(axis))])


def after(early, *arrays):
    return lax.optimization_barrier((early, arrays))[1]


def scan(keep, send, reverse, beside):
    count = lax.axis_size("seq")
    core, team, far = split(lax.axis_index("seq"))
    if reverse:
        core, team, far = 1 - core, PIECES - 1 - team, count // 8 - 1 - far
    extra = {}

    def beside_of(name, ready, come):
        if name in beside:
            come, extra[name] = lax.optimization_barrier((come, beside[name](ready, extra)))
        return come

    def to_team(pieces, name):
        come = [exchange("seq", lambda i: i ^ (2 * r), pieces[r]) for r in range(1, PIECES)]
        come[-1] = beside_of(name, pieces[-1], come[-1])
        return [pieces[0], *come]

    got = exchange("seq", lambda i: i ^ 1, send)
    both = keep + got
    edge = lax.optimization_barrier(jnp.where(core == 0, keep, got))
    parts = to_team([both[r] for r in range(PIECES)], "gather")
    total = parts[0] + parts[1] + (parts[2] + parts[3])

    before = jnp.zeros_like(total)
    steps = count // 8
    hop = 1
    while hop < steps:
        if steps & (steps - 1) == 0:
            come = exchange("seq", lambda i: i ^ (8 * hop), total)
            earlier = jnp.where(far & hop != 0, come, 0.0)
        else:
            up = [(i, i + 8 * hop) for i in range(count - 8 * hop)]
            come = lax.ppermute(total, "seq", [(d, s) for s, d in up] if reverse else up)
            earlier = come
        if 2 * hop >= steps:
            come, earlier = beside_of("far", total, (come, earlier))
        before = before + earlier
        total = total + come
        hop *= 2

    starts = []
    for r in range(PIECES):
        start = before
        for other in range(PIECES):
            if other != r:
                start = start + jnp.where((team ^ other) < (team ^ r), parts[other], 0.0)
        starts.append(start)
    base = jnp.stack(to_team(starts, "back"))
    away = exchange("seq", lambda i: i ^ 1, base + jnp.where(core == 0, edge, 0.0))
    own = base + jnp.where(core == 1, edge, 0.0)
    return own, away, extra


def local(query, key_in, value, cotangent):
    rows, width = query.shape
    heads = width // HEAD_DIM
    features = width * lax.axis_size("head")
    half_heads, half_wide = heads // 2, width // 2
    state_flops = heads * rows * HEAD_DIM * HEAD_DIM
    block_flops = heads * rows * rows * HEAD_DIM
    whole = like((rows, width), BF16)
    packed = like((rows, half_wide), BF16)
    wide = like((rows, half_wide))
    states = like((PIECES, half_heads * HEAD_DIM // PIECES, HEAD_DIM))
    spots = [pl.ds(head * HEAD_DIM, HEAD_DIM) for head in range(half_heads)]
    cuts = 2
    cut_heads = half_heads // cuts
    cut_wide = half_wide // cuts

    def loads(half, sources, targets, sems):
        return [
            [
                pltpu.make_async_copy(a.at[:, half.columns(cut * cut_wide, cut_wide)], b.at[:, pl.ds(cut * cut_wide, cut_wide)], sems.at[cut, j])
                for j, (a, b) in enumerate(zip(sources, targets))
            ]
            for cut in range(cuts)
        ]

    def start(copies):
        for copy in copies:
            copy.start()

    def wait(copies):
        for copy in copies:
            copy.wait()

    def first_states(k_any, v_any, k_own_ref, v_own_ref, k_ref, v_ref, out_ref, own_sems, sems):
        half = Half(AWAY, heads)
        near = loads(Half(OWN, heads), (k_any, v_any), (k_own_ref, v_own_ref), own_sems)
        copies = loads(half, (k_any, v_any), (k_ref, v_ref), sems)
        for part in copies + near:
            start(part)
        for head, spot in enumerate(spots):
            if head % cut_heads == 0:
                wait(copies[head // cut_heads])
            half.put(out_ref, head, dot(k_ref[:, spot], v_ref[:, spot], ((0,), (0,))))
        for part in near:
            wait(part)

    k_own, v_own, k_away, v_away, send = call(
        first_states,
        [packed] * 4 + [states],
        (key_in, value),
        state_flops,
        (0, 1),
        (),
        [pltpu.SemaphoreType.DMA((cuts, 2))] * 2,
    )

    def second_states(k_ref, v_ref, out_ref):
        half = Half(OWN, heads)
        for head, spot in enumerate(spots):
            half.put(out_ref, head, dot(k_ref[:, spot], v_ref[:, spot], ((0,), (0,))))

    (keep,) = call(second_states, [states], (k_own, v_own), state_flops)

    def inner(ready, _):
        def kernel(q_ref, *refs):
            mask = causal(rows)
            for which in (OWN, AWAY):
                half = Half(which, heads)
                k_ref, v_ref, near_ref = refs[which], refs[2 + which], refs[4 + which]
                for head, spot in enumerate(spots):
                    q = q_ref[:, half.columns(head * HEAD_DIM, HEAD_DIM)]
                    scores = jnp.where(mask, dot(q, k_ref[:, spot], ((1,), (1,))), 0.0).astype(BF16)
                    near_ref[:, spot] = dot(scores, v_ref[:, spot], ((1,), (0,)))

        args = after(ready, query, k_own, k_away, v_own, v_away)
        return call(kernel, [wide] * 2, args, 4 * block_flops)

    def bring(ready, _):
        def kernel(c_any, own_ref, away_ref, sems):
            copies = [
                pltpu.make_async_copy(c_any.at[:, Half(which, heads).columns()], ref, sems.at[which])
                for which, ref in ((OWN, own_ref), (AWAY, away_ref))
            ]
            start(copies)
            wait(copies)

        return call(kernel, [packed] * 2, after(ready, cotangent), width * rows, (0,), (), [pltpu.SemaphoreType.DMA((2,))])

    own, away, extra = scan(keep, send, False, {"far": inner, "back": bring})
    near, cots = extra["far"], extra["back"]

    def mix(which, prefix):
        def kernel(q_ref, c_ref, near_ref, prefix_ref, mixed_ref, stats_ref, rounded_ref):
            half = Half(which, heads)
            square = jnp.zeros((rows, HEAD_DIM), F32)
            along = jnp.zeros((rows, HEAD_DIM), F32)
            for head, spot in enumerate(spots):
                cols = half.columns(head * HEAD_DIM, HEAD_DIM)
                prefix_b = half.get(prefix_ref, head)
                rounded_ref[spot, :] = prefix_b
                mixed = near_ref[:, spot] + dot(q_ref[:, cols], prefix_b, ((1,), (0,)))
                mixed_ref[:, spot] = mixed
                square += mixed * mixed
                along += c_ref[:, spot].astype(F32) * mixed
            stats_ref[0:1, :] = jnp.sum(square.T, axis=0, keepdims=True)
            stats_ref[1:2, :] = jnp.sum(along.T, axis=0, keepdims=True)

        args = (query, cots[which], near[which], prefix)
        outs = [wide, like((2, rows)), like((half_wide, HEAD_DIM), BF16)]
        return call(kernel, outs, args, state_flops, alias={2: 0})

    mixed_own, stats_own, prefix_own = mix(OWN, own)
    mixed_away, stats_away, prefix_away = mix(AWAY, away)
    mixed = (mixed_own, mixed_away)
    stats = stats_own + stats_away
    if lax.axis_size("head") == 2:
        stats = stats + exchange("head", lambda i: 1 - i, stats)
    else:
        stats = lax.psum(stats, "head")

    def token_scales(stats_ref):
        rstd = lax.rsqrt(stats_ref[0:1, :] / features + EPS)
        slope = rstd * rstd * (stats_ref[1:2, :] / features)
        return (
            jnp.broadcast_to(rstd, (HEAD_DIM, rows)).T,
            jnp.broadcast_to(slope, (HEAD_DIM, rows)).T,
        )

    def grads(which):
        def kernel(q_ref, c_ref, mixed_ref, stats_ref, d_ref, out_ref):
            half = Half(which, heads)
            rstd, slope = token_scales(stats_ref)
            for head, spot in enumerate(spots):
                cols = half.columns(head * HEAD_DIM, HEAD_DIM)
                d_mixed = (rstd * (c_ref[:, spot].astype(F32) - mixed_ref[:, spot] * slope)).astype(BF16)
                d_ref[:, spot] = d_mixed
                half.put(out_ref, head, dot(q_ref[:, cols], d_mixed, ((0,), (0,))))

        return call(kernel, [packed, states], (query, cots[which], mixed[which], stats), state_flops, alias={1: 0})

    d_away, g_send = grads(AWAY)
    d_own, g_keep = grads(OWN)

    def middle_head(q, k, v, d, prefix, mask, spot, gq_ref, gk_ref, gv_ref):
        scores = jnp.where(mask, dot(q, k, ((1,), (1,))), 0.0).astype(BF16)
        d_scores = jnp.where(mask, dot(d, v, ((1,), (1,))), 0.0).astype(BF16)
        gq_ref[:, spot] = (dot(d_scores, k, ((1,), (0,))) + dot(d, prefix, ((1,), (1,)))).astype(BF16)
        gk_ref[:, spot] = dot(d_scores, q, ((0,), (0,))).astype(BF16)
        gv_ref[:, spot] = dot(scores, d, ((0,), (0,))).astype(BF16)

    half_room = pltpu.VMEM((rows, half_wide), BF16)

    def middle_own(ready, _):
        def kernel(
            stats_ref, mixed_own_ref, mixed_away_ref, d_ref, prefix_ref, q_any, k_any, v_any,
            out_any, gq_ref, gk_ref, gv_ref, q_ref, k_ref, v_ref, in_sems, out_own_ref, out_away_ref, out_sems,
        ):
            half = Half(OWN, heads)
            copies = loads(half, (q_any, k_any, v_any), (q_ref, k_ref, v_ref), in_sems)
            for part in copies:
                start(part)
            rstd, _ = token_scales(stats_ref)
            outs = []
            for which, mixed_ref, out_ref in ((OWN, mixed_own_ref, out_own_ref), (AWAY, mixed_away_ref, out_away_ref)):
                for spot in spots:
                    out_ref[:, spot] = (mixed_ref[:, spot] * rstd).astype(BF16)
                there = out_any.at[:, Half(which, heads).columns()]
                outs.append(pltpu.make_async_copy(out_ref, there, out_sems.at[which]))
                outs[-1].start()
            mask = causal(rows)
            for head, spot in enumerate(spots):
                if head % cut_heads == 0:
                    wait(copies[head // cut_heads])
                middle_head(
                    q_ref[:, spot], k_ref[:, spot], v_ref[:, spot], d_ref[:, spot], prefix_ref[spot, :], mask, spot,
                    gq_ref, gk_ref, gv_ref,
                )
            wait(outs)

        args = after(ready, stats, *mixed, d_own, prefix_own, query, key_in, value)
        scratch = [half_room] * 3 + [pltpu.SemaphoreType.DMA((cuts, 3))] + [half_room] * 2 + [pltpu.SemaphoreType.DMA((2,))]
        return call(kernel, [whole, packed, packed, packed], args, 5 * block_flops, (5, 6, 7), (0,), scratch, {3: 1})

    def middle_away(ready, _):
        def kernel(d_ref, prefix_ref, q_any, k_any, v_any, gq_ref, gk_ref, gv_ref, q_ref, k_ref, v_ref, in_sems):
            copies = loads(Half(AWAY, heads), (q_any, k_any, v_any), (q_ref, k_ref, v_ref), in_sems)
            for part in copies:
                start(part)
            mask = causal(rows)
            for head, spot in enumerate(spots):
                if head % cut_heads == 0:
                    wait(copies[head // cut_heads])
                middle_head(
                    q_ref[:, spot], k_ref[:, spot], v_ref[:, spot], d_ref[:, spot], prefix_ref[spot, :], mask, spot,
                    gq_ref, gk_ref, gv_ref,
                )

        args = after(ready, d_away, prefix_away, query, key_in, value)
        scratch = [half_room] * 3 + [pltpu.SemaphoreType.DMA((cuts, 3))]
        return call(kernel, [packed] * 3, args, 5 * block_flops, (2, 3, 4), (), scratch, {0: 0})

    def turn(ready, extra):
        def kernel(own_ref, away_ref, k_any, v_any, out_any, k_own_ref, v_own_ref, k_away_ref, v_away_ref, sems):
            copies = []
            for which, ref, k_ref, v_ref in ((OWN, own_ref, k_own_ref, v_own_ref), (AWAY, away_ref, k_away_ref, v_away_ref)):
                cols = Half(which, heads).columns()
                copies.append(pltpu.make_async_copy(k_any.at[:, cols], k_ref, sems.at[which, 0]))
                copies.append(pltpu.make_async_copy(v_any.at[:, cols], v_ref, sems.at[which, 1]))
                copies.append(pltpu.make_async_copy(ref, out_any.at[:, cols], sems.at[which, 2]))
            start(copies)
            wait(copies)

        args = after(ready, extra["gather"][1], extra["far"][0], key_in, value)
        scratch = [pltpu.SemaphoreType.DMA((2, 3))]
        return call(kernel, [whole] + [packed] * 4, args, width * rows, (2, 3), (0,), scratch)

    beside = {"gather": middle_own, "far": middle_away, "back": turn}
    g_own, g_away, extra = scan(g_keep, g_send, True, beside)
    output, _, *near_own = extra["gather"]
    _, *near_away = extra["far"]
    grad_q, *known = extra["back"]

    def last(which, suffix, so_far):
        def kernel(k_ref, v_ref, near_k_ref, near_v_ref, suffix_ref, *refs):
            gk_any, gv_any, gk_ref, gv_ref, sems = refs[len(so_far) :]
            half = Half(which, heads)
            copies = []
            for head, spot in enumerate(spots):
                state = half.get(suffix_ref, head)
                gk_ref[:, spot] = (near_k_ref[:, spot] + dot(v_ref[:, spot], state, ((1,), (1,)))).astype(BF16)
                gv_ref[:, spot] = (near_v_ref[:, spot] + dot(k_ref[:, spot], state, ((1,), (0,)))).astype(BF16)
                if (head + 1) % cut_heads == 0:
                    cut = head // cut_heads
                    here = pl.ds(cut * cut_wide, cut_wide)
                    there = half.columns(cut * cut_wide, cut_wide)
                    for j, (ref, out) in enumerate(((gk_ref, gk_any), (gv_ref, gv_any))):
                        copies.append(pltpu.make_async_copy(ref.at[:, here], out.at[:, there], sems.at[cut, j]))
                        copies[-1].start()
            wait(copies)

        args = (*known[2 * which : 2 * which + 2], *(near_own, near_away)[which], suffix, *so_far)
        return call(
            kernel,
            [whole, whole],
            args,
            2 * state_flops,
            tuple(5 + i for i in range(len(so_far))),
            (0, 1),
            [pltpu.VMEM((rows, half_wide), BF16)] * 2 + [pltpu.SemaphoreType.DMA((cuts, 2))],
            {5 + i: i for i in range(len(so_far))},
        )

    grad_k, grad_v = last(AWAY, g_away, tuple(last(OWN, g_own, ())))
    return output, grad_q, grad_k, grad_v


def solution(mesh):
    spec = P("seq", "head")
    return jax.shard_map(local, mesh=mesh, in_specs=(spec,) * 4, out_specs=(spec,) * 4, check_vma=False)
```

time: 221 us -> 55.9 us (0.25)
  waiting for transfers between devices: 157 us -> 16.3 us
  starting transfers between devices: 0.08 us -> 23.4 us
  other arithmetic: 19.9 us -> 0.35 us
  Pallas kernels: 0 us -> 14.7 us
  between operations: 14.3 us -> 0.86 us
  matrix products: 12.3 us -> 0 us
  local copies, waits for them, and re-layouts: 11.1 us -> 0.04 us
  blocking collectives: 4.92 us -> 0 us
    all_gather x2 -> x0, waiting for transfers between devices: 157 us -> none  [entering(): gathered = lax.all_gather(part, axis)]
    ppermute x0 -> x19, starting transfers between devices: none -> 23.4 us  [exchange(): lax.ppermute(array, axis, [(i, partner(i)) for i in range(lax.axis_size(a...]
    add x15 -> x8, other arithmetic: 17.6 us -> 0.26 us  [the longest x2 0.13 us: scan(): start = start + jnp.where(team ^ other < team ^ r, parts[other], 0.0)]
    ppermute x0 -> x19, waiting for transfers between devices: none -> 16.3 us  [exchange(): lax.ppermute(array, axis, [(i, partner(i)) for i in range(lax.axis_size(a...]
    pallas_call x0 -> x13, Pallas kernels: none -> 14.7 us  [call(): pl.pallas_call(kernel, out_shape=outs, in_specs=[HBM if i in in_hbm else...]
    dot_general x12 -> x0, matrix products: 12.3 us -> none  [the longest x1 2.57 us: local(): jnp.einsum('thd,hde->the', queries, prefix_b, preferred_element_type=jnp....]
    unnamed x27 -> x2, local copies, waits for them, and re-layouts: 8.42 us -> 0.01 us
    psum x1 -> x0, blocking collectives: 4.92 us -> none  [local(): square = lax.psum(local_square, 'head')]
  transfers between devices with their start and end apart: 2 -> 19, of which waited for: 2 -> 15; matrix products, arithmetic and copies ran while one was open for 5% -> 0% of each run, Pallas kernels for 0% -> 20%
where the time goes in v3:
time: 55.9 us; the launch traced here: 55.7 us
  starting transfers between devices  23.4 us (42%)
  waiting for transfers between devices  16.3 us (29%)
  Pallas kernels  14.7 us (26%)
  between operations  0.86 us (2%)
    ppermute x19, starting transfers between devices, exchange(): lax.ppermute(array, axis, [(i, partner(i)) for i in range(lax.axis_size(a...  23.4 us
    ppermute x19, waiting for transfers between devices, exchange(): lax.ppermute(array, axis, [(i, partner(i)) for i in range(lax.axis_size(a...  16.3 us
    pallas_call x13, Pallas kernels, call(): pl.pallas_call(kernel, out_shape=outs, in_specs=[HBM if i in in_hbm else...  14.7 us
  transfers between devices with their start and end apart: 19, of which 15 were waited for; matrix products, arithmetic and copies ran while one was open for 0% of the time, Pallas kernels for 20%

profile of v3, /device:TPU:0, one launch (start us, length us, event | category | flops | bytes accessed | tf_op | source)
XLA Modules:
  0.0 55.7 jit_solution(4826519776710477903)
XLA Ops:
  0.6 1.6 %shard_map.75 = (bf16[256,512]{1,0:T(8,128)(2,1)S(1)}, bf16[256,512]{1,0:T(8,128)(2,1)S(1)}, bf16[256,512]{1,0:T(8,128)(2,1)S(1)}, bf16[256,512]{1,0:T(8,128)(2,1)S(1)}, f32[4,128,128]{2,1,0:T(8,128)S(1)}) custom-call(bf16[256,1024]{1,0:T(8,128)(2,1)} %k_any.4, bf16[256,1024]{1,0:T(8,128)(2,1)} %v_any.4), custom_call_target="tpu_custom_call" | custom-call | flops 33554432 | bytes 2359296 | tf_op jit(solution)/shard_map/pallas_call | solution.py:65
  4.0 4.0 %collective-permute-start.3 = (f32[128,128]{1,0:T(8,128)S(1)}, f32[128,128]{1,0:T(8,128)S(1)}, u32[]{:S(2)}, u32[]{:S(2)}) collective-permute-start(f32[128,128]{1,0:T(8,128)S(1)} %get-tuple-element.181), channel_id=1, source_target_pairs={{0,12},{2,14},{4,8},{6,10},{8,4},{10,6},{12,0},{14,2},{16,28},{18,... | collective-permute-start | bytes 196616 | tf_op jit(solution)/shard_map/ppermute | solution.py:78
  8.6 1.8 %collective-permute-done.3 = f32[128,128]{1,0:T(8,128)S(1)} collective-permute-done((f32[128,128]{1,0:T(8,128)S(1)}, f32[128,128]{1,0:T(8,128)S(1)}, u32[]{:S(2)}, u32[]{:S(2)}) %collective-permute-start.3) | collective-permute-done | bytes 65568 | tf_op jit(solution)/shard_map/ppermute | solution.py:78
  10.3 1.9 %collective-permute-done.2 = f32[128,128]{1,0:T(8,128)S(1)} collective-permute-done((f32[128,128]{1,0:T(8,128)S(1)}, f32[128,128]{1,0:T(8,128)S(1)}, u32[]{:S(2)}, u32[]{:S(2)}) %collective-permute-start.2) | collective-permute-done | bytes 65568 | tf_op jit(solution)/shard_map/ppermute | solution.py:78
  12.7 2.7 %collective-permute-start.4 = (f32[128,128]{1,0:T(8,128)S(1)}, f32[128,128]{1,0:T(8,128)S(1)}, u32[]{:S(2)}, u32[]{:S(2)}) collective-permute-start(f32[128,128]{1,0:T(8,128)S(1)} %add_add_fusion.1), channel_id=1, source_target_pairs={{0,16},{2,18},{4,20},{6,22},{8,24},{10,26},{12,28},{14,30},{16,0},... | collective-permute-start | bytes 196616 | tf_op jit(solution)/shard_map/ppermute | solution.py:78
  16.3 1.6 %collective-permute-done.4 = f32[128,128]{1,0:T(8,128)S(1)} collective-permute-done((f32[128,128]{1,0:T(8,128)S(1)}, f32[128,128]{1,0:T(8,128)S(1)}, u32[]{:S(2)}, u32[]{:S(2)}) %collective-permute-start.4) | collective-permute-done | bytes 65568 | tf_op jit(solution)/shard_map/ppermute | solution.py:78
  18.0 1.8 %collective-permute-start.5 = (f32[128,128]{1,0:T(8,128)S(1)}, f32[128,128]{1,0:T(8,128)S(1)}, u32[]{:S(2)}, u32[]{:S(2)}) collective-permute-start(f32[128,128]{1,0:T(8,128)S(1)} %get-tuple-element.174), channel_id=1, source_target_pairs={{0,12},{2,14},{4,8},{6,10},{8,4},{10,6},{12,0},{14,2},{16,28},{18,... | collective-permute-start | bytes 196616 | tf_op jit(solution)/shard_map/ppermute | solution.py:78
  19.8 1.3 %collective-permute-start.6 = (f32[128,128]{1,0:T(8,128)S(1)}, f32[128,128]{1,0:T(8,128)S(1)}, u32[]{:S(2)}, u32[]{:S(2)}) collective-permute-start(f32[128,128]{1,0:T(8,128)S(1)} %get-tuple-element.173), channel_id=1, source_target_pairs={{0,4},{2,6},{4,0},{6,2},{8,12},{10,14},{12,8},{14,10},{16,20},{18,... | collective-permute-start | bytes 196616 | tf_op jit(solution)/shard_map/ppermute | solution.py:78
  21.5 1.0 %shard_map.78 = (bf16[256,512]{1,0:T(8,128)(2,1)S(1)}, bf16[256,512]{1,0:T(8,128)(2,1)S(1)}) custom-call(bf16[256,1024]{1,0:T(8,128)(2,1)} %c_any), custom_call_target="tpu_custom_call" | custom-call | flops 262144 | bytes 1048576 | tf_op jit(solution)/shard_map/pallas_call | solution.py:65
  24.0 1.3 %collective-permute-done.7 = f32[128,128]{1,0:T(8,128)S(1)} collective-permute-done((f32[128,128]{1,0:T(8,128)S(1)}, f32[128,128]{1,0:T(8,128)S(1)}, u32[]{:S(2)}, u32[]{:S(2)}) %collective-permute-start.7) | collective-permute-done | bytes 65568 | tf_op jit(solution)/shard_map/ppermute | solution.py:78
  25.9 1.1 %collective-permute-done.8.prefix_ref = f32[4,128,128]{2,1,0:T(8,128)S(1)} collective-permute-done((f32[4,128,128]{2,1,0:T(8,128)S(1)}, f32[4,128,128]{2,1,0:T(8,128)S(1)}, u32[]{:S(2)}, u32[]{:S(2)}) %collective-permute-start.8) | collective-permute-done | bytes 262176 | tf_op jit(solution)/shard_map/ppermute | solution.py:78
  27.5 1.6 %collective-permute-start.9 = (f32[2,256]{1,0:T(2,128)S(1)}, f32[2,256]{1,0:T(2,128)S(1)}, u32[]{:S(2)}, u32[]{:S(2)}) collective-permute-start(f32[2,256]{1,0:T(2,128)S(1)} %add.132), channel_id=1, source_target_pairs={{0,1},{1,0},{2,3},{3,2},{4,5},{5,4},{6,7},{7,6},{8,9},{9,8},{10,11... | collective-permute-start | bytes 6152 | tf_op jit(solution)/shard_map/ppermute | solution.py:78
  29.1 2.1 %collective-permute-done.9 = f32[2,256]{1,0:T(2,128)S(1)} collective-permute-done((f32[2,256]{1,0:T(2,128)S(1)}, f32[2,256]{1,0:T(2,128)S(1)}, u32[]{:S(2)}, u32[]{:S(2)}) %collective-permute-start.9) | collective-permute-done | bytes 2080 | tf_op jit(solution)/shard_map/ppermute | solution.py:78
  32.1 1.1 %collective-permute-done.10 = f32[4,128,128]{2,1,0:T(8,128)S(1)} collective-permute-done((f32[4,128,128]{2,1,0:T(8,128)S(1)}, f32[4,128,128]{2,1,0:T(8,128)S(1)}, u32[]{:S(2)}, u32[]{:S(2)}) %collective-permute-start.10) | collective-permute-done | bytes 262176 | tf_op jit(solution)/shard_map/ppermute | solution.py:78
  34.1 1.1 %collective-permute-start.12 = (f32[128,128]{1,0:T(8,128)S(1)}, f32[128,128]{1,0:T(8,128)S(1)}, u32[]{:S(2)}, u32[]{:S(2)}) collective-permute-start(f32[128,128]{1,0:T(8,128)S(1)} %get-tuple-element.178), channel_id=1, source_target_pairs={{0,4},{2,6},{4,0},{6,2},{8,12},{10,14},{12,8},{14,10},{16,20},{18,... | collective-permute-start | bytes 196616 | tf_op jit(solution)/shard_map/ppermute | solution.py:78
  35.2 1.6 %collective-permute-start.13 = (f32[128,128]{1,0:T(8,128)S(1)}, f32[128,128]{1,0:T(8,128)S(1)}, u32[]{:S(2)}, u32[]{:S(2)}) collective-permute-start(f32[128,128]{1,0:T(8,128)S(1)} %get-tuple-element.179), channel_id=1, source_target_pairs={{0,8},{2,10},{4,12},{6,14},{8,0},{10,2},{12,4},{14,6},{16,24},{18,... | collective-permute-start | bytes 196616 | tf_op jit(solution)/shard_map/ppermute | solution.py:78
  36.8 2.8 %shard_map.83 = (bf16[256,1024]{1,0:T(8,128)(2,1)}, bf16[256,512]{1,0:T(8,128)(2,1)S(1)}, bf16[256,512]{1,0:T(8,128)(2,1)S(1)}, bf16[256,512]{1,0:T(8,128)(2,1)S(1)}) custom-call(f32[2,256]{1,0:T(2,128)S(1)} %add.133.stats_ref, f32[256,512]{1,0:T(8,128)S(1)} %get-tuple-element.113.mixed_ref.mixed_own_ref, ...), custom_call_target="tpu_custom_call", output_to_operand_aliasing={{1}: (3, {})} | custom-call | flops 335544320 | bytes 4327424 | tf_op jit(solution)/shard_map/pallas_call | solution.py:65
  39.7 3.2 %collective-permute-start.14 = (f32[128,128]{1,0:T(8,128)S(1)}, f32[128,128]{1,0:T(8,128)S(1)}, u32[]{:S(2)}, u32[]{:S(2)}) collective-permute-start(f32[128,128]{1,0:T(8,128)S(1)} %add_add_fusion), channel_id=1, source_target_pairs={{0,16},{2,18},{4,20},{6,22},{8,24},{10,26},{12,28},{14,30},{16,0},... | collective-permute-start | bytes 196616 | tf_op jit(solution)/shard_map/ppermute | solution.py:78
  42.9 2.7 %shard_map.84 = (bf16[256,512]{1,0:T(8,128)(2,1)S(1)}, bf16[256,512]{1,0:T(8,128)(2,1)S(1)}, bf16[256,512]{1,0:T(8,128)(2,1)S(1)}) custom-call(bf16[256,512]{1,0:T(8,128)(2,1)S(1)} %get-tuple-element.128.d_ref, bf16[512,128]{1,0:T(8,128)(2,1)S(1)} %get-tuple-element.129.prefix_ref, bf16[256,1024]{1,0:T(8,128)(2,1)} %q_any.1, ...), custom_call_target="tpu_custom_call", output_to_operand_aliasing={{0}: (0, {})} | custom-call | flops 335544320 | bytes 2752512 | tf_op jit(solution)/shard_map/pallas_call | solution.py:65
  45.8 1.6 %collective-permute-start.15 = (f32[128,128]{1,0:T(8,128)S(1)}, f32[128,128]{1,0:T(8,128)S(1)}, u32[]{:S(2)}, u32[]{:S(2)}) collective-permute-start(f32[128,128]{1,0:T(8,128)S(1)} %get-tuple-element.171), channel_id=1, source_target_pairs={{0,12},{2,14},{4,8},{6,10},{8,4},{10,6},{12,0},{14,2},{16,28},{18,... | collective-permute-start | bytes 196616 | tf_op jit(solution)/shard_map/ppermute | solution.py:78
  47.4 1.3 %collective-permute-start.16 = (f32[128,128]{1,0:T(8,128)S(1)}, f32[128,128]{1,0:T(8,128)S(1)}, u32[]{:S(2)}, u32[]{:S(2)}) collective-permute-start(f32[128,128]{1,0:T(8,128)S(1)} %get-tuple-element.170), channel_id=1, source_target_pairs={{0,4},{2,6},{4,0},{6,2},{8,12},{10,14},{12,8},{14,10},{16,20},{18,... | collective-permute-start | bytes 196616 | tf_op jit(solution)/shard_map/ppermute | solution.py:78
  49.4 1.4 %shard_map.85 = (bf16[256,1024]{1,0:T(8,128)(2,1)}, bf16[256,512]{1,0:T(8,128)(2,1)S(1)}, bf16[256,512]{1,0:T(8,128)(2,1)S(1)}, bf16[256,512]{1,0:T(8,128)(2,1)S(1)}, bf16[256,512]{1,0:T(8,128)(2,1)S(1)}) custom-call(bf16[256,512]{1,0:T(8,128)(2,1)S(1)} %get-tuple-element.139.own_ref, bf16[256,512]{1,0:T(8,128)(2,1)S(1)} %get-tuple-element.140.away_ref, ...), custom_call_target="tpu_custom_call" | custom-call | flops 262144 | bytes 3145728 | tf_op jit(solution)/shard_map/pallas_call | solution.py:65
  51.7 1.2 %collective-permute-done.17 = f32[128,128]{1,0:T(8,128)S(1)} collective-permute-done((f32[128,128]{1,0:T(8,128)S(1)}, f32[128,128]{1,0:T(8,128)S(1)}, u32[]{:S(2)}, u32[]{:S(2)}) %collective-permute-start.17) | collective-permute-done | bytes 65568 | tf_op jit(solution)/shard_map/ppermute | solution.py:78
  53.1 1.0 %shard_map.86 = (bf16[256,1024]{1,0:T(8,128)(2,1)}, bf16[256,1024]{1,0:T(8,128)(2,1)}) custom-call(bf16[256,512]{1,0:T(8,128)(2,1)S(1)} %get-tuple-element.154.k_ref, bf16[256,512]{1,0:T(8,128)(2,1)S(1)} %get-tuple-element.155.v_ref, bf16[256,512]{1,0:T(8,128)(2,1)S(1)} %get-tuple-element.156.near_k_ref, bf16[256,512]{1,0:T(8,128)(2,1)S(1)} %get-tuple-element.157.near_v_ref, ...), custom_call_target="tpu_custom_call" | custom-call | flops 67108864 | bytes 2359296 | tf_op jit(solution)/shard_map/pallas_call | solution.py:65
  (43 shorter events, 12.0 us)
Async XLA Ops:
  2.2 1.7 %collective-permute-start = (f32[4,128,128]{2,1,0:T(8,128)S(1)}, f32[4,128,128]{2,1,0:T(8,128)S(1)}, u32[]{:S(2)}, u32[]{:S(2)}) collective-permute-start(f32[4,128,128]{2,1,0:T(8,128)S(1)} %get-tuple-element.85), channel_id=1, source_target_pairs={{0,2},{2,0},{4,6},{6,4},{8,10},{10,8},{12,14},{14,12},{16,18},{18,... | collective-permute-start | bytes 786440 | tf_op jit(solution)/shard_map/ppermute | solution.py:78
  3.9 11.4 %copy-start = (bf16[256,1024]{1,0:T(8,128)(2,1)S(1)}, bf16[256,1024]{1,0:T(8,128)(2,1)}, u32[]{:S(2)}) copy-start(bf16[256,1024]{1,0:T(8,128)(2,1)} %q_any.1) | copy-start | bytes 1572868
  4.0 6.4 %collective-permute-start.3 = (f32[128,128]{1,0:T(8,128)S(1)}, f32[128,128]{1,0:T(8,128)S(1)}, u32[]{:S(2)}, u32[]{:S(2)}) collective-permute-start(f32[128,128]{1,0:T(8,128)S(1)} %get-tuple-element.181), channel_id=1, source_target_pairs={{0,12},{2,14},{4,8},{6,10},{8,4},{10,6},{12,0},{14,2},{16,28},{18,... | collective-permute-start | bytes 196616 | tf_op jit(solution)/shard_map/ppermute | solution.py:78
  7.9 4.3 %collective-permute-start.2 = (f32[128,128]{1,0:T(8,128)S(1)}, f32[128,128]{1,0:T(8,128)S(1)}, u32[]{:S(2)}, u32[]{:S(2)}) collective-permute-start(f32[128,128]{1,0:T(8,128)S(1)} %get-tuple-element.182), channel_id=1, source_target_pairs={{0,8},{2,10},{4,12},{6,14},{8,0},{10,2},{12,4},{14,6},{16,24},{18,... | collective-permute-start | bytes 196616 | tf_op jit(solution)/shard_map/ppermute | solution.py:78
  8.4 4.3 %collective-permute-start.1 = (f32[128,128]{1,0:T(8,128)S(1)}, f32[128,128]{1,0:T(8,128)S(1)}, u32[]{:S(2)}, u32[]{:S(2)}) collective-permute-start(f32[128,128]{1,0:T(8,128)S(1)} %get-tuple-element.183), channel_id=1, source_target_pairs={{0,4},{2,6},{4,0},{6,2},{8,12},{10,14},{12,8},{14,10},{16,20},{18,... | collective-permute-start | bytes 196616 | tf_op jit(solution)/shard_map/ppermute | solution.py:78
  12.7 5.2 %collective-permute-start.4 = (f32[128,128]{1,0:T(8,128)S(1)}, f32[128,128]{1,0:T(8,128)S(1)}, u32[]{:S(2)}, u32[]{:S(2)}) collective-permute-start(f32[128,128]{1,0:T(8,128)S(1)} %add_add_fusion.1), channel_id=1, source_target_pairs={{0,16},{2,18},{4,20},{6,22},{8,24},{10,26},{12,28},{14,30},{16,0},... | collective-permute-start | bytes 196616 | tf_op jit(solution)/shard_map/ppermute | solution.py:78
  18.0 5.2 %collective-permute-start.5 = (f32[128,128]{1,0:T(8,128)S(1)}, f32[128,128]{1,0:T(8,128)S(1)}, u32[]{:S(2)}, u32[]{:S(2)}) collective-permute-start(f32[128,128]{1,0:T(8,128)S(1)} %get-tuple-element.174), channel_id=1, source_target_pairs={{0,12},{2,14},{4,8},{6,10},{8,4},{10,6},{12,0},{14,2},{16,28},{18,... | collective-permute-start | bytes 196616 | tf_op jit(solution)/shard_map/ppermute | solution.py:78
  19.8 4.3 %collective-permute-start.6 = (f32[128,128]{1,0:T(8,128)S(1)}, f32[128,128]{1,0:T(8,128)S(1)}, u32[]{:S(2)}, u32[]{:S(2)}) collective-permute-start(f32[128,128]{1,0:T(8,128)S(1)} %get-tuple-element.173), channel_id=1, source_target_pairs={{0,4},{2,6},{4,0},{6,2},{8,12},{10,14},{12,8},{14,10},{16,20},{18,... | collective-permute-start | bytes 196616 | tf_op jit(solution)/shard_map/ppermute | solution.py:78
  21.1 4.3 %collective-permute-start.7 = (f32[128,128]{1,0:T(8,128)S(1)}, f32[128,128]{1,0:T(8,128)S(1)}, u32[]{:S(2)}, u32[]{:S(2)}) collective-permute-start(f32[128,128]{1,0:T(8,128)S(1)} %get-tuple-element.175), channel_id=1, source_target_pairs={{0,8},{2,10},{4,12},{6,14},{8,0},{10,2},{12,4},{14,6},{16,24},{18,... | collective-permute-start | bytes 196616 | tf_op jit(solution)/shard_map/ppermute | solution.py:78
  25.4 1.6 %collective-permute-start.8 = (f32[4,128,128]{2,1,0:T(8,128)S(1)}, f32[4,128,128]{2,1,0:T(8,128)S(1)}, u32[]{:S(2)}, u32[]{:S(2)}) collective-permute-start(f32[4,128,128]{2,1,0:T(8,128)S(1)} %get-tuple-element.166), channel_id=1, source_target_pairs={{0,2},{2,0},{4,6},{6,4},{8,10},{10,8},{12,14},{14,12},{16,18},{18,... | collective-permute-start | bytes 786440 | tf_op jit(solution)/shard_map/ppermute | solution.py:78
  27.5 3.7 %collective-permute-start.9 = (f32[2,256]{1,0:T(2,128)S(1)}, f32[2,256]{1,0:T(2,128)S(1)}, u32[]{:S(2)}, u32[]{:S(2)}) collective-permute-start(f32[2,256]{1,0:T(2,128)S(1)} %add.132), channel_id=1, source_target_pairs={{0,1},{1,0},{2,3},{3,2},{4,5},{5,4},{6,7},{7,6},{8,9},{9,8},{10,11... | collective-permute-start | bytes 6152 | tf_op jit(solution)/shard_map/ppermute | solution.py:78
  31.6 1.6 %collective-permute-start.10 = (f32[4,128,128]{2,1,0:T(8,128)S(1)}, f32[4,128,128]{2,1,0:T(8,128)S(1)}, u32[]{:S(2)}, u32[]{:S(2)}) collective-permute-start(f32[4,128,128]{2,1,0:T(8,128)S(1)} %get-tuple-element.109), channel_id=1, source_target_pairs={{0,2},{2,0},{4,6},{6,4},{8,10},{10,8},{12,14},{14,12},{16,18},{18,... | collective-permute-start | bytes 786440 | tf_op jit(solution)/shard_map/ppermute | solution.py:78
  33.2 6.4 %collective-permute-start.11 = (f32[128,128]{1,0:T(8,128)S(1)}, f32[128,128]{1,0:T(8,128)S(1)}, u32[]{:S(2)}, u32[]{:S(2)}) collective-permute-start(f32[128,128]{1,0:T(8,128)S(1)} %get-tuple-element.180), channel_id=1, source_target_pairs={{0,12},{2,14},{4,8},{6,10},{8,4},{10,6},{12,0},{14,2},{16,28},{18,... | collective-permute-start | bytes 196616 | tf_op jit(solution)/shard_map/ppermute | solution.py:78
  34.1 5.5 %collective-permute-start.12 = (f32[128,128]{1,0:T(8,128)S(1)}, f32[128,128]{1,0:T(8,128)S(1)}, u32[]{:S(2)}, u32[]{:S(2)}) collective-permute-start(f32[128,128]{1,0:T(8,128)S(1)} %get-tuple-element.178), channel_id=1, source_target_pairs={{0,4},{2,6},{4,0},{6,2},{8,12},{10,14},{12,8},{14,10},{16,20},{18,... | collective-permute-start | bytes 196616 | tf_op jit(solution)/shard_map/ppermute | solution.py:78
  35.2 4.4 %collective-permute-start.13 = (f32[128,128]{1,0:T(8,128)S(1)}, f32[128,128]{1,0:T(8,128)S(1)}, u32[]{:S(2)}, u32[]{:S(2)}) collective-permute-start(f32[128,128]{1,0:T(8,128)S(1)} %get-tuple-element.179), channel_id=1, source_target_pairs={{0,8},{2,10},{4,12},{6,14},{8,0},{10,2},{12,4},{14,6},{16,24},{18,... | collective-permute-start | bytes 196616 | tf_op jit(solution)/shard_map/ppermute | solution.py:78
  39.7 6.0 %collective-permute-start.14 = (f32[128,128]{1,0:T(8,128)S(1)}, f32[128,128]{1,0:T(8,128)S(1)}, u32[]{:S(2)}, u32[]{:S(2)}) collective-permute-start(f32[128,128]{1,0:T(8,128)S(1)} %add_add_fusion), channel_id=1, source_target_pairs={{0,16},{2,18},{4,20},{6,22},{8,24},{10,26},{12,28},{14,30},{16,0},... | collective-permute-start | bytes 196616 | tf_op jit(solution)/shard_map/ppermute | solution.py:78
  45.8 5.2 %collective-permute-start.15 = (f32[128,128]{1,0:T(8,128)S(1)}, f32[128,128]{1,0:T(8,128)S(1)}, u32[]{:S(2)}, u32[]{:S(2)}) collective-permute-start(f32[128,128]{1,0:T(8,128)S(1)} %get-tuple-element.171), channel_id=1, source_target_pairs={{0,12},{2,14},{4,8},{6,10},{8,4},{10,6},{12,0},{14,2},{16,28},{18,... | collective-permute-start | bytes 196616 | tf_op jit(solution)/shard_map/ppermute | solution.py:78
  47.4 4.3 %collective-permute-start.16 = (f32[128,128]{1,0:T(8,128)S(1)}, f32[128,128]{1,0:T(8,128)S(1)}, u32[]{:S(2)}, u32[]{:S(2)}) collective-permute-start(f32[128,128]{1,0:T(8,128)S(1)} %get-tuple-element.170), channel_id=1, source_target_pairs={{0,4},{2,6},{4,0},{6,2},{8,12},{10,14},{12,8},{14,10},{16,20},{18,... | collective-permute-start | bytes 196616 | tf_op jit(solution)/shard_map/ppermute | solution.py:78
  48.7 4.3 %collective-permute-start.17 = (f32[128,128]{1,0:T(8,128)S(1)}, f32[128,128]{1,0:T(8,128)S(1)}, u32[]{:S(2)}, u32[]{:S(2)}) collective-permute-start(f32[128,128]{1,0:T(8,128)S(1)} %get-tuple-element.172), channel_id=1, source_target_pairs={{0,8},{2,10},{4,12},{6,14},{8,0},{10,2},{12,4},{14,6},{16,24},{18,... | collective-permute-start | bytes 196616 | tf_op jit(solution)/shard_map/ppermute | solution.py:78
  53.0 1.6 %collective-permute-start.18 = (f32[4,128,128]{2,1,0:T(8,128)S(1)}, f32[4,128,128]{2,1,0:T(8,128)S(1)}, u32[]{:S(2)}, u32[]{:S(2)}) collective-permute-start(f32[4,128,128]{2,1,0:T(8,128)S(1)} %get-tuple-element.163), channel_id=1, source_target_pairs={{0,2},{2,0},{4,6},{6,4},{8,10},{10,8},{12,14},{14,12},{16,18},{18,... | collective-permute-start | bytes 786440 | tf_op jit(solution)/shard_map/ppermute | solution.py:78

commit v4 on v3

--- a/solution.py
+++ b/solution.py
@@ -14,6 +14,11 @@
 OWN, AWAY = 0, 1
 
 PIECES = 4
+ORDER = (2, 1, 3)
+
+
+def crosses(bits):
+    return (bits & 1) ^ (bits >> 1)
 
 
 def split(block):
@@ -23,7 +28,8 @@
 class Half:
     def __init__(self, which, heads):
         core, self.team, _ = split(lax.axis_index("seq"))
-        number = core if which == OWN else 1 - core
+        own = core ^ crosses(self.team)
+        number = own if which == OWN else 1 - own
         self.heads = heads // 2
         self.base = number * (self.heads * HEAD_DIM)
         self.piece_rows = self.heads * HEAD_DIM // PIECES
@@ -95,9 +101,11 @@
         return come
 
     def to_team(pieces, name):
-        come = [exchange("seq", lambda i: i ^ (2 * r), pieces[r]) for r in range(1, PIECES)]
-        come[-1] = beside_of(name, pieces[-1], come[-1])
-        return [pieces[0], *come]
+        come = {0: pieces[0]}
+        for r in ORDER:
+            come[r] = exchange("seq", lambda i: i ^ (2 * r) ^ crosses(r), pieces[r])
+        come[r] = beside_of(name, pieces[r], come[r])
+        return [come[r] for r in range(PIECES)]
 
     got = exchange("seq", lambda i: i ^ 1, send)
     both = keep + got

time: 55.9 us -> 55.2 us (0.987)
  starting transfers between devices: 23.4 us -> 22.2 us
  waiting for transfers between devices: 16.3 us -> 16.9 us
    ppermute x19, starting transfers between devices: 23.4 us -> 22.2 us  [exchange(): lax.ppermute(array, axis, [(i, partner(i)) for i in range(lax.axis_size(a...]
    ppermute x19, waiting for transfers between devices: 16.3 us -> 16.9 us  [exchange(): lax.ppermute(array, axis, [(i, partner(i)) for i in range(lax.axis_size(a...]
  transfers between devices with their start and end apart: 19 -> 19, of which waited for: 15 -> 14; matrix products, arithmetic and copies ran while one was open for 0% -> 0% of each run, Pallas kernels for 20% -> 20%
where the time goes in v4:
time: 55.2 us; the launch traced here: 54.9 us
  starting transfers between devices  22.2 us (40%)
  waiting for transfers between devices  16.9 us (31%)
  Pallas kernels  14.7 us (27%)
  between operations  0.82 us (1%)
    ppermute x19, starting transfers between devices, exchange(): lax.ppermute(array, axis, [(i, partner(i)) for i in range(lax.axis_size(a...  22.2 us
    ppermute x19, waiting for transfers between devices, exchange(): lax.ppermute(array, axis, [(i, partner(i)) for i in range(lax.axis_size(a...  16.9 us
    pallas_call x13, Pallas kernels, call(): pl.pallas_call(kernel, out_shape=outs, in_specs=[HBM if i in in_hbm else...  14.7 us
  transfers between devices with their start and end apart: 19, of which 14 were waited for; matrix products, arithmetic and copies ran while one was open for 0% of the time, Pallas kernels for 20%

profile of v4, /device:TPU:0, one launch (start us, length us, event | category | flops | bytes accessed | tf_op | source)
XLA Modules:
  0.0 54.9 jit_solution(16803192201334067977)
XLA Ops:
  0.6 1.6 %shard_map.75 = (bf16[256,512]{1,0:T(8,128)(2,1)S(1)}, bf16[256,512]{1,0:T(8,128)(2,1)S(1)}, bf16[256,512]{1,0:T(8,128)(2,1)S(1)}, bf16[256,512]{1,0:T(8,128)(2,1)S(1)}, f32[4,128,128]{2,1,0:T(8,128)S(1)}) custom-call(bf16[256,1024]{1,0:T(8,128)(2,1)} %k_any.4, bf16[256,1024]{1,0:T(8,128)(2,1)} %v_any.4), custom_call_target="tpu_custom_call" | custom-call | flops 33554432 | bytes 2359296 | tf_op jit(solution)/shard_map/pallas_call | solution.py:71
  4.0 4.0 %collective-permute-start.3 = (f32[128,128]{1,0:T(8,128)S(1)}, f32[128,128]{1,0:T(8,128)S(1)}, u32[]{:S(2)}, u32[]{:S(2)}) collective-permute-start(f32[128,128]{1,0:T(8,128)S(1)} %get-tuple-element.181), channel_id=1, source_target_pairs={{0,12},{2,14},{4,8},{6,10},{8,4},{10,6},{12,0},{14,2},{16,28},{18,... | collective-permute-start | bytes 196616 | tf_op jit(solution)/shard_map/ppermute | solution.py:84
  8.3 2.0 %collective-permute-done.3 = f32[128,128]{1,0:T(8,128)S(1)} collective-permute-done((f32[128,128]{1,0:T(8,128)S(1)}, f32[128,128]{1,0:T(8,128)S(1)}, u32[]{:S(2)}, u32[]{:S(2)}) %collective-permute-start.3) | collective-permute-done | bytes 65568 | tf_op jit(solution)/shard_map/ppermute | solution.py:84
  10.3 2.0 %collective-permute-done.2 = f32[128,128]{1,0:T(8,128)S(1)} collective-permute-done((f32[128,128]{1,0:T(8,128)S(1)}, f32[128,128]{1,0:T(8,128)S(1)}, u32[]{:S(2)}, u32[]{:S(2)}) %collective-permute-start.2) | collective-permute-done | bytes 65568 | tf_op jit(solution)/shard_map/ppermute | solution.py:84
  12.3 2.7 %collective-permute-start.4 = (f32[128,128]{1,0:T(8,128)S(1)}, f32[128,128]{1,0:T(8,128)S(1)}, u32[]{:S(2)}, u32[]{:S(2)}) collective-permute-start(f32[128,128]{1,0:T(8,128)S(1)} %add_add_fusion.1), channel_id=1, source_target_pairs={{0,16},{2,18},{4,20},{6,22},{8,24},{10,26},{12,28},{14,30},{16,0},... | collective-permute-start | bytes 196616 | tf_op jit(solution)/shard_map/ppermute | solution.py:84
  15.9 3.0 %collective-permute-done.4 = f32[128,128]{1,0:T(8,128)S(1)} collective-permute-done((f32[128,128]{1,0:T(8,128)S(1)}, f32[128,128]{1,0:T(8,128)S(1)}, u32[]{:S(2)}, u32[]{:S(2)}) %collective-permute-start.4) | collective-permute-done | bytes 65568 | tf_op jit(solution)/shard_map/ppermute | solution.py:84
  19.0 1.0 %collective-permute-start.5 = (f32[128,128]{1,0:T(8,128)S(1)}, f32[128,128]{1,0:T(8,128)S(1)}, u32[]{:S(2)}, u32[]{:S(2)}) collective-permute-start(f32[128,128]{1,0:T(8,128)S(1)} %get-tuple-element.174), channel_id=1, source_target_pairs={{0,12},{2,14},{4,8},{6,10},{8,4},{10,6},{12,0},{14,2},{16,28},{18,... | collective-permute-start | bytes 196616 | tf_op jit(solution)/shard_map/ppermute | solution.py:84
  20.4 1.9 %collective-permute-start.7 = (f32[128,128]{1,0:T(8,128)S(1)}, f32[128,128]{1,0:T(8,128)S(1)}, u32[]{:S(2)}, u32[]{:S(2)}) collective-permute-start(f32[128,128]{1,0:T(8,128)S(1)} %get-tuple-element.175), channel_id=1, source_target_pairs={{0,10},{2,8},{4,14},{6,12},{8,2},{10,0},{12,6},{14,4},{16,26},{18,... | collective-permute-start | bytes 196616 | tf_op jit(solution)/shard_map/ppermute | solution.py:84
  22.3 1.0 %shard_map.78 = (bf16[256,512]{1,0:T(8,128)(2,1)S(1)}, bf16[256,512]{1,0:T(8,128)(2,1)S(1)}) custom-call(bf16[256,1024]{1,0:T(8,128)(2,1)} %c_any), custom_call_target="tpu_custom_call" | custom-call | flops 262144 | bytes 1048576 | tf_op jit(solution)/shard_map/pallas_call | solution.py:71
  23.4 1.2 %collective-permute-done.5 = f32[128,128]{1,0:T(8,128)S(1)} collective-permute-done((f32[128,128]{1,0:T(8,128)S(1)}, f32[128,128]{1,0:T(8,128)S(1)}, u32[]{:S(2)}, u32[]{:S(2)}) %collective-permute-start.5) | collective-permute-done | bytes 65568 | tf_op jit(solution)/shard_map/ppermute | solution.py:84
  25.6 1.0 %collective-permute-done.8.prefix_ref = f32[4,128,128]{2,1,0:T(8,128)S(1)} collective-permute-done((f32[4,128,128]{2,1,0:T(8,128)S(1)}, f32[4,128,128]{2,1,0:T(8,128)S(1)}, u32[]{:S(2)}, u32[]{:S(2)}) %collective-permute-start.8) | collective-permute-done | bytes 262176 | tf_op jit(solution)/shard_map/ppermute | solution.py:84
  27.1 1.6 %collective-permute-start.9 = (f32[2,256]{1,0:T(2,128)S(1)}, f32[2,256]{1,0:T(2,128)S(1)}, u32[]{:S(2)}, u32[]{:S(2)}) collective-permute-start(f32[2,256]{1,0:T(2,128)S(1)} %add.132), channel_id=1, source_target_pairs={{0,1},{1,0},{2,3},{3,2},{4,5},{5,4},{6,7},{7,6},{8,9},{9,8},{10,11... | collective-permute-start | bytes 6152 | tf_op jit(solution)/shard_map/ppermute | solution.py:84
  28.7 2.1 %collective-permute-done.9 = f32[2,256]{1,0:T(2,128)S(1)} collective-permute-done((f32[2,256]{1,0:T(2,128)S(1)}, f32[2,256]{1,0:T(2,128)S(1)}, u32[]{:S(2)}, u32[]{:S(2)}) %collective-permute-start.9) | collective-permute-done | bytes 2080 | tf_op jit(solution)/shard_map/ppermute | solution.py:84
  31.7 1.1 %collective-permute-done.10 = f32[4,128,128]{2,1,0:T(8,128)S(1)} collective-permute-done((f32[4,128,128]{2,1,0:T(8,128)S(1)}, f32[4,128,128]{2,1,0:T(8,128)S(1)}, u32[]{:S(2)}, u32[]{:S(2)}) %collective-permute-start.10) | collective-permute-done | bytes 262176 | tf_op jit(solution)/shard_map/ppermute | solution.py:84
  32.9 1.7 %collective-permute-start.11 = (f32[128,128]{1,0:T(8,128)S(1)}, f32[128,128]{1,0:T(8,128)S(1)}, u32[]{:S(2)}, u32[]{:S(2)}) collective-permute-start(f32[128,128]{1,0:T(8,128)S(1)} %get-tuple-element.180), channel_id=1, source_target_pairs={{0,12},{2,14},{4,8},{6,10},{8,4},{10,6},{12,0},{14,2},{16,28},{18,... | collective-permute-start | bytes 196616 | tf_op jit(solution)/shard_map/ppermute | solution.py:84
  35.1 1.1 %collective-permute-start.13 = (f32[128,128]{1,0:T(8,128)S(1)}, f32[128,128]{1,0:T(8,128)S(1)}, u32[]{:S(2)}, u32[]{:S(2)}) collective-permute-start(f32[128,128]{1,0:T(8,128)S(1)} %get-tuple-element.179), channel_id=1, source_target_pairs={{0,10},{2,8},{4,14},{6,12},{8,2},{10,0},{12,6},{14,4},{16,26},{18,... | collective-permute-start | bytes 196616 | tf_op jit(solution)/shard_map/ppermute | solution.py:84
  36.2 2.8 %shard_map.83 = (bf16[256,1024]{1,0:T(8,128)(2,1)}, bf16[256,512]{1,0:T(8,128)(2,1)S(1)}, bf16[256,512]{1,0:T(8,128)(2,1)S(1)}, bf16[256,512]{1,0:T(8,128)(2,1)S(1)}) custom-call(f32[2,256]{1,0:T(2,128)S(1)} %add.133.stats_ref, f32[256,512]{1,0:T(8,128)S(1)} %get-tuple-element.113.mixed_ref.mixed_own_ref, ...), custom_call_target="tpu_custom_call", output_to_operand_aliasing={{1}: (3, {})} | custom-call | flops 335544320 | bytes 4327424 | tf_op jit(solution)/shard_map/pallas_call | solution.py:71
  39.5 2.9 %collective-permute-start.14 = (f32[128,128]{1,0:T(8,128)S(1)}, f32[128,128]{1,0:T(8,128)S(1)}, u32[]{:S(2)}, u32[]{:S(2)}) collective-permute-start(f32[128,128]{1,0:T(8,128)S(1)} %add_add_fusion), channel_id=1, source_target_pairs={{0,16},{2,18},{4,20},{6,22},{8,24},{10,26},{12,28},{14,30},{16,0},... | collective-permute-start | bytes 196616 | tf_op jit(solution)/shard_map/ppermute | solution.py:84
  42.4 2.7 %shard_map.84 = (bf16[256,512]{1,0:T(8,128)(2,1)S(1)}, bf16[256,512]{1,0:T(8,128)(2,1)S(1)}, bf16[256,512]{1,0:T(8,128)(2,1)S(1)}) custom-call(bf16[256,512]{1,0:T(8,128)(2,1)S(1)} %get-tuple-element.128.d_ref, bf16[512,128]{1,0:T(8,128)(2,1)S(1)} %get-tuple-element.129.prefix_ref, bf16[256,1024]{1,0:T(8,128)(2,1)} %q_any.1, ...), custom_call_target="tpu_custom_call", output_to_operand_aliasing={{0}: (0, {})} | custom-call | flops 335544320 | bytes 2752512 | tf_op jit(solution)/shard_map/pallas_call | solution.py:71
  45.1 1.0 %collective-permute-done.14 = f32[128,128]{1,0:T(8,128)S(1)} collective-permute-done((f32[128,128]{1,0:T(8,128)S(1)}, f32[128,128]{1,0:T(8,128)S(1)}, u32[]{:S(2)}, u32[]{:S(2)}) %collective-permute-start.14) | collective-permute-done | bytes 65568 | tf_op jit(solution)/shard_map/ppermute | solution.py:84
  47.0 2.5 %collective-permute-start.17 = (f32[128,128]{1,0:T(8,128)S(1)}, f32[128,128]{1,0:T(8,128)S(1)}, u32[]{:S(2)}, u32[]{:S(2)}) collective-permute-start(f32[128,128]{1,0:T(8,128)S(1)} %get-tuple-element.172), channel_id=1, source_target_pairs={{0,10},{2,8},{4,14},{6,12},{8,2},{10,0},{12,6},{14,4},{16,26},{18,... | collective-permute-start | bytes 196616 | tf_op jit(solution)/shard_map/ppermute | solution.py:84
  49.5 1.4 %shard_map.85 = (bf16[256,1024]{1,0:T(8,128)(2,1)}, bf16[256,512]{1,0:T(8,128)(2,1)S(1)}, bf16[256,512]{1,0:T(8,128)(2,1)S(1)}, bf16[256,512]{1,0:T(8,128)(2,1)S(1)}, bf16[256,512]{1,0:T(8,128)(2,1)S(1)}) custom-call(bf16[256,512]{1,0:T(8,128)(2,1)S(1)} %get-tuple-element.139.own_ref, bf16[256,512]{1,0:T(8,128)(2,1)S(1)} %get-tuple-element.140.away_ref, ...), custom_call_target="tpu_custom_call" | custom-call | flops 262144 | bytes 3145728 | tf_op jit(solution)/shard_map/pallas_call | solution.py:71
  52.5 1.0 %shard_map.86 = (bf16[256,1024]{1,0:T(8,128)(2,1)}, bf16[256,1024]{1,0:T(8,128)(2,1)}) custom-call(bf16[256,512]{1,0:T(8,128)(2,1)S(1)} %get-tuple-element.154.k_ref, bf16[256,512]{1,0:T(8,128)(2,1)S(1)} %get-tuple-element.155.v_ref, bf16[256,512]{1,0:T(8,128)(2,1)S(1)} %get-tuple-element.156.near_k_ref, bf16[256,512]{1,0:T(8,128)(2,1)S(1)} %get-tuple-element.157.near_v_ref, ...), custom_call_target="tpu_custom_call" | custom-call | flops 67108864 | bytes 2359296 | tf_op jit(solution)/shard_map/pallas_call | solution.py:71
  53.9 1.0 %shard_map.87 = (bf16[256,1024]{1,0:T(8,128)(2,1)}, bf16[256,1024]{1,0:T(8,128)(2,1)}) custom-call(bf16[256,512]{1,0:T(8,128)(2,1)S(1)} %get-tuple-element.149.k_ref, bf16[256,512]{1,0:T(8,128)(2,1)S(1)} %get-tuple-element.150.v_ref, bf16[256,512]{1,0:T(8,128)(2,1)S(1)} %get-tuple-element.151.near_k_ref, ...), custom_call_target="tpu_custom_call", output_to_operand_aliasing={{0}: (5, {}), {1}: (6, {})} | custom-call | flops 67108864 | bytes 3407872 | tf_op jit(solution)/shard_map/pallas_call | solution.py:71
  (43 shorter events, 9.7 us)
Async XLA Ops:
  2.2 1.7 %collective-permute-start = (f32[4,128,128]{2,1,0:T(8,128)S(1)}, f32[4,128,128]{2,1,0:T(8,128)S(1)}, u32[]{:S(2)}, u32[]{:S(2)}) collective-permute-start(f32[4,128,128]{2,1,0:T(8,128)S(1)} %get-tuple-element.85), channel_id=1, source_target_pairs={{0,2},{2,0},{4,6},{6,4},{8,10},{10,8},{12,14},{14,12},{16,18},{18,... | collective-permute-start | bytes 786440 | tf_op jit(solution)/shard_map/ppermute | solution.py:84
  3.9 11.0 %copy-start = (bf16[256,1024]{1,0:T(8,128)(2,1)S(1)}, bf16[256,1024]{1,0:T(8,128)(2,1)}, u32[]{:S(2)}) copy-start(bf16[256,1024]{1,0:T(8,128)(2,1)} %q_any.1) | copy-start | bytes 1572868
  4.0 6.4 %collective-permute-start.3 = (f32[128,128]{1,0:T(8,128)S(1)}, f32[128,128]{1,0:T(8,128)S(1)}, u32[]{:S(2)}, u32[]{:S(2)}) collective-permute-start(f32[128,128]{1,0:T(8,128)S(1)} %get-tuple-element.181), channel_id=1, source_target_pairs={{0,12},{2,14},{4,8},{6,10},{8,4},{10,6},{12,0},{14,2},{16,28},{18,... | collective-permute-start | bytes 196616 | tf_op jit(solution)/shard_map/ppermute | solution.py:84
  7.9 4.4 %collective-permute-start.2 = (f32[128,128]{1,0:T(8,128)S(1)}, f32[128,128]{1,0:T(8,128)S(1)}, u32[]{:S(2)}, u32[]{:S(2)}) collective-permute-start(f32[128,128]{1,0:T(8,128)S(1)} %get-tuple-element.182), channel_id=1, source_target_pairs={{0,10},{2,8},{4,14},{6,12},{8,2},{10,0},{12,6},{14,4},{16,26},{18,... | collective-permute-start | bytes 196616 | tf_op jit(solution)/shard_map/ppermute | solution.py:84
  7.9 4.4 %collective-permute-start.1 = (f32[128,128]{1,0:T(8,128)S(1)}, f32[128,128]{1,0:T(8,128)S(1)}, u32[]{:S(2)}, u32[]{:S(2)}) collective-permute-start(f32[128,128]{1,0:T(8,128)S(1)} %get-tuple-element.183), channel_id=1, source_target_pairs={{0,6},{2,4},{4,2},{6,0},{8,14},{10,12},{12,10},{14,8},{16,22},{18,... | collective-permute-start | bytes 196616 | tf_op jit(solution)/shard_map/ppermute | solution.py:84
  12.3 6.6 %collective-permute-start.4 = (f32[128,128]{1,0:T(8,128)S(1)}, f32[128,128]{1,0:T(8,128)S(1)}, u32[]{:S(2)}, u32[]{:S(2)}) collective-permute-start(f32[128,128]{1,0:T(8,128)S(1)} %add_add_fusion.1), channel_id=1, source_target_pairs={{0,16},{2,18},{4,20},{6,22},{8,24},{10,26},{12,28},{14,30},{16,0},... | collective-permute-start | bytes 196616 | tf_op jit(solution)/shard_map/ppermute | solution.py:84
  19.0 5.5 %collective-permute-start.5 = (f32[128,128]{1,0:T(8,128)S(1)}, f32[128,128]{1,0:T(8,128)S(1)}, u32[]{:S(2)}, u32[]{:S(2)}) collective-permute-start(f32[128,128]{1,0:T(8,128)S(1)} %get-tuple-element.174), channel_id=1, source_target_pairs={{0,12},{2,14},{4,8},{6,10},{8,4},{10,6},{12,0},{14,2},{16,28},{18,... | collective-permute-start | bytes 196616 | tf_op jit(solution)/shard_map/ppermute | solution.py:84
  20.1 4.9 %collective-permute-start.6 = (f32[128,128]{1,0:T(8,128)S(1)}, f32[128,128]{1,0:T(8,128)S(1)}, u32[]{:S(2)}, u32[]{:S(2)}) collective-permute-start(f32[128,128]{1,0:T(8,128)S(1)} %get-tuple-element.173), channel_id=1, source_target_pairs={{0,6},{2,4},{4,2},{6,0},{8,14},{10,12},{12,10},{14,8},{16,22},{18,... | collective-permute-start | bytes 196616 | tf_op jit(solution)/shard_map/ppermute | solution.py:84
  20.4 4.6 %collective-permute-start.7 = (f32[128,128]{1,0:T(8,128)S(1)}, f32[128,128]{1,0:T(8,128)S(1)}, u32[]{:S(2)}, u32[]{:S(2)}) collective-permute-start(f32[128,128]{1,0:T(8,128)S(1)} %get-tuple-element.175), channel_id=1, source_target_pairs={{0,10},{2,8},{4,14},{6,12},{8,2},{10,0},{12,6},{14,4},{16,26},{18,... | collective-permute-start | bytes 196616 | tf_op jit(solution)/shard_map/ppermute | solution.py:84
  25.0 1.6 %collective-permute-start.8 = (f32[4,128,128]{2,1,0:T(8,128)S(1)}, f32[4,128,128]{2,1,0:T(8,128)S(1)}, u32[]{:S(2)}, u32[]{:S(2)}) collective-permute-start(f32[4,128,128]{2,1,0:T(8,128)S(1)} %get-tuple-element.166), channel_id=1, source_target_pairs={{0,2},{2,0},{4,6},{6,4},{8,10},{10,8},{12,14},{14,12},{16,18},{18,... | collective-permute-start | bytes 786440 | tf_op jit(solution)/shard_map/ppermute | solution.py:84
  27.1 3.7 %collective-permute-start.9 = (f32[2,256]{1,0:T(2,128)S(1)}, f32[2,256]{1,0:T(2,128)S(1)}, u32[]{:S(2)}, u32[]{:S(2)}) collective-permute-start(f32[2,256]{1,0:T(2,128)S(1)} %add.132), channel_id=1, source_target_pairs={{0,1},{1,0},{2,3},{3,2},{4,5},{5,4},{6,7},{7,6},{8,9},{9,8},{10,11... | collective-permute-start | bytes 6152 | tf_op jit(solution)/shard_map/ppermute | solution.py:84
  31.2 1.6 %collective-permute-start.10 = (f32[4,128,128]{2,1,0:T(8,128)S(1)}, f32[4,128,128]{2,1,0:T(8,128)S(1)}, u32[]{:S(2)}, u32[]{:S(2)}) collective-permute-start(f32[4,128,128]{2,1,0:T(8,128)S(1)} %get-tuple-element.109), channel_id=1, source_target_pairs={{0,2},{2,0},{4,6},{6,4},{8,10},{10,8},{12,14},{14,12},{16,18},{18,... | collective-permute-start | bytes 786440 | tf_op jit(solution)/shard_map/ppermute | solution.py:84
  32.9 6.1 %collective-permute-start.11 = (f32[128,128]{1,0:T(8,128)S(1)}, f32[128,128]{1,0:T(8,128)S(1)}, u32[]{:S(2)}, u32[]{:S(2)}) collective-permute-start(f32[128,128]{1,0:T(8,128)S(1)} %get-tuple-element.180), channel_id=1, source_target_pairs={{0,12},{2,14},{4,8},{6,10},{8,4},{10,6},{12,0},{14,2},{16,28},{18,... | collective-permute-start | bytes 196616 | tf_op jit(solution)/shard_map/ppermute | solution.py:84
  34.6 4.9 %collective-permute-start.12 = (f32[128,128]{1,0:T(8,128)S(1)}, f32[128,128]{1,0:T(8,128)S(1)}, u32[]{:S(2)}, u32[]{:S(2)}) collective-permute-start(f32[128,128]{1,0:T(8,128)S(1)} %get-tuple-element.178), channel_id=1, source_target_pairs={{0,6},{2,4},{4,2},{6,0},{8,14},{10,12},{12,10},{14,8},{16,22},{18,... | collective-permute-start | bytes 196616 | tf_op jit(solution)/shard_map/ppermute | solution.py:84
  35.1 4.4 %collective-permute-start.13 = (f32[128,128]{1,0:T(8,128)S(1)}, f32[128,128]{1,0:T(8,128)S(1)}, u32[]{:S(2)}, u32[]{:S(2)}) collective-permute-start(f32[128,128]{1,0:T(8,128)S(1)} %get-tuple-element.179), channel_id=1, source_target_pairs={{0,10},{2,8},{4,14},{6,12},{8,2},{10,0},{12,6},{14,4},{16,26},{18,... | collective-permute-start | bytes 196616 | tf_op jit(solution)/shard_map/ppermute | solution.py:84
  39.5 6.6 %collective-permute-start.14 = (f32[128,128]{1,0:T(8,128)S(1)}, f32[128,128]{1,0:T(8,128)S(1)}, u32[]{:S(2)}, u32[]{:S(2)}) collective-permute-start(f32[128,128]{1,0:T(8,128)S(1)} %add_add_fusion), channel_id=1, source_target_pairs={{0,16},{2,18},{4,20},{6,22},{8,24},{10,26},{12,28},{14,30},{16,0},... | collective-permute-start | bytes 196616 | tf_op jit(solution)/shard_map/ppermute | solution.py:84
  46.3 5.6 %collective-permute-start.15 = (f32[128,128]{1,0:T(8,128)S(1)}, f32[128,128]{1,0:T(8,128)S(1)}, u32[]{:S(2)}, u32[]{:S(2)}) collective-permute-start(f32[128,128]{1,0:T(8,128)S(1)} %get-tuple-element.171), channel_id=1, source_target_pairs={{0,12},{2,14},{4,8},{6,10},{8,4},{10,6},{12,0},{14,2},{16,28},{18,... | collective-permute-start | bytes 196616 | tf_op jit(solution)/shard_map/ppermute | solution.py:84
  47.0 5.2 %collective-permute-start.16 = (f32[128,128]{1,0:T(8,128)S(1)}, f32[128,128]{1,0:T(8,128)S(1)}, u32[]{:S(2)}, u32[]{:S(2)}) collective-permute-start(f32[128,128]{1,0:T(8,128)S(1)} %get-tuple-element.170), channel_id=1, source_target_pairs={{0,6},{2,4},{4,2},{6,0},{8,14},{10,12},{12,10},{14,8},{16,22},{18,... | collective-permute-start | bytes 196616 | tf_op jit(solution)/shard_map/ppermute | solution.py:84
  47.0 5.2 %collective-permute-start.17 = (f32[128,128]{1,0:T(8,128)S(1)}, f32[128,128]{1,0:T(8,128)S(1)}, u32[]{:S(2)}, u32[]{:S(2)}) collective-permute-start(f32[128,128]{1,0:T(8,128)S(1)} %get-tuple-element.172), channel_id=1, source_target_pairs={{0,10},{2,8},{4,14},{6,12},{8,2},{10,0},{12,6},{14,4},{16,26},{18,... | collective-permute-start | bytes 196616 | tf_op jit(solution)/shard_map/ppermute | solution.py:84
  52.3 1.6 %collective-permute-start.18 = (f32[4,128,128]{2,1,0:T(8,128)S(1)}, f32[4,128,128]{2,1,0:T(8,128)S(1)}, u32[]{:S(2)}, u32[]{:S(2)}) collective-permute-start(f32[4,128,128]{2,1,0:T(8,128)S(1)} %get-tuple-element.163), channel_id=1, source_target_pairs={{0,2},{2,0},{4,6},{6,4},{8,10},{10,8},{12,14},{14,12},{16,18},{18,... | collective-permute-start | bytes 786440 | tf_op jit(solution)/shard_map/ppermute | solution.py:84

commit v5 on v4

--- a/solution.py
+++ b/solution.py
@@ -14,7 +14,7 @@
 OWN, AWAY = 0, 1
 
 PIECES = 4
-ORDER = (2, 1, 3)
+ORDER = {"gather": (1, 2, 3), "back": (2, 1, 3)}
 
 
 def crosses(bits):
@@ -102,7 +102,7 @@
 
     def to_team(pieces, name):
         come = {0: pieces[0]}
-        for r in ORDER:
+        for r in ORDER[name]:
             come[r] = exchange("seq", lambda i: i ^ (2 * r) ^ crosses(r), pieces[r])
         come[r] = beside_of(name, pieces[r], come[r])
         return [come[r] for r in range(PIECES)]
@@ -155,7 +155,7 @@
     wide = like((rows, half_wide))
     states = like((PIECES, half_heads * HEAD_DIM // PIECES, HEAD_DIM))
     spots = [pl.ds(head * HEAD_DIM, HEAD_DIM) for head in range(half_heads)]
-    cuts = 2
+    cuts = 1
     cut_heads = half_heads // cuts
     cut_wide = half_wide // cuts
 
@@ -365,6 +365,9 @@
     _, *near_away = extra["far"]
     grad_q, *known = extra["back"]
 
+    gives = 2
+    give_heads, give_wide = half_heads // gives, half_wide // gives
+
     def last(which, suffix, so_far):
         def kernel(k_ref, v_ref, near_k_ref, near_v_ref, suffix_ref, *refs):
             gk_any, gv_any, gk_ref, gv_ref, sems = refs[len(so_far) :]
@@ -374,10 +377,10 @@
                 state = half.get(suffix_ref, head)
                 gk_ref[:, spot] = (near_k_ref[:, spot] + dot(v_ref[:, spot], state, ((1,), (1,)))).astype(BF16)
                 gv_ref[:, spot] = (near_v_ref[:, spot] + dot(k_ref[:, spot], state, ((1,), (0,)))).astype(BF16)
-                if (head + 1) % cut_heads == 0:
-                    cut = head // cut_heads
-                    here = pl.ds(cut * cut_wide, cut_wide)
-                    there = half.columns(cut * cut_wide, cut_wide)
+                if (head + 1) % give_heads == 0:
+                    cut = head // give_heads
+                    here = pl.ds(cut * give_wide, give_wide)
+                    there = half.columns(cut * give_wide, give_wide)
                     for j, (ref, out) in enumerate(((gk_ref, gk_any), (gv_ref, gv_any))):
                         copies.append(pltpu.make_async_copy(ref.at[:, here], out.at[:, there], sems.at[cut, j]))
                         copies[-1].start()
@@ -391,7 +394,7 @@
             2 * state_flops,
             tuple(5 + i for i in range(len(so_far))),
             (0, 1),
-            [pltpu.VMEM((rows, half_wide), BF16)] * 2 + [pltpu.SemaphoreType.DMA((cuts, 2))],
+            [pltpu.VMEM((rows, half_wide), BF16)] * 2 + [pltpu.SemaphoreType.DMA((gives, 2))],
             {5 + i: i for i in range(len(so_far))},
         )
 

time: 55.2 us -> 55 us (level)
  no operation moved by 1% of the time
where the time goes in v5:
time: 55 us; the launch traced here: 54.8 us
  starting transfers between devices  22.2 us (40%)
  waiting for transfers between devices  17.1 us (31%)
  Pallas kernels  14.3 us (26%)
  between operations  0.82 us (1%)
    ppermute x19, starting transfers between devices, exchange(): lax.ppermute(array, axis, [(i, partner(i)) for i in range(lax.axis_size(a...  22.2 us
    ppermute x19, waiting for transfers between devices, exchange(): lax.ppermute(array, axis, [(i, partner(i)) for i in range(lax.axis_size(a...  17.1 us
    pallas_call x13, Pallas kernels, call(): pl.pallas_call(kernel, out_shape=outs, in_specs=[HBM if i in in_hbm else...  14.3 us
  transfers between devices with their start and end apart: 19, of which 14 were waited for; matrix products, arithmetic and copies ran while one was open for 0% of the time, Pallas kernels for 20%

profile of v5, /device:TPU:0, one launch (start us, length us, event | category | flops | bytes accessed | tf_op | source)
XLA Modules:
  0.0 54.8 jit_solution(17967814974744625236)
XLA Ops:
  0.6 1.4 %shard_map.75 = (bf16[256,512]{1,0:T(8,128)(2,1)S(1)}, bf16[256,512]{1,0:T(8,128)(2,1)S(1)}, bf16[256,512]{1,0:T(8,128)(2,1)S(1)}, bf16[256,512]{1,0:T(8,128)(2,1)S(1)}, f32[4,128,128]{2,1,0:T(8,128)S(1)}) custom-call(bf16[256,1024]{1,0:T(8,128)(2,1)} %k_any.4, bf16[256,1024]{1,0:T(8,128)(2,1)} %v_any.4), custom_call_target="tpu_custom_call" | custom-call | flops 33554432 | bytes 2359296 | tf_op jit(solution)/shard_map/pallas_call | solution.py:71
  3.8 4.0 %collective-permute-start.3 = (f32[128,128]{1,0:T(8,128)S(1)}, f32[128,128]{1,0:T(8,128)S(1)}, u32[]{:S(2)}, u32[]{:S(2)}) collective-permute-start(f32[128,128]{1,0:T(8,128)S(1)} %get-tuple-element.181), channel_id=1, source_target_pairs={{0,12},{2,14},{4,8},{6,10},{8,4},{10,6},{12,0},{14,2},{16,28},{18,... | collective-permute-start | bytes 196616 | tf_op jit(solution)/shard_map/ppermute | solution.py:84
  8.2 2.0 %collective-permute-done.3 = f32[128,128]{1,0:T(8,128)S(1)} collective-permute-done((f32[128,128]{1,0:T(8,128)S(1)}, f32[128,128]{1,0:T(8,128)S(1)}, u32[]{:S(2)}, u32[]{:S(2)}) %collective-permute-start.3) | collective-permute-done | bytes 65568 | tf_op jit(solution)/shard_map/ppermute | solution.py:84
  10.2 2.0 %collective-permute-done.2 = f32[128,128]{1,0:T(8,128)S(1)} collective-permute-done((f32[128,128]{1,0:T(8,128)S(1)}, f32[128,128]{1,0:T(8,128)S(1)}, u32[]{:S(2)}, u32[]{:S(2)}) %collective-permute-start.2) | collective-permute-done | bytes 65568 | tf_op jit(solution)/shard_map/ppermute | solution.py:84
  12.2 2.7 %collective-permute-start.4 = (f32[128,128]{1,0:T(8,128)S(1)}, f32[128,128]{1,0:T(8,128)S(1)}, u32[]{:S(2)}, u32[]{:S(2)}) collective-permute-start(f32[128,128]{1,0:T(8,128)S(1)} %add_add_fusion.1), channel_id=1, source_target_pairs={{0,16},{2,18},{4,20},{6,22},{8,24},{10,26},{12,28},{14,30},{16,0},... | collective-permute-start | bytes 196616 | tf_op jit(solution)/shard_map/ppermute | solution.py:84
  15.8 3.0 %collective-permute-done.4 = f32[128,128]{1,0:T(8,128)S(1)} collective-permute-done((f32[128,128]{1,0:T(8,128)S(1)}, f32[128,128]{1,0:T(8,128)S(1)}, u32[]{:S(2)}, u32[]{:S(2)}) %collective-permute-start.4) | collective-permute-done | bytes 65568 | tf_op jit(solution)/shard_map/ppermute | solution.py:84
  18.9 1.0 %collective-permute-start.5 = (f32[128,128]{1,0:T(8,128)S(1)}, f32[128,128]{1,0:T(8,128)S(1)}, u32[]{:S(2)}, u32[]{:S(2)}) collective-permute-start(f32[128,128]{1,0:T(8,128)S(1)} %get-tuple-element.174), channel_id=1, source_target_pairs={{0,12},{2,14},{4,8},{6,10},{8,4},{10,6},{12,0},{14,2},{16,28},{18,... | collective-permute-start | bytes 196616 | tf_op jit(solution)/shard_map/ppermute | solution.py:84
  20.3 1.9 %collective-permute-start.7 = (f32[128,128]{1,0:T(8,128)S(1)}, f32[128,128]{1,0:T(8,128)S(1)}, u32[]{:S(2)}, u32[]{:S(2)}) collective-permute-start(f32[128,128]{1,0:T(8,128)S(1)} %get-tuple-element.175), channel_id=1, source_target_pairs={{0,10},{2,8},{4,14},{6,12},{8,2},{10,0},{12,6},{14,4},{16,26},{18,... | collective-permute-start | bytes 196616 | tf_op jit(solution)/shard_map/ppermute | solution.py:84
  22.2 1.0 %shard_map.78 = (bf16[256,512]{1,0:T(8,128)(2,1)S(1)}, bf16[256,512]{1,0:T(8,128)(2,1)S(1)}) custom-call(bf16[256,1024]{1,0:T(8,128)(2,1)} %c_any), custom_call_target="tpu_custom_call" | custom-call | flops 262144 | bytes 1048576 | tf_op jit(solution)/shard_map/pallas_call | solution.py:71
  23.2 1.2 %collective-permute-done.5 = f32[128,128]{1,0:T(8,128)S(1)} collective-permute-done((f32[128,128]{1,0:T(8,128)S(1)}, f32[128,128]{1,0:T(8,128)S(1)}, u32[]{:S(2)}, u32[]{:S(2)}) %collective-permute-start.5) | collective-permute-done | bytes 65568 | tf_op jit(solution)/shard_map/ppermute | solution.py:84
  25.5 1.0 %collective-permute-done.8.prefix_ref = f32[4,128,128]{2,1,0:T(8,128)S(1)} collective-permute-done((f32[4,128,128]{2,1,0:T(8,128)S(1)}, f32[4,128,128]{2,1,0:T(8,128)S(1)}, u32[]{:S(2)}, u32[]{:S(2)}) %collective-permute-start.8) | collective-permute-done | bytes 262176 | tf_op jit(solution)/shard_map/ppermute | solution.py:84
  27.0 1.6 %collective-permute-start.9 = (f32[2,256]{1,0:T(2,128)S(1)}, f32[2,256]{1,0:T(2,128)S(1)}, u32[]{:S(2)}, u32[]{:S(2)}) collective-permute-start(f32[2,256]{1,0:T(2,128)S(1)} %add.132), channel_id=1, source_target_pairs={{0,1},{1,0},{2,3},{3,2},{4,5},{5,4},{6,7},{7,6},{8,9},{9,8},{10,11... | collective-permute-start | bytes 6152 | tf_op jit(solution)/shard_map/ppermute | solution.py:84
  28.5 2.1 %collective-permute-done.9 = f32[2,256]{1,0:T(2,128)S(1)} collective-permute-done((f32[2,256]{1,0:T(2,128)S(1)}, f32[2,256]{1,0:T(2,128)S(1)}, u32[]{:S(2)}, u32[]{:S(2)}) %collective-permute-start.9) | collective-permute-done | bytes 2080 | tf_op jit(solution)/shard_map/ppermute | solution.py:84
  31.6 1.1 %collective-permute-done.10 = f32[4,128,128]{2,1,0:T(8,128)S(1)} collective-permute-done((f32[4,128,128]{2,1,0:T(8,128)S(1)}, f32[4,128,128]{2,1,0:T(8,128)S(1)}, u32[]{:S(2)}, u32[]{:S(2)}) %collective-permute-start.10) | collective-permute-done | bytes 262176 | tf_op jit(solution)/shard_map/ppermute | solution.py:84
  32.7 1.7 %collective-permute-start.11 = (f32[128,128]{1,0:T(8,128)S(1)}, f32[128,128]{1,0:T(8,128)S(1)}, u32[]{:S(2)}, u32[]{:S(2)}) collective-permute-start(f32[128,128]{1,0:T(8,128)S(1)} %get-tuple-element.180), channel_id=1, source_target_pairs={{0,12},{2,14},{4,8},{6,10},{8,4},{10,6},{12,0},{14,2},{16,28},{18,... | collective-permute-start | bytes 196616 | tf_op jit(solution)/shard_map/ppermute | solution.py:84
  34.9 1.1 %collective-permute-start.13 = (f32[128,128]{1,0:T(8,128)S(1)}, f32[128,128]{1,0:T(8,128)S(1)}, u32[]{:S(2)}, u32[]{:S(2)}) collective-permute-start(f32[128,128]{1,0:T(8,128)S(1)} %get-tuple-element.179), channel_id=1, source_target_pairs={{0,10},{2,8},{4,14},{6,12},{8,2},{10,0},{12,6},{14,4},{16,26},{18,... | collective-permute-start | bytes 196616 | tf_op jit(solution)/shard_map/ppermute | solution.py:84
  36.0 2.8 %shard_map.83 = (bf16[256,1024]{1,0:T(8,128)(2,1)}, bf16[256,512]{1,0:T(8,128)(2,1)S(1)}, bf16[256,512]{1,0:T(8,128)(2,1)S(1)}, bf16[256,512]{1,0:T(8,128)(2,1)S(1)}) custom-call(f32[2,256]{1,0:T(2,128)S(1)} %add.133.stats_ref, f32[256,512]{1,0:T(8,128)S(1)} %get-tuple-element.113.mixed_ref.mixed_own_ref, ...), custom_call_target="tpu_custom_call", output_to_operand_aliasing={{1}: (3, {})} | custom-call | flops 335544320 | bytes 4327424 | tf_op jit(solution)/shard_map/pallas_call | solution.py:71
  39.4 2.9 %collective-permute-start.14 = (f32[128,128]{1,0:T(8,128)S(1)}, f32[128,128]{1,0:T(8,128)S(1)}, u32[]{:S(2)}, u32[]{:S(2)}) collective-permute-start(f32[128,128]{1,0:T(8,128)S(1)} %add_add_fusion), channel_id=1, source_target_pairs={{0,16},{2,18},{4,20},{6,22},{8,24},{10,26},{12,28},{14,30},{16,0},... | collective-permute-start | bytes 196616 | tf_op jit(solution)/shard_map/ppermute | solution.py:84
  42.2 2.6 %shard_map.84 = (bf16[256,512]{1,0:T(8,128)(2,1)S(1)}, bf16[256,512]{1,0:T(8,128)(2,1)S(1)}, bf16[256,512]{1,0:T(8,128)(2,1)S(1)}) custom-call(bf16[256,512]{1,0:T(8,128)(2,1)S(1)} %get-tuple-element.128.d_ref, bf16[512,128]{1,0:T(8,128)(2,1)S(1)} %get-tuple-element.129.prefix_ref, bf16[256,1024]{1,0:T(8,128)(2,1)} %q_any.1, ...), custom_call_target="tpu_custom_call", output_to_operand_aliasing={{0}: (0, {})} | custom-call | flops 335544320 | bytes 2752512 | tf_op jit(solution)/shard_map/pallas_call | solution.py:71
  44.8 1.2 %collective-permute-done.14 = f32[128,128]{1,0:T(8,128)S(1)} collective-permute-done((f32[128,128]{1,0:T(8,128)S(1)}, f32[128,128]{1,0:T(8,128)S(1)}, u32[]{:S(2)}, u32[]{:S(2)}) %collective-permute-start.14) | collective-permute-done | bytes 65568 | tf_op jit(solution)/shard_map/ppermute | solution.py:84
  46.9 2.5 %collective-permute-start.17 = (f32[128,128]{1,0:T(8,128)S(1)}, f32[128,128]{1,0:T(8,128)S(1)}, u32[]{:S(2)}, u32[]{:S(2)}) collective-permute-start(f32[128,128]{1,0:T(8,128)S(1)} %get-tuple-element.172), channel_id=1, source_target_pairs={{0,10},{2,8},{4,14},{6,12},{8,2},{10,0},{12,6},{14,4},{16,26},{18,... | collective-permute-start | bytes 196616 | tf_op jit(solution)/shard_map/ppermute | solution.py:84
  49.4 1.4 %shard_map.85 = (bf16[256,1024]{1,0:T(8,128)(2,1)}, bf16[256,512]{1,0:T(8,128)(2,1)S(1)}, bf16[256,512]{1,0:T(8,128)(2,1)S(1)}, bf16[256,512]{1,0:T(8,128)(2,1)S(1)}, bf16[256,512]{1,0:T(8,128)(2,1)S(1)}) custom-call(bf16[256,512]{1,0:T(8,128)(2,1)S(1)} %get-tuple-element.139.own_ref, bf16[256,512]{1,0:T(8,128)(2,1)S(1)} %get-tuple-element.140.away_ref, ...), custom_call_target="tpu_custom_call" | custom-call | flops 262144 | bytes 3145728 | tf_op jit(solution)/shard_map/pallas_call | solution.py:71
  52.3 1.0 %shard_map.86 = (bf16[256,1024]{1,0:T(8,128)(2,1)}, bf16[256,1024]{1,0:T(8,128)(2,1)}) custom-call(bf16[256,512]{1,0:T(8,128)(2,1)S(1)} %get-tuple-element.154.k_ref, bf16[256,512]{1,0:T(8,128)(2,1)S(1)} %get-tuple-element.155.v_ref, bf16[256,512]{1,0:T(8,128)(2,1)S(1)} %get-tuple-element.156.near_k_ref, bf16[256,512]{1,0:T(8,128)(2,1)S(1)} %get-tuple-element.157.near_v_ref, ...), custom_call_target="tpu_custom_call" | custom-call | flops 67108864 | bytes 2359296 | tf_op jit(solution)/shard_map/pallas_call | solution.py:71
  53.7 1.0 %shard_map.87 = (bf16[256,1024]{1,0:T(8,128)(2,1)}, bf16[256,1024]{1,0:T(8,128)(2,1)}) custom-call(bf16[256,512]{1,0:T(8,128)(2,1)S(1)} %get-tuple-element.149.k_ref, bf16[256,512]{1,0:T(8,128)(2,1)S(1)} %get-tuple-element.150.v_ref, bf16[256,512]{1,0:T(8,128)(2,1)S(1)} %get-tuple-element.151.near_k_ref, ...), custom_call_target="tpu_custom_call", output_to_operand_aliasing={{0}: (5, {}), {1}: (6, {})} | custom-call | flops 67108864 | bytes 3407872 | tf_op jit(solution)/shard_map/pallas_call | solution.py:71
  (43 shorter events, 9.8 us)
Async XLA Ops:
  2.1 1.7 %collective-permute-start = (f32[4,128,128]{2,1,0:T(8,128)S(1)}, f32[4,128,128]{2,1,0:T(8,128)S(1)}, u32[]{:S(2)}, u32[]{:S(2)}) collective-permute-start(f32[4,128,128]{2,1,0:T(8,128)S(1)} %get-tuple-element.85), channel_id=1, source_target_pairs={{0,2},{2,0},{4,6},{6,4},{8,10},{10,8},{12,14},{14,12},{16,18},{18,... | collective-permute-start | bytes 786440 | tf_op jit(solution)/shard_map/ppermute | solution.py:84
  3.8 11.0 %copy-start = (bf16[256,1024]{1,0:T(8,128)(2,1)S(1)}, bf16[256,1024]{1,0:T(8,128)(2,1)}, u32[]{:S(2)}) copy-start(bf16[256,1024]{1,0:T(8,128)(2,1)} %q_any.1) | copy-start | bytes 1572868
  3.8 6.4 %collective-permute-start.3 = (f32[128,128]{1,0:T(8,128)S(1)}, f32[128,128]{1,0:T(8,128)S(1)}, u32[]{:S(2)}, u32[]{:S(2)}) collective-permute-start(f32[128,128]{1,0:T(8,128)S(1)} %get-tuple-element.181), channel_id=1, source_target_pairs={{0,12},{2,14},{4,8},{6,10},{8,4},{10,6},{12,0},{14,2},{16,28},{18,... | collective-permute-start | bytes 196616 | tf_op jit(solution)/shard_map/ppermute | solution.py:84
  7.8 4.4 %collective-permute-start.2 = (f32[128,128]{1,0:T(8,128)S(1)}, f32[128,128]{1,0:T(8,128)S(1)}, u32[]{:S(2)}, u32[]{:S(2)}) collective-permute-start(f32[128,128]{1,0:T(8,128)S(1)} %get-tuple-element.182), channel_id=1, source_target_pairs={{0,10},{2,8},{4,14},{6,12},{8,2},{10,0},{12,6},{14,4},{16,26},{18,... | collective-permute-start | bytes 196616 | tf_op jit(solution)/shard_map/ppermute | solution.py:84
  7.8 4.4 %collective-permute-start.1 = (f32[128,128]{1,0:T(8,128)S(1)}, f32[128,128]{1,0:T(8,128)S(1)}, u32[]{:S(2)}, u32[]{:S(2)}) collective-permute-start(f32[128,128]{1,0:T(8,128)S(1)} %get-tuple-element.183), channel_id=1, source_target_pairs={{0,6},{2,4},{4,2},{6,0},{8,14},{10,12},{12,10},{14,8},{16,22},{18,... | collective-permute-start | bytes 196616 | tf_op jit(solution)/shard_map/ppermute | solution.py:84
  12.2 6.6 %collective-permute-start.4 = (f32[128,128]{1,0:T(8,128)S(1)}, f32[128,128]{1,0:T(8,128)S(1)}, u32[]{:S(2)}, u32[]{:S(2)}) collective-permute-start(f32[128,128]{1,0:T(8,128)S(1)} %add_add_fusion.1), channel_id=1, source_target_pairs={{0,16},{2,18},{4,20},{6,22},{8,24},{10,26},{12,28},{14,30},{16,0},... | collective-permute-start | bytes 196616 | tf_op jit(solution)/shard_map/ppermute | solution.py:84
  18.9 5.5 %collective-permute-start.5 = (f32[128,128]{1,0:T(8,128)S(1)}, f32[128,128]{1,0:T(8,128)S(1)}, u32[]{:S(2)}, u32[]{:S(2)}) collective-permute-start(f32[128,128]{1,0:T(8,128)S(1)} %get-tuple-element.174), channel_id=1, source_target_pairs={{0,12},{2,14},{4,8},{6,10},{8,4},{10,6},{12,0},{14,2},{16,28},{18,... | collective-permute-start | bytes 196616 | tf_op jit(solution)/shard_map/ppermute | solution.py:84
  19.9 4.9 %collective-permute-start.6 = (f32[128,128]{1,0:T(8,128)S(1)}, f32[128,128]{1,0:T(8,128)S(1)}, u32[]{:S(2)}, u32[]{:S(2)}) collective-permute-start(f32[128,128]{1,0:T(8,128)S(1)} %get-tuple-element.173), channel_id=1, source_target_pairs={{0,6},{2,4},{4,2},{6,0},{8,14},{10,12},{12,10},{14,8},{16,22},{18,... | collective-permute-start | bytes 196616 | tf_op jit(solution)/shard_map/ppermute | solution.py:84
  20.3 4.6 %collective-permute-start.7 = (f32[128,128]{1,0:T(8,128)S(1)}, f32[128,128]{1,0:T(8,128)S(1)}, u32[]{:S(2)}, u32[]{:S(2)}) collective-permute-start(f32[128,128]{1,0:T(8,128)S(1)} %get-tuple-element.175), channel_id=1, source_target_pairs={{0,10},{2,8},{4,14},{6,12},{8,2},{10,0},{12,6},{14,4},{16,26},{18,... | collective-permute-start | bytes 196616 | tf_op jit(solution)/shard_map/ppermute | solution.py:84
  24.9 1.6 %collective-permute-start.8 = (f32[4,128,128]{2,1,0:T(8,128)S(1)}, f32[4,128,128]{2,1,0:T(8,128)S(1)}, u32[]{:S(2)}, u32[]{:S(2)}) collective-permute-start(f32[4,128,128]{2,1,0:T(8,128)S(1)} %get-tuple-element.166), channel_id=1, source_target_pairs={{0,2},{2,0},{4,6},{6,4},{8,10},{10,8},{12,14},{14,12},{16,18},{18,... | collective-permute-start | bytes 786440 | tf_op jit(solution)/shard_map/ppermute | solution.py:84
  27.0 3.7 %collective-permute-start.9 = (f32[2,256]{1,0:T(2,128)S(1)}, f32[2,256]{1,0:T(2,128)S(1)}, u32[]{:S(2)}, u32[]{:S(2)}) collective-permute-start(f32[2,256]{1,0:T(2,128)S(1)} %add.132), channel_id=1, source_target_pairs={{0,1},{1,0},{2,3},{3,2},{4,5},{5,4},{6,7},{7,6},{8,9},{9,8},{10,11... | collective-permute-start | bytes 6152 | tf_op jit(solution)/shard_map/ppermute | solution.py:84
  31.1 1.6 %collective-permute-start.10 = (f32[4,128,128]{2,1,0:T(8,128)S(1)}, f32[4,128,128]{2,1,0:T(8,128)S(1)}, u32[]{:S(2)}, u32[]{:S(2)}) collective-permute-start(f32[4,128,128]{2,1,0:T(8,128)S(1)} %get-tuple-element.109), channel_id=1, source_target_pairs={{0,2},{2,0},{4,6},{6,4},{8,10},{10,8},{12,14},{14,12},{16,18},{18,... | collective-permute-start | bytes 786440 | tf_op jit(solution)/shard_map/ppermute | solution.py:84
  32.7 6.1 %collective-permute-start.11 = (f32[128,128]{1,0:T(8,128)S(1)}, f32[128,128]{1,0:T(8,128)S(1)}, u32[]{:S(2)}, u32[]{:S(2)}) collective-permute-start(f32[128,128]{1,0:T(8,128)S(1)} %get-tuple-element.180), channel_id=1, source_target_pairs={{0,12},{2,14},{4,8},{6,10},{8,4},{10,6},{12,0},{14,2},{16,28},{18,... | collective-permute-start | bytes 196616 | tf_op jit(solution)/shard_map/ppermute | solution.py:84
  34.4 4.9 %collective-permute-start.12 = (f32[128,128]{1,0:T(8,128)S(1)}, f32[128,128]{1,0:T(8,128)S(1)}, u32[]{:S(2)}, u32[]{:S(2)}) collective-permute-start(f32[128,128]{1,0:T(8,128)S(1)} %get-tuple-element.178), channel_id=1, source_target_pairs={{0,6},{2,4},{4,2},{6,0},{8,14},{10,12},{12,10},{14,8},{16,22},{18,... | collective-permute-start | bytes 196616 | tf_op jit(solution)/shard_map/ppermute | solution.py:84
  34.9 4.4 %collective-permute-start.13 = (f32[128,128]{1,0:T(8,128)S(1)}, f32[128,128]{1,0:T(8,128)S(1)}, u32[]{:S(2)}, u32[]{:S(2)}) collective-permute-start(f32[128,128]{1,0:T(8,128)S(1)} %get-tuple-element.179), channel_id=1, source_target_pairs={{0,10},{2,8},{4,14},{6,12},{8,2},{10,0},{12,6},{14,4},{16,26},{18,... | collective-permute-start | bytes 196616 | tf_op jit(solution)/shard_map/ppermute | solution.py:84
  39.4 6.6 %collective-permute-start.14 = (f32[128,128]{1,0:T(8,128)S(1)}, f32[128,128]{1,0:T(8,128)S(1)}, u32[]{:S(2)}, u32[]{:S(2)}) collective-permute-start(f32[128,128]{1,0:T(8,128)S(1)} %add_add_fusion), channel_id=1, source_target_pairs={{0,16},{2,18},{4,20},{6,22},{8,24},{10,26},{12,28},{14,30},{16,0},... | collective-permute-start | bytes 196616 | tf_op jit(solution)/shard_map/ppermute | solution.py:84
  46.1 5.6 %collective-permute-start.15 = (f32[128,128]{1,0:T(8,128)S(1)}, f32[128,128]{1,0:T(8,128)S(1)}, u32[]{:S(2)}, u32[]{:S(2)}) collective-permute-start(f32[128,128]{1,0:T(8,128)S(1)} %get-tuple-element.171), channel_id=1, source_target_pairs={{0,12},{2,14},{4,8},{6,10},{8,4},{10,6},{12,0},{14,2},{16,28},{18,... | collective-permute-start | bytes 196616 | tf_op jit(solution)/shard_map/ppermute | solution.py:84
  46.9 5.2 %collective-permute-start.16 = (f32[128,128]{1,0:T(8,128)S(1)}, f32[128,128]{1,0:T(8,128)S(1)}, u32[]{:S(2)}, u32[]{:S(2)}) collective-permute-start(f32[128,128]{1,0:T(8,128)S(1)} %get-tuple-element.170), channel_id=1, source_target_pairs={{0,6},{2,4},{4,2},{6,0},{8,14},{10,12},{12,10},{14,8},{16,22},{18,... | collective-permute-start | bytes 196616 | tf_op jit(solution)/shard_map/ppermute | solution.py:84
  46.9 5.2 %collective-permute-start.17 = (f32[128,128]{1,0:T(8,128)S(1)}, f32[128,128]{1,0:T(8,128)S(1)}, u32[]{:S(2)}, u32[]{:S(2)}) collective-permute-start(f32[128,128]{1,0:T(8,128)S(1)} %get-tuple-element.172), channel_id=1, source_target_pairs={{0,10},{2,8},{4,14},{6,12},{8,2},{10,0},{12,6},{14,4},{16,26},{18,... | collective-permute-start | bytes 196616 | tf_op jit(solution)/shard_map/ppermute | solution.py:84
  52.1 1.6 %collective-permute-start.18 = (f32[4,128,128]{2,1,0:T(8,128)S(1)}, f32[4,128,128]{2,1,0:T(8,128)S(1)}, u32[]{:S(2)}, u32[]{:S(2)}) collective-permute-start(f32[4,128,128]{2,1,0:T(8,128)S(1)} %get-tuple-element.163), channel_id=1, source_target_pairs={{0,2},{2,0},{4,6},{6,4},{8,10},{10,8},{12,14},{14,12},{16,18},{18,... | collective-permute-start | bytes 786440 | tf_op jit(solution)/shard_map/ppermute | solution.py:84

commit v6 on v5

--- a/solution.py
+++ b/solution.py
@@ -234,8 +234,9 @@
     own, away, extra = scan(keep, send, False, {"far": inner, "back": bring})
     near, cots = extra["far"], extra["back"]
 
-    def mix(which, prefix):
-        def kernel(q_ref, c_ref, near_ref, prefix_ref, mixed_ref, stats_ref, rounded_ref):
+    def mix(which, prefix, so_far):
+        def kernel(q_ref, c_ref, near_ref, prefix_ref, *refs):
+            so_far_refs, (mixed_ref, stats_ref, rounded_ref) = refs[:-3], refs[-3:]
             half = Half(which, heads)
             square = jnp.zeros((rows, HEAD_DIM), F32)
             along = jnp.zeros((rows, HEAD_DIM), F32)
@@ -249,39 +250,42 @@
                 along += c_ref[:, spot].astype(F32) * mixed
             stats_ref[0:1, :] = jnp.sum(square.T, axis=0, keepdims=True)
             stats_ref[1:2, :] = jnp.sum(along.T, axis=0, keepdims=True)
-
-        args = (query, cots[which], near[which], prefix)
+            for ref in so_far_refs:
+                stats_ref[...] += ref[...]
+
+        args = (query, cots[which], near[which], prefix, *([] if so_far is None else [so_far]))
         outs = [wide, like((2, rows)), like((half_wide, HEAD_DIM), BF16)]
         return call(kernel, outs, args, state_flops, alias={2: 0})
 
-    mixed_own, stats_own, prefix_own = mix(OWN, own)
-    mixed_away, stats_away, prefix_away = mix(AWAY, away)
+    mixed_own, stats_own, prefix_own = mix(OWN, own, None)
+    mixed_away, stats, prefix_away = mix(AWAY, away, stats_own)
     mixed = (mixed_own, mixed_away)
-    stats = stats_own + stats_away
     if lax.axis_size("head") == 2:
-        stats = stats + exchange("head", lambda i: 1 - i, stats)
+        sums = (stats, exchange("head", lambda i: 1 - i, stats))
     else:
-        stats = lax.psum(stats, "head")
-
-    def token_scales(stats_ref):
-        rstd = lax.rsqrt(stats_ref[0:1, :] / features + EPS)
-        slope = rstd * rstd * (stats_ref[1:2, :] / features)
+        sums = (lax.psum(stats, "head"),)
+
+    def token_scales(stats_refs):
+        stats = sum(ref[...] for ref in stats_refs)
+        rstd = lax.rsqrt(stats[0:1, :] / features + EPS)
+        slope = rstd * rstd * (stats[1:2, :] / features)
         return (
             jnp.broadcast_to(rstd, (HEAD_DIM, rows)).T,
             jnp.broadcast_to(slope, (HEAD_DIM, rows)).T,
         )
 
     def grads(which):
-        def kernel(q_ref, c_ref, mixed_ref, stats_ref, d_ref, out_ref):
+        def kernel(q_ref, c_ref, mixed_ref, *refs):
+            stats_refs, (d_ref, out_ref) = refs[:-2], refs[-2:]
             half = Half(which, heads)
-            rstd, slope = token_scales(stats_ref)
+            rstd, slope = token_scales(stats_refs)
             for head, spot in enumerate(spots):
                 cols = half.columns(head * HEAD_DIM, HEAD_DIM)
                 d_mixed = (rstd * (c_ref[:, spot].astype(F32) - mixed_ref[:, spot] * slope)).astype(BF16)
                 d_ref[:, spot] = d_mixed
                 half.put(out_ref, head, dot(q_ref[:, cols], d_mixed, ((0,), (0,))))
 
-        return call(kernel, [packed, states], (query, cots[which], mixed[which], stats), state_flops, alias={1: 0})
+        return call(kernel, [packed, states], (query, cots[which], mixed[which], *sums), state_flops, alias={1: 0})
 
     d_away, g_send = grads(AWAY)
     d_own, g_keep = grads(OWN)
@@ -296,15 +300,14 @@
     half_room = pltpu.VMEM((rows, half_wide), BF16)
 
     def middle_own(ready, _):
-        def kernel(
-            stats_ref, mixed_own_ref, mixed_away_ref, d_ref, prefix_ref, q_any, k_any, v_any,
-            out_any, gq_ref, gk_ref, gv_ref, q_ref, k_ref, v_ref, in_sems, out_own_ref, out_away_ref, out_sems,
-        ):
+        def kernel(mixed_own_ref, mixed_away_ref, d_ref, prefix_ref, q_any, k_any, v_any, *refs):
+            stats_refs, refs = refs[: len(sums)], refs[len(sums) :]
+            out_any, gq_ref, gk_ref, gv_ref, q_ref, k_ref, v_ref, in_sems, out_own_ref, out_away_ref, out_sems = refs
             half = Half(OWN, heads)
             copies = loads(half, (q_any, k_any, v_any), (q_ref, k_ref, v_ref), in_sems)
             for part in copies:
                 start(part)
-            rstd, _ = token_scales(stats_ref)
+            rstd, _ = token_scales(stats_refs)
             outs = []
             for which, mixed_ref, out_ref in ((OWN, mixed_own_ref, out_own_ref), (AWAY, mixed_away_ref, out_away_ref)):
                 for spot in spots:
@@ -322,9 +325,9 @@
                 )
             wait(outs)
 
-        args = after(ready, stats, *mixed, d_own, prefix_own, query, key_in, value)
+        args = after(ready, *mixed, d_own, prefix_own, query, key_in, value, *sums)
         scratch = [half_room] * 3 + [pltpu.SemaphoreType.DMA((cuts, 3))] + [half_room] * 2 + [pltpu.SemaphoreType.DMA((2,))]
-        return call(kernel, [whole, packed, packed, packed], args, 5 * block_flops, (5, 6, 7), (0,), scratch, {3: 1})
+        return call(kernel, [whole, packed, packed, packed], args, 5 * block_flops, (4, 5, 6), (0,), scratch, {2: 1})
 
     def middle_away(ready, _):
         def kernel(d_ref, prefix_ref, q_any, k_any, v_any, gq_ref, gk_ref, gv_ref, q_ref, k_ref, v_ref, in_sems):

time: 55 us -> 55 us (level)
  no operation moved by 1% of the time
where the time goes in v6:
time: 55 us; the launch traced here: 54.8 us
  starting transfers between devices  22.2 us (40%)
  waiting for transfers between devices  17.1 us (31%)
  Pallas kernels  14.3 us (26%)
  between operations  0.82 us (1%)
    ppermute x19, starting transfers between devices, exchange(): lax.ppermute(array, axis, [(i, partner(i)) for i in range(lax.axis_size(a...  22.2 us
    ppermute x19, waiting for transfers between devices, exchange(): lax.ppermute(array, axis, [(i, partner(i)) for i in range(lax.axis_size(a...  17.1 us
    pallas_call x13, Pallas kernels, call(): pl.pallas_call(kernel, out_shape=outs, in_specs=[HBM if i in in_hbm else...  14.3 us
  transfers between devices with their start and end apart: 19, of which 14 were waited for; matrix products, arithmetic and copies ran while one was open for 0% of the time, Pallas kernels for 20%

profile of v6, /device:TPU:0, one launch (start us, length us, event | category | flops | bytes accessed | tf_op | source)
XLA Modules:
  0.0 54.8 jit_solution(13190452448943800839)
XLA Ops:
  0.6 1.4 %shard_map.75 = (bf16[256,512]{1,0:T(8,128)(2,1)S(1)}, bf16[256,512]{1,0:T(8,128)(2,1)S(1)}, bf16[256,512]{1,0:T(8,128)(2,1)S(1)}, bf16[256,512]{1,0:T(8,128)(2,1)S(1)}, f32[4,128,128]{2,1,0:T(8,128)S(1)}) custom-call(bf16[256,1024]{1,0:T(8,128)(2,1)} %k_any.4, bf16[256,1024]{1,0:T(8,128)(2,1)} %v_any.4), custom_call_target="tpu_custom_call" | custom-call | flops 33554432 | bytes 2359296 | tf_op jit(solution)/shard_map/pallas_call | solution.py:71
  3.8 4.0 %collective-permute-start.3 = (f32[128,128]{1,0:T(8,128)S(1)}, f32[128,128]{1,0:T(8,128)S(1)}, u32[]{:S(2)}, u32[]{:S(2)}) collective-permute-start(f32[128,128]{1,0:T(8,128)S(1)} %get-tuple-element.183), channel_id=1, source_target_pairs={{0,12},{2,14},{4,8},{6,10},{8,4},{10,6},{12,0},{14,2},{16,28},{18,... | collective-permute-start | bytes 196616 | tf_op jit(solution)/shard_map/ppermute | solution.py:84
  8.2 2.0 %collective-permute-done.3 = f32[128,128]{1,0:T(8,128)S(1)} collective-permute-done((f32[128,128]{1,0:T(8,128)S(1)}, f32[128,128]{1,0:T(8,128)S(1)}, u32[]{:S(2)}, u32[]{:S(2)}) %collective-permute-start.3) | collective-permute-done | bytes 65568 | tf_op jit(solution)/shard_map/ppermute | solution.py:84
  10.2 2.0 %collective-permute-done.2 = f32[128,128]{1,0:T(8,128)S(1)} collective-permute-done((f32[128,128]{1,0:T(8,128)S(1)}, f32[128,128]{1,0:T(8,128)S(1)}, u32[]{:S(2)}, u32[]{:S(2)}) %collective-permute-start.2) | collective-permute-done | bytes 65568 | tf_op jit(solution)/shard_map/ppermute | solution.py:84
  12.2 2.7 %collective-permute-start.4 = (f32[128,128]{1,0:T(8,128)S(1)}, f32[128,128]{1,0:T(8,128)S(1)}, u32[]{:S(2)}, u32[]{:S(2)}) collective-permute-start(f32[128,128]{1,0:T(8,128)S(1)} %add_add_fusion.1), channel_id=1, source_target_pairs={{0,16},{2,18},{4,20},{6,22},{8,24},{10,26},{12,28},{14,30},{16,0},... | collective-permute-start | bytes 196616 | tf_op jit(solution)/shard_map/ppermute | solution.py:84
  15.8 3.0 %collective-permute-done.4 = f32[128,128]{1,0:T(8,128)S(1)} collective-permute-done((f32[128,128]{1,0:T(8,128)S(1)}, f32[128,128]{1,0:T(8,128)S(1)}, u32[]{:S(2)}, u32[]{:S(2)}) %collective-permute-start.4) | collective-permute-done | bytes 65568 | tf_op jit(solution)/shard_map/ppermute | solution.py:84
  18.9 1.0 %collective-permute-start.5 = (f32[128,128]{1,0:T(8,128)S(1)}, f32[128,128]{1,0:T(8,128)S(1)}, u32[]{:S(2)}, u32[]{:S(2)}) collective-permute-start(f32[128,128]{1,0:T(8,128)S(1)} %get-tuple-element.176), channel_id=1, source_target_pairs={{0,12},{2,14},{4,8},{6,10},{8,4},{10,6},{12,0},{14,2},{16,28},{18,... | collective-permute-start | bytes 196616 | tf_op jit(solution)/shard_map/ppermute | solution.py:84
  20.3 1.9 %collective-permute-start.7 = (f32[128,128]{1,0:T(8,128)S(1)}, f32[128,128]{1,0:T(8,128)S(1)}, u32[]{:S(2)}, u32[]{:S(2)}) collective-permute-start(f32[128,128]{1,0:T(8,128)S(1)} %get-tuple-element.177), channel_id=1, source_target_pairs={{0,10},{2,8},{4,14},{6,12},{8,2},{10,0},{12,6},{14,4},{16,26},{18,... | collective-permute-start | bytes 196616 | tf_op jit(solution)/shard_map/ppermute | solution.py:84
  22.2 1.0 %shard_map.78 = (bf16[256,512]{1,0:T(8,128)(2,1)S(1)}, bf16[256,512]{1,0:T(8,128)(2,1)S(1)}) custom-call(bf16[256,1024]{1,0:T(8,128)(2,1)} %c_any), custom_call_target="tpu_custom_call" | custom-call | flops 262144 | bytes 1048576 | tf_op jit(solution)/shard_map/pallas_call | solution.py:71
  23.2 1.2 %collective-permute-done.5 = f32[128,128]{1,0:T(8,128)S(1)} collective-permute-done((f32[128,128]{1,0:T(8,128)S(1)}, f32[128,128]{1,0:T(8,128)S(1)}, u32[]{:S(2)}, u32[]{:S(2)}) %collective-permute-start.5) | collective-permute-done | bytes 65568 | tf_op jit(solution)/shard_map/ppermute | solution.py:84
  25.5 1.0 %collective-permute-done.8.prefix_ref = f32[4,128,128]{2,1,0:T(8,128)S(1)} collective-permute-done((f32[4,128,128]{2,1,0:T(8,128)S(1)}, f32[4,128,128]{2,1,0:T(8,128)S(1)}, u32[]{:S(2)}, u32[]{:S(2)}) %collective-permute-start.8) | collective-permute-done | bytes 262176 | tf_op jit(solution)/shard_map/ppermute | solution.py:84
  27.0 1.6 %collective-permute-start.9 = (f32[2,256]{1,0:T(2,128)S(1)}, f32[2,256]{1,0:T(2,128)S(1)}, u32[]{:S(2)}, u32[]{:S(2)}) collective-permute-start(f32[2,256]{1,0:T(2,128)S(1)} %get-tuple-element.120.refs_0_), channel_id=1, source_target_pairs={{0,1},{1,0},{2,3},{3,2},{4,5},{5,4},{6,7},{7,6},{8,9},{9,8},{10,11... | collective-permute-start | bytes 6152 | tf_op jit(solution)/shard_map/ppermute | solution.py:84
  28.5 2.1 %collective-permute-done.9.refs_1_ = f32[2,256]{1,0:T(2,128)S(1)} collective-permute-done((f32[2,256]{1,0:T(2,128)S(1)}, f32[2,256]{1,0:T(2,128)S(1)}, u32[]{:S(2)}, u32[]{:S(2)}) %collective-permute-start.9) | collective-permute-done | bytes 2080 | tf_op jit(solution)/shard_map/ppermute | solution.py:84
  31.6 1.1 %collective-permute-done.10 = f32[4,128,128]{2,1,0:T(8,128)S(1)} collective-permute-done((f32[4,128,128]{2,1,0:T(8,128)S(1)}, f32[4,128,128]{2,1,0:T(8,128)S(1)}, u32[]{:S(2)}, u32[]{:S(2)}) %collective-permute-start.10) | collective-permute-done | bytes 262176 | tf_op jit(solution)/shard_map/ppermute | solution.py:84
  32.7 1.7 %collective-permute-start.11 = (f32[128,128]{1,0:T(8,128)S(1)}, f32[128,128]{1,0:T(8,128)S(1)}, u32[]{:S(2)}, u32[]{:S(2)}) collective-permute-start(f32[128,128]{1,0:T(8,128)S(1)} %get-tuple-element.182), channel_id=1, source_target_pairs={{0,12},{2,14},{4,8},{6,10},{8,4},{10,6},{12,0},{14,2},{16,28},{18,... | collective-permute-start | bytes 196616 | tf_op jit(solution)/shard_map/ppermute | solution.py:84
  34.9 1.1 %collective-permute-start.13 = (f32[128,128]{1,0:T(8,128)S(1)}, f32[128,128]{1,0:T(8,128)S(1)}, u32[]{:S(2)}, u32[]{:S(2)}) collective-permute-start(f32[128,128]{1,0:T(8,128)S(1)} %get-tuple-element.181), channel_id=1, source_target_pairs={{0,10},{2,8},{4,14},{6,12},{8,2},{10,0},{12,6},{14,4},{16,26},{18,... | collective-permute-start | bytes 196616 | tf_op jit(solution)/shard_map/ppermute | solution.py:84
  36.0 2.8 %shard_map.83 = (bf16[256,1024]{1,0:T(8,128)(2,1)}, bf16[256,512]{1,0:T(8,128)(2,1)S(1)}, bf16[256,512]{1,0:T(8,128)(2,1)S(1)}, bf16[256,512]{1,0:T(8,128)(2,1)S(1)}) custom-call(f32[256,512]{1,0:T(8,128)S(1)} %get-tuple-element.113.mixed_ref.mixed_own_ref, ...), custom_call_target="tpu_custom_call", output_to_operand_aliasing={{1}: (2, {})} | custom-call | flops 335544320 | bytes 4329472 | tf_op jit(solution)/shard_map/pallas_call | solution.py:71
  39.4 2.9 %collective-permute-start.14 = (f32[128,128]{1,0:T(8,128)S(1)}, f32[128,128]{1,0:T(8,128)S(1)}, u32[]{:S(2)}, u32[]{:S(2)}) collective-permute-start(f32[128,128]{1,0:T(8,128)S(1)} %add_add_fusion), channel_id=1, source_target_pairs={{0,16},{2,18},{4,20},{6,22},{8,24},{10,26},{12,28},{14,30},{16,0},... | collective-permute-start | bytes 196616 | tf_op jit(solution)/shard_map/ppermute | solution.py:84
  42.2 2.6 %shard_map.84 = (bf16[256,512]{1,0:T(8,128)(2,1)S(1)}, bf16[256,512]{1,0:T(8,128)(2,1)S(1)}, bf16[256,512]{1,0:T(8,128)(2,1)S(1)}) custom-call(bf16[256,512]{1,0:T(8,128)(2,1)S(1)} %get-tuple-element.130.d_ref, bf16[512,128]{1,0:T(8,128)(2,1)S(1)} %get-tuple-element.131.prefix_ref, bf16[256,1024]{1,0:T(8,128)(2,1)} %q_any.1, ...), custom_call_target="tpu_custom_call", output_to_operand_aliasing={{0}: (0, {})} | custom-call | flops 335544320 | bytes 2752512 | tf_op jit(solution)/shard_map/pallas_call | solution.py:71
  44.8 1.2 %collective-permute-done.14 = f32[128,128]{1,0:T(8,128)S(1)} collective-permute-done((f32[128,128]{1,0:T(8,128)S(1)}, f32[128,128]{1,0:T(8,128)S(1)}, u32[]{:S(2)}, u32[]{:S(2)}) %collective-permute-start.14) | collective-permute-done | bytes 65568 | tf_op jit(solution)/shard_map/ppermute | solution.py:84
  46.9 2.5 %collective-permute-start.17 = (f32[128,128]{1,0:T(8,128)S(1)}, f32[128,128]{1,0:T(8,128)S(1)}, u32[]{:S(2)}, u32[]{:S(2)}) collective-permute-start(f32[128,128]{1,0:T(8,128)S(1)} %get-tuple-element.174), channel_id=1, source_target_pairs={{0,10},{2,8},{4,14},{6,12},{8,2},{10,0},{12,6},{14,4},{16,26},{18,... | collective-permute-start | bytes 196616 | tf_op jit(solution)/shard_map/ppermute | solution.py:84
  49.4 1.4 %shard_map.85 = (bf16[256,1024]{1,0:T(8,128)(2,1)}, bf16[256,512]{1,0:T(8,128)(2,1)S(1)}, bf16[256,512]{1,0:T(8,128)(2,1)S(1)}, bf16[256,512]{1,0:T(8,128)(2,1)S(1)}, bf16[256,512]{1,0:T(8,128)(2,1)S(1)}) custom-call(bf16[256,512]{1,0:T(8,128)(2,1)S(1)} %get-tuple-element.141.own_ref, bf16[256,512]{1,0:T(8,128)(2,1)S(1)} %get-tuple-element.142.away_ref, ...), custom_call_target="tpu_custom_call" | custom-call | flops 262144 | bytes 3145728 | tf_op jit(solution)/shard_map/pallas_call | solution.py:71
  52.3 1.0 %shard_map.86 = (bf16[256,1024]{1,0:T(8,128)(2,1)}, bf16[256,1024]{1,0:T(8,128)(2,1)}) custom-call(bf16[256,512]{1,0:T(8,128)(2,1)S(1)} %get-tuple-element.156.k_ref, bf16[256,512]{1,0:T(8,128)(2,1)S(1)} %get-tuple-element.157.v_ref, bf16[256,512]{1,0:T(8,128)(2,1)S(1)} %get-tuple-element.158.near_k_ref, bf16[256,512]{1,0:T(8,128)(2,1)S(1)} %get-tuple-element.159.near_v_ref, ...), custom_call_target="tpu_custom_call" | custom-call | flops 67108864 | bytes 2359296 | tf_op jit(solution)/shard_map/pallas_call | solution.py:71
  53.7 1.0 %shard_map.87 = (bf16[256,1024]{1,0:T(8,128)(2,1)}, bf16[256,1024]{1,0:T(8,128)(2,1)}) custom-call(bf16[256,512]{1,0:T(8,128)(2,1)S(1)} %get-tuple-element.151.k_ref, bf16[256,512]{1,0:T(8,128)(2,1)S(1)} %get-tuple-element.152.v_ref, bf16[256,512]{1,0:T(8,128)(2,1)S(1)} %get-tuple-element.153.near_k_ref, ...), custom_call_target="tpu_custom_call", output_to_operand_aliasing={{0}: (5, {}), {1}: (6, {})} | custom-call | flops 67108864 | bytes 3407872 | tf_op jit(solution)/shard_map/pallas_call | solution.py:71
  (41 shorter events, 9.8 us)
Async XLA Ops:
  2.1 1.7 %collective-permute-start = (f32[4,128,128]{2,1,0:T(8,128)S(1)}, f32[4,128,128]{2,1,0:T(8,128)S(1)}, u32[]{:S(2)}, u32[]{:S(2)}) collective-permute-start(f32[4,128,128]{2,1,0:T(8,128)S(1)} %get-tuple-element.86), channel_id=1, source_target_pairs={{0,2},{2,0},{4,6},{6,4},{8,10},{10,8},{12,14},{14,12},{16,18},{18,... | collective-permute-start | bytes 786440 | tf_op jit(solution)/shard_map/ppermute | solution.py:84
  3.8 11.0 %copy-start = (bf16[256,1024]{1,0:T(8,128)(2,1)S(1)}, bf16[256,1024]{1,0:T(8,128)(2,1)}, u32[]{:S(2)}) copy-start(bf16[256,1024]{1,0:T(8,128)(2,1)} %q_any.1) | copy-start | bytes 1572868
  3.8 6.4 %collective-permute-start.3 = (f32[128,128]{1,0:T(8,128)S(1)}, f32[128,128]{1,0:T(8,128)S(1)}, u32[]{:S(2)}, u32[]{:S(2)}) collective-permute-start(f32[128,128]{1,0:T(8,128)S(1)} %get-tuple-element.183), channel_id=1, source_target_pairs={{0,12},{2,14},{4,8},{6,10},{8,4},{10,6},{12,0},{14,2},{16,28},{18,... | collective-permute-start | bytes 196616 | tf_op jit(solution)/shard_map/ppermute | solution.py:84
  7.8 4.4 %collective-permute-start.2 = (f32[128,128]{1,0:T(8,128)S(1)}, f32[128,128]{1,0:T(8,128)S(1)}, u32[]{:S(2)}, u32[]{:S(2)}) collective-permute-start(f32[128,128]{1,0:T(8,128)S(1)} %get-tuple-element.184), channel_id=1, source_target_pairs={{0,10},{2,8},{4,14},{6,12},{8,2},{10,0},{12,6},{14,4},{16,26},{18,... | collective-permute-start | bytes 196616 | tf_op jit(solution)/shard_map/ppermute | solution.py:84
  7.8 4.4 %collective-permute-start.1 = (f32[128,128]{1,0:T(8,128)S(1)}, f32[128,128]{1,0:T(8,128)S(1)}, u32[]{:S(2)}, u32[]{:S(2)}) collective-permute-start(f32[128,128]{1,0:T(8,128)S(1)} %get-tuple-element.185), channel_id=1, source_target_pairs={{0,6},{2,4},{4,2},{6,0},{8,14},{10,12},{12,10},{14,8},{16,22},{18,... | collective-permute-start | bytes 196616 | tf_op jit(solution)/shard_map/ppermute | solution.py:84
  12.2 6.6 %collective-permute-start.4 = (f32[128,128]{1,0:T(8,128)S(1)}, f32[128,128]{1,0:T(8,128)S(1)}, u32[]{:S(2)}, u32[]{:S(2)}) collective-permute-start(f32[128,128]{1,0:T(8,128)S(1)} %add_add_fusion.1), channel_id=1, source_target_pairs={{0,16},{2,18},{4,20},{6,22},{8,24},{10,26},{12,28},{14,30},{16,0},... | collective-permute-start | bytes 196616 | tf_op jit(solution)/shard_map/ppermute | solution.py:84
  18.9 5.5 %collective-permute-start.5 = (f32[128,128]{1,0:T(8,128)S(1)}, f32[128,128]{1,0:T(8,128)S(1)}, u32[]{:S(2)}, u32[]{:S(2)}) collective-permute-start(f32[128,128]{1,0:T(8,128)S(1)} %get-tuple-element.176), channel_id=1, source_target_pairs={{0,12},{2,14},{4,8},{6,10},{8,4},{10,6},{12,0},{14,2},{16,28},{18,... | collective-permute-start | bytes 196616 | tf_op jit(solution)/shard_map/ppermute | solution.py:84
  19.9 4.9 %collective-permute-start.6 = (f32[128,128]{1,0:T(8,128)S(1)}, f32[128,128]{1,0:T(8,128)S(1)}, u32[]{:S(2)}, u32[]{:S(2)}) collective-permute-start(f32[128,128]{1,0:T(8,128)S(1)} %get-tuple-element.175), channel_id=1, source_target_pairs={{0,6},{2,4},{4,2},{6,0},{8,14},{10,12},{12,10},{14,8},{16,22},{18,... | collective-permute-start | bytes 196616 | tf_op jit(solution)/shard_map/ppermute | solution.py:84
  20.3 4.6 %collective-permute-start.7 = (f32[128,128]{1,0:T(8,128)S(1)}, f32[128,128]{1,0:T(8,128)S(1)}, u32[]{:S(2)}, u32[]{:S(2)}) collective-permute-start(f32[128,128]{1,0:T(8,128)S(1)} %get-tuple-element.177), channel_id=1, source_target_pairs={{0,10},{2,8},{4,14},{6,12},{8,2},{10,0},{12,6},{14,4},{16,26},{18,... | collective-permute-start | bytes 196616 | tf_op jit(solution)/shard_map/ppermute | solution.py:84
  24.9 1.6 %collective-permute-start.8 = (f32[4,128,128]{2,1,0:T(8,128)S(1)}, f32[4,128,128]{2,1,0:T(8,128)S(1)}, u32[]{:S(2)}, u32[]{:S(2)}) collective-permute-start(f32[4,128,128]{2,1,0:T(8,128)S(1)} %get-tuple-element.168), channel_id=1, source_target_pairs={{0,2},{2,0},{4,6},{6,4},{8,10},{10,8},{12,14},{14,12},{16,18},{18,... | collective-permute-start | bytes 786440 | tf_op jit(solution)/shard_map/ppermute | solution.py:84
  27.0 3.6 %collective-permute-start.9 = (f32[2,256]{1,0:T(2,128)S(1)}, f32[2,256]{1,0:T(2,128)S(1)}, u32[]{:S(2)}, u32[]{:S(2)}) collective-permute-start(f32[2,256]{1,0:T(2,128)S(1)} %get-tuple-element.120.refs_0_), channel_id=1, source_target_pairs={{0,1},{1,0},{2,3},{3,2},{4,5},{5,4},{6,7},{7,6},{8,9},{9,8},{10,11... | collective-permute-start | bytes 6152 | tf_op jit(solution)/shard_map/ppermute | solution.py:84
  31.0 1.6 %collective-permute-start.10 = (f32[4,128,128]{2,1,0:T(8,128)S(1)}, f32[4,128,128]{2,1,0:T(8,128)S(1)}, u32[]{:S(2)}, u32[]{:S(2)}) collective-permute-start(f32[4,128,128]{2,1,0:T(8,128)S(1)} %get-tuple-element.110), channel_id=1, source_target_pairs={{0,2},{2,0},{4,6},{6,4},{8,10},{10,8},{12,14},{14,12},{16,18},{18,... | collective-permute-start | bytes 786440 | tf_op jit(solution)/shard_map/ppermute | solution.py:84
  32.7 6.1 %collective-permute-start.11 = (f32[128,128]{1,0:T(8,128)S(1)}, f32[128,128]{1,0:T(8,128)S(1)}, u32[]{:S(2)}, u32[]{:S(2)}) collective-permute-start(f32[128,128]{1,0:T(8,128)S(1)} %get-tuple-element.182), channel_id=1, source_target_pairs={{0,12},{2,14},{4,8},{6,10},{8,4},{10,6},{12,0},{14,2},{16,28},{18,... | collective-permute-start | bytes 196616 | tf_op jit(solution)/shard_map/ppermute | solution.py:84
  34.4 4.9 %collective-permute-start.12 = (f32[128,128]{1,0:T(8,128)S(1)}, f32[128,128]{1,0:T(8,128)S(1)}, u32[]{:S(2)}, u32[]{:S(2)}) collective-permute-start(f32[128,128]{1,0:T(8,128)S(1)} %get-tuple-element.180), channel_id=1, source_target_pairs={{0,6},{2,4},{4,2},{6,0},{8,14},{10,12},{12,10},{14,8},{16,22},{18,... | collective-permute-start | bytes 196616 | tf_op jit(solution)/shard_map/ppermute | solution.py:84
  34.9 4.4 %collective-permute-start.13 = (f32[128,128]{1,0:T(8,128)S(1)}, f32[128,128]{1,0:T(8,128)S(1)}, u32[]{:S(2)}, u32[]{:S(2)}) collective-permute-start(f32[128,128]{1,0:T(8,128)S(1)} %get-tuple-element.181), channel_id=1, source_target_pairs={{0,10},{2,8},{4,14},{6,12},{8,2},{10,0},{12,6},{14,4},{16,26},{18,... | collective-permute-start | bytes 196616 | tf_op jit(solution)/shard_map/ppermute | solution.py:84
  39.4 6.6 %collective-permute-start.14 = (f32[128,128]{1,0:T(8,128)S(1)}, f32[128,128]{1,0:T(8,128)S(1)}, u32[]{:S(2)}, u32[]{:S(2)}) collective-permute-start(f32[128,128]{1,0:T(8,128)S(1)} %add_add_fusion), channel_id=1, source_target_pairs={{0,16},{2,18},{4,20},{6,22},{8,24},{10,26},{12,28},{14,30},{16,0},... | collective-permute-start | bytes 196616 | tf_op jit(solution)/shard_map/ppermute | solution.py:84
  46.1 5.6 %collective-permute-start.15 = (f32[128,128]{1,0:T(8,128)S(1)}, f32[128,128]{1,0:T(8,128)S(1)}, u32[]{:S(2)}, u32[]{:S(2)}) collective-permute-start(f32[128,128]{1,0:T(8,128)S(1)} %get-tuple-element.173), channel_id=1, source_target_pairs={{0,12},{2,14},{4,8},{6,10},{8,4},{10,6},{12,0},{14,2},{16,28},{18,... | collective-permute-start | bytes 196616 | tf_op jit(solution)/shard_map/ppermute | solution.py:84
  46.9 5.2 %collective-permute-start.16 = (f32[128,128]{1,0:T(8,128)S(1)}, f32[128,128]{1,0:T(8,128)S(1)}, u32[]{:S(2)}, u32[]{:S(2)}) collective-permute-start(f32[128,128]{1,0:T(8,128)S(1)} %get-tuple-element.172), channel_id=1, source_target_pairs={{0,6},{2,4},{4,2},{6,0},{8,14},{10,12},{12,10},{14,8},{16,22},{18,... | collective-permute-start | bytes 196616 | tf_op jit(solution)/shard_map/ppermute | solution.py:84
  46.9 5.2 %collective-permute-start.17 = (f32[128,128]{1,0:T(8,128)S(1)}, f32[128,128]{1,0:T(8,128)S(1)}, u32[]{:S(2)}, u32[]{:S(2)}) collective-permute-start(f32[128,128]{1,0:T(8,128)S(1)} %get-tuple-element.174), channel_id=1, source_target_pairs={{0,10},{2,8},{4,14},{6,12},{8,2},{10,0},{12,6},{14,4},{16,26},{18,... | collective-permute-start | bytes 196616 | tf_op jit(solution)/shard_map/ppermute | solution.py:84
  52.1 1.6 %collective-permute-start.18 = (f32[4,128,128]{2,1,0:T(8,128)S(1)}, f32[4,128,128]{2,1,0:T(8,128)S(1)}, u32[]{:S(2)}, u32[]{:S(2)}) collective-permute-start(f32[4,128,128]{2,1,0:T(8,128)S(1)} %get-tuple-element.165), channel_id=1, source_target_pairs={{0,2},{2,0},{4,6},{6,4},{8,10},{10,8},{12,14},{14,12},{16,18},{18,... | collective-permute-start | bytes 786440 | tf_op jit(solution)/shard_map/ppermute | solution.py:84

commit v7 on v6

--- a/solution.py
+++ b/solution.py
@@ -248,8 +248,12 @@
                 mixed_ref[:, spot] = mixed
                 square += mixed * mixed
                 along += c_ref[:, spot].astype(F32) * mixed
-            stats_ref[0:1, :] = jnp.sum(square.T, axis=0, keepdims=True)
-            stats_ref[1:2, :] = jnp.sum(along.T, axis=0, keepdims=True)
+            fold = HEAD_DIM // 2
+            left = lax.broadcasted_iota(jnp.int32, (rows, HEAD_DIM), 1) < fold
+            both = jnp.where(left, square, along) + pltpu.roll(jnp.where(left, along, square), fold, 1)
+            both = both.T
+            stats_ref[0:1, :] = jnp.sum(both[:fold], axis=0, keepdims=True)
+            stats_ref[1:2, :] = jnp.sum(both[fold:], axis=0, keepdims=True)
             for ref in so_far_refs:
                 stats_ref[...] += ref[...]
 

time: 55 us -> 55 us (level)
  no operation moved by 1% of the time
where the time goes in v7:
time: 55 us; the launch traced here: 54.8 us
  starting transfers between devices  22.2 us (40%)
  waiting for transfers between devices  17 us (31%)
  Pallas kernels  14.4 us (26%)
  between operations  0.82 us (1%)
    ppermute x19, starting transfers between devices, exchange(): lax.ppermute(array, axis, [(i, partner(i)) for i in range(lax.axis_size(a...  22.2 us
    ppermute x19, waiting for transfers between devices, exchange(): lax.ppermute(array, axis, [(i, partner(i)) for i in range(lax.axis_size(a...  17 us
    pallas_call x13, Pallas kernels, call(): pl.pallas_call(kernel, out_shape=outs, in_specs=[HBM if i in in_hbm else...  14.4 us
  transfers between devices with their start and end apart: 19, of which 14 were waited for; matrix products, arithmetic and copies ran while one was open for 0% of the time, Pallas kernels for 20%

profile of v7, /device:TPU:0, one launch (start us, length us, event | category | flops | bytes accessed | tf_op | source)
XLA Modules:
  0.0 54.8 jit_solution(14307449550767444443)
XLA Ops:
  0.6 1.4 %shard_map.75 = (bf16[256,512]{1,0:T(8,128)(2,1)S(1)}, bf16[256,512]{1,0:T(8,128)(2,1)S(1)}, bf16[256,512]{1,0:T(8,128)(2,1)S(1)}, bf16[256,512]{1,0:T(8,128)(2,1)S(1)}, f32[4,128,128]{2,1,0:T(8,128)S(1)}) custom-call(bf16[256,1024]{1,0:T(8,128)(2,1)} %k_any.4, bf16[256,1024]{1,0:T(8,128)(2,1)} %v_any.4), custom_call_target="tpu_custom_call" | custom-call | flops 33554432 | bytes 2359296 | tf_op jit(solution)/shard_map/pallas_call | solution.py:71
  3.8 4.0 %collective-permute-start.3 = (f32[128,128]{1,0:T(8,128)S(1)}, f32[128,128]{1,0:T(8,128)S(1)}, u32[]{:S(2)}, u32[]{:S(2)}) collective-permute-start(f32[128,128]{1,0:T(8,128)S(1)} %get-tuple-element.183), channel_id=1, source_target_pairs={{0,12},{2,14},{4,8},{6,10},{8,4},{10,6},{12,0},{14,2},{16,28},{18,... | collective-permute-start | bytes 196616 | tf_op jit(solution)/shard_map/ppermute | solution.py:84
  8.2 2.0 %collective-permute-done.3 = f32[128,128]{1,0:T(8,128)S(1)} collective-permute-done((f32[128,128]{1,0:T(8,128)S(1)}, f32[128,128]{1,0:T(8,128)S(1)}, u32[]{:S(2)}, u32[]{:S(2)}) %collective-permute-start.3) | collective-permute-done | bytes 65568 | tf_op jit(solution)/shard_map/ppermute | solution.py:84
  10.2 2.0 %collective-permute-done.2 = f32[128,128]{1,0:T(8,128)S(1)} collective-permute-done((f32[128,128]{1,0:T(8,128)S(1)}, f32[128,128]{1,0:T(8,128)S(1)}, u32[]{:S(2)}, u32[]{:S(2)}) %collective-permute-start.2) | collective-permute-done | bytes 65568 | tf_op jit(solution)/shard_map/ppermute | solution.py:84
  12.2 2.7 %collective-permute-start.4 = (f32[128,128]{1,0:T(8,128)S(1)}, f32[128,128]{1,0:T(8,128)S(1)}, u32[]{:S(2)}, u32[]{:S(2)}) collective-permute-start(f32[128,128]{1,0:T(8,128)S(1)} %add_add_fusion.1), channel_id=1, source_target_pairs={{0,16},{2,18},{4,20},{6,22},{8,24},{10,26},{12,28},{14,30},{16,0},... | collective-permute-start | bytes 196616 | tf_op jit(solution)/shard_map/ppermute | solution.py:84
  14.8 0.9 %shard_map.77 = (f32[256,512]{1,0:T(8,128)S(1)}, f32[256,512]{1,0:T(8,128)S(1)}) custom-call(bf16[256,1024]{1,0:T(8,128)(2,1)S(1)} %copy-done, bf16[256,512]{1,0:T(8,128)(2,1)S(1)} %get-tuple-element.90.k_ref.refs_0_, bf16[256,512]{1,0:T(8,128)(2,1)S(1)} %get-tuple-element.91.refs_1_, bf16[256,512]{1,0:T(8,128)(2,1)S(1)} %get-tuple-element.92.v_ref.refs_2_, ...), custom_call_target="tpu_custom_call" | custom-call | flops 268435456 | bytes 2621440 | tf_op jit(solution)/shard_map/pallas_call | solution.py:71
  15.8 3.0 %collective-permute-done.4 = f32[128,128]{1,0:T(8,128)S(1)} collective-permute-done((f32[128,128]{1,0:T(8,128)S(1)}, f32[128,128]{1,0:T(8,128)S(1)}, u32[]{:S(2)}, u32[]{:S(2)}) %collective-permute-start.4) | collective-permute-done | bytes 65568 | tf_op jit(solution)/shard_map/ppermute | solution.py:84
  18.9 1.0 %collective-permute-start.5 = (f32[128,128]{1,0:T(8,128)S(1)}, f32[128,128]{1,0:T(8,128)S(1)}, u32[]{:S(2)}, u32[]{:S(2)}) collective-permute-start(f32[128,128]{1,0:T(8,128)S(1)} %get-tuple-element.176), channel_id=1, source_target_pairs={{0,12},{2,14},{4,8},{6,10},{8,4},{10,6},{12,0},{14,2},{16,28},{18,... | collective-permute-start | bytes 196616 | tf_op jit(solution)/shard_map/ppermute | solution.py:84
  20.3 1.9 %collective-permute-start.7 = (f32[128,128]{1,0:T(8,128)S(1)}, f32[128,128]{1,0:T(8,128)S(1)}, u32[]{:S(2)}, u32[]{:S(2)}) collective-permute-start(f32[128,128]{1,0:T(8,128)S(1)} %get-tuple-element.177), channel_id=1, source_target_pairs={{0,10},{2,8},{4,14},{6,12},{8,2},{10,0},{12,6},{14,4},{16,26},{18,... | collective-permute-start | bytes 196616 | tf_op jit(solution)/shard_map/ppermute | solution.py:84
  22.2 1.0 %shard_map.78 = (bf16[256,512]{1,0:T(8,128)(2,1)S(1)}, bf16[256,512]{1,0:T(8,128)(2,1)S(1)}) custom-call(bf16[256,1024]{1,0:T(8,128)(2,1)} %c_any), custom_call_target="tpu_custom_call" | custom-call | flops 262144 | bytes 1048576 | tf_op jit(solution)/shard_map/pallas_call | solution.py:71
  23.2 1.2 %collective-permute-done.5 = f32[128,128]{1,0:T(8,128)S(1)} collective-permute-done((f32[128,128]{1,0:T(8,128)S(1)}, f32[128,128]{1,0:T(8,128)S(1)}, u32[]{:S(2)}, u32[]{:S(2)}) %collective-permute-start.5) | collective-permute-done | bytes 65568 | tf_op jit(solution)/shard_map/ppermute | solution.py:84
  27.0 1.6 %collective-permute-start.9 = (f32[2,256]{1,0:T(2,128)S(1)}, f32[2,256]{1,0:T(2,128)S(1)}, u32[]{:S(2)}, u32[]{:S(2)}) collective-permute-start(f32[2,256]{1,0:T(2,128)S(1)} %get-tuple-element.120.refs_0_), channel_id=1, source_target_pairs={{0,1},{1,0},{2,3},{3,2},{4,5},{5,4},{6,7},{7,6},{8,9},{9,8},{10,11... | collective-permute-start | bytes 6152 | tf_op jit(solution)/shard_map/ppermute | solution.py:84
  28.5 2.1 %collective-permute-done.9.refs_1_ = f32[2,256]{1,0:T(2,128)S(1)} collective-permute-done((f32[2,256]{1,0:T(2,128)S(1)}, f32[2,256]{1,0:T(2,128)S(1)}, u32[]{:S(2)}, u32[]{:S(2)}) %collective-permute-start.9) | collective-permute-done | bytes 2080 | tf_op jit(solution)/shard_map/ppermute | solution.py:84
  31.5 1.1 %collective-permute-done.10 = f32[4,128,128]{2,1,0:T(8,128)S(1)} collective-permute-done((f32[4,128,128]{2,1,0:T(8,128)S(1)}, f32[4,128,128]{2,1,0:T(8,128)S(1)}, u32[]{:S(2)}, u32[]{:S(2)}) %collective-permute-start.10) | collective-permute-done | bytes 262176 | tf_op jit(solution)/shard_map/ppermute | solution.py:84
  32.7 1.7 %collective-permute-start.11 = (f32[128,128]{1,0:T(8,128)S(1)}, f32[128,128]{1,0:T(8,128)S(1)}, u32[]{:S(2)}, u32[]{:S(2)}) collective-permute-start(f32[128,128]{1,0:T(8,128)S(1)} %get-tuple-element.182), channel_id=1, source_target_pairs={{0,12},{2,14},{4,8},{6,10},{8,4},{10,6},{12,0},{14,2},{16,28},{18,... | collective-permute-start | bytes 196616 | tf_op jit(solution)/shard_map/ppermute | solution.py:84
  34.9 1.1 %collective-permute-start.13 = (f32[128,128]{1,0:T(8,128)S(1)}, f32[128,128]{1,0:T(8,128)S(1)}, u32[]{:S(2)}, u32[]{:S(2)}) collective-permute-start(f32[128,128]{1,0:T(8,128)S(1)} %get-tuple-element.181), channel_id=1, source_target_pairs={{0,10},{2,8},{4,14},{6,12},{8,2},{10,0},{12,6},{14,4},{16,26},{18,... | collective-permute-start | bytes 196616 | tf_op jit(solution)/shard_map/ppermute | solution.py:84
  36.0 2.8 %shard_map.83 = (bf16[256,1024]{1,0:T(8,128)(2,1)}, bf16[256,512]{1,0:T(8,128)(2,1)S(1)}, bf16[256,512]{1,0:T(8,128)(2,1)S(1)}, bf16[256,512]{1,0:T(8,128)(2,1)S(1)}) custom-call(f32[256,512]{1,0:T(8,128)S(1)} %get-tuple-element.113.mixed_ref.mixed_own_ref, ...), custom_call_target="tpu_custom_call", output_to_operand_aliasing={{1}: (2, {})} | custom-call | flops 335544320 | bytes 4329472 | tf_op jit(solution)/shard_map/pallas_call | solution.py:71
  39.4 2.9 %collective-permute-start.14 = (f32[128,128]{1,0:T(8,128)S(1)}, f32[128,128]{1,0:T(8,128)S(1)}, u32[]{:S(2)}, u32[]{:S(2)}) collective-permute-start(f32[128,128]{1,0:T(8,128)S(1)} %add_add_fusion), channel_id=1, source_target_pairs={{0,16},{2,18},{4,20},{6,22},{8,24},{10,26},{12,28},{14,30},{16,0},... | collective-permute-start | bytes 196616 | tf_op jit(solution)/shard_map/ppermute | solution.py:84
  42.2 2.6 %shard_map.84 = (bf16[256,512]{1,0:T(8,128)(2,1)S(1)}, bf16[256,512]{1,0:T(8,128)(2,1)S(1)}, bf16[256,512]{1,0:T(8,128)(2,1)S(1)}) custom-call(bf16[256,512]{1,0:T(8,128)(2,1)S(1)} %get-tuple-element.130.d_ref, bf16[512,128]{1,0:T(8,128)(2,1)S(1)} %get-tuple-element.131.prefix_ref, bf16[256,1024]{1,0:T(8,128)(2,1)} %q_any.1, ...), custom_call_target="tpu_custom_call", output_to_operand_aliasing={{0}: (0, {})} | custom-call | flops 335544320 | bytes 2752512 | tf_op jit(solution)/shard_map/pallas_call | solution.py:71
  44.8 1.2 %collective-permute-done.14 = f32[128,128]{1,0:T(8,128)S(1)} collective-permute-done((f32[128,128]{1,0:T(8,128)S(1)}, f32[128,128]{1,0:T(8,128)S(1)}, u32[]{:S(2)}, u32[]{:S(2)}) %collective-permute-start.14) | collective-permute-done | bytes 65568 | tf_op jit(solution)/shard_map/ppermute | solution.py:84
  46.9 2.5 %collective-permute-start.17 = (f32[128,128]{1,0:T(8,128)S(1)}, f32[128,128]{1,0:T(8,128)S(1)}, u32[]{:S(2)}, u32[]{:S(2)}) collective-permute-start(f32[128,128]{1,0:T(8,128)S(1)} %get-tuple-element.174), channel_id=1, source_target_pairs={{0,10},{2,8},{4,14},{6,12},{8,2},{10,0},{12,6},{14,4},{16,26},{18,... | collective-permute-start | bytes 196616 | tf_op jit(solution)/shard_map/ppermute | solution.py:84
  49.3 1.4 %shard_map.85 = (bf16[256,1024]{1,0:T(8,128)(2,1)}, bf16[256,512]{1,0:T(8,128)(2,1)S(1)}, bf16[256,512]{1,0:T(8,128)(2,1)S(1)}, bf16[256,512]{1,0:T(8,128)(2,1)S(1)}, bf16[256,512]{1,0:T(8,128)(2,1)S(1)}) custom-call(bf16[256,512]{1,0:T(8,128)(2,1)S(1)} %get-tuple-element.141.own_ref, bf16[256,512]{1,0:T(8,128)(2,1)S(1)} %get-tuple-element.142.away_ref, ...), custom_call_target="tpu_custom_call" | custom-call | flops 262144 | bytes 3145728 | tf_op jit(solution)/shard_map/pallas_call | solution.py:71
  52.3 1.0 %shard_map.86 = (bf16[256,1024]{1,0:T(8,128)(2,1)}, bf16[256,1024]{1,0:T(8,128)(2,1)}) custom-call(bf16[256,512]{1,0:T(8,128)(2,1)S(1)} %get-tuple-element.156.k_ref, bf16[256,512]{1,0:T(8,128)(2,1)S(1)} %get-tuple-element.157.v_ref, bf16[256,512]{1,0:T(8,128)(2,1)S(1)} %get-tuple-element.158.near_k_ref, bf16[256,512]{1,0:T(8,128)(2,1)S(1)} %get-tuple-element.159.near_v_ref, ...), custom_call_target="tpu_custom_call" | custom-call | flops 67108864 | bytes 2359296 | tf_op jit(solution)/shard_map/pallas_call | solution.py:71
  53.7 1.0 %shard_map.87 = (bf16[256,1024]{1,0:T(8,128)(2,1)}, bf16[256,1024]{1,0:T(8,128)(2,1)}) custom-call(bf16[256,512]{1,0:T(8,128)(2,1)S(1)} %get-tuple-element.151.k_ref, bf16[256,512]{1,0:T(8,128)(2,1)S(1)} %get-tuple-element.152.v_ref, bf16[256,512]{1,0:T(8,128)(2,1)S(1)} %get-tuple-element.153.near_k_ref, ...), custom_call_target="tpu_custom_call", output_to_operand_aliasing={{0}: (5, {}), {1}: (6, {})} | custom-call | flops 67108864 | bytes 3407872 | tf_op jit(solution)/shard_map/pallas_call | solution.py:71
  (41 shorter events, 9.8 us)
Async XLA Ops:
  2.1 1.7 %collective-permute-start = (f32[4,128,128]{2,1,0:T(8,128)S(1)}, f32[4,128,128]{2,1,0:T(8,128)S(1)}, u32[]{:S(2)}, u32[]{:S(2)}) collective-permute-start(f32[4,128,128]{2,1,0:T(8,128)S(1)} %get-tuple-element.86), channel_id=1, source_target_pairs={{0,2},{2,0},{4,6},{6,4},{8,10},{10,8},{12,14},{14,12},{16,18},{18,... | collective-permute-start | bytes 786440 | tf_op jit(solution)/shard_map/ppermute | solution.py:84
  3.8 11.0 %copy-start = (bf16[256,1024]{1,0:T(8,128)(2,1)S(1)}, bf16[256,1024]{1,0:T(8,128)(2,1)}, u32[]{:S(2)}) copy-start(bf16[256,1024]{1,0:T(8,128)(2,1)} %q_any.1) | copy-start | bytes 1572868
  3.8 6.4 %collective-permute-start.3 = (f32[128,128]{1,0:T(8,128)S(1)}, f32[128,128]{1,0:T(8,128)S(1)}, u32[]{:S(2)}, u32[]{:S(2)}) collective-permute-start(f32[128,128]{1,0:T(8,128)S(1)} %get-tuple-element.183), channel_id=1, source_target_pairs={{0,12},{2,14},{4,8},{6,10},{8,4},{10,6},{12,0},{14,2},{16,28},{18,... | collective-permute-start | bytes 196616 | tf_op jit(solution)/shard_map/ppermute | solution.py:84
  7.8 4.4 %collective-permute-start.2 = (f32[128,128]{1,0:T(8,128)S(1)}, f32[128,128]{1,0:T(8,128)S(1)}, u32[]{:S(2)}, u32[]{:S(2)}) collective-permute-start(f32[128,128]{1,0:T(8,128)S(1)} %get-tuple-element.184), channel_id=1, source_target_pairs={{0,10},{2,8},{4,14},{6,12},{8,2},{10,0},{12,6},{14,4},{16,26},{18,... | collective-permute-start | bytes 196616 | tf_op jit(solution)/shard_map/ppermute | solution.py:84
  7.8 4.4 %collective-permute-start.1 = (f32[128,128]{1,0:T(8,128)S(1)}, f32[128,128]{1,0:T(8,128)S(1)}, u32[]{:S(2)}, u32[]{:S(2)}) collective-permute-start(f32[128,128]{1,0:T(8,128)S(1)} %get-tuple-element.185), channel_id=1, source_target_pairs={{0,6},{2,4},{4,2},{6,0},{8,14},{10,12},{12,10},{14,8},{16,22},{18,... | collective-permute-start | bytes 196616 | tf_op jit(solution)/shard_map/ppermute | solution.py:84
  12.2 6.6 %collective-permute-start.4 = (f32[128,128]{1,0:T(8,128)S(1)}, f32[128,128]{1,0:T(8,128)S(1)}, u32[]{:S(2)}, u32[]{:S(2)}) collective-permute-start(f32[128,128]{1,0:T(8,128)S(1)} %add_add_fusion.1), channel_id=1, source_target_pairs={{0,16},{2,18},{4,20},{6,22},{8,24},{10,26},{12,28},{14,30},{16,0},... | collective-permute-start | bytes 196616 | tf_op jit(solution)/shard_map/ppermute | solution.py:84
  18.9 5.5 %collective-permute-start.5 = (f32[128,128]{1,0:T(8,128)S(1)}, f32[128,128]{1,0:T(8,128)S(1)}, u32[]{:S(2)}, u32[]{:S(2)}) collective-permute-start(f32[128,128]{1,0:T(8,128)S(1)} %get-tuple-element.176), channel_id=1, source_target_pairs={{0,12},{2,14},{4,8},{6,10},{8,4},{10,6},{12,0},{14,2},{16,28},{18,... | collective-permute-start | bytes 196616 | tf_op jit(solution)/shard_map/ppermute | solution.py:84
  19.9 4.9 %collective-permute-start.6 = (f32[128,128]{1,0:T(8,128)S(1)}, f32[128,128]{1,0:T(8,128)S(1)}, u32[]{:S(2)}, u32[]{:S(2)}) collective-permute-start(f32[128,128]{1,0:T(8,128)S(1)} %get-tuple-element.175), channel_id=1, source_target_pairs={{0,6},{2,4},{4,2},{6,0},{8,14},{10,12},{12,10},{14,8},{16,22},{18,... | collective-permute-start | bytes 196616 | tf_op jit(solution)/shard_map/ppermute | solution.py:84
  20.3 4.6 %collective-permute-start.7 = (f32[128,128]{1,0:T(8,128)S(1)}, f32[128,128]{1,0:T(8,128)S(1)}, u32[]{:S(2)}, u32[]{:S(2)}) collective-permute-start(f32[128,128]{1,0:T(8,128)S(1)} %get-tuple-element.177), channel_id=1, source_target_pairs={{0,10},{2,8},{4,14},{6,12},{8,2},{10,0},{12,6},{14,4},{16,26},{18,... | collective-permute-start | bytes 196616 | tf_op jit(solution)/shard_map/ppermute | solution.py:84
  24.9 1.6 %collective-permute-start.8 = (f32[4,128,128]{2,1,0:T(8,128)S(1)}, f32[4,128,128]{2,1,0:T(8,128)S(1)}, u32[]{:S(2)}, u32[]{:S(2)}) collective-permute-start(f32[4,128,128]{2,1,0:T(8,128)S(1)} %get-tuple-element.168), channel_id=1, source_target_pairs={{0,2},{2,0},{4,6},{6,4},{8,10},{10,8},{12,14},{14,12},{16,18},{18,... | collective-permute-start | bytes 786440 | tf_op jit(solution)/shard_map/ppermute | solution.py:84
  27.0 3.6 %collective-permute-start.9 = (f32[2,256]{1,0:T(2,128)S(1)}, f32[2,256]{1,0:T(2,128)S(1)}, u32[]{:S(2)}, u32[]{:S(2)}) collective-permute-start(f32[2,256]{1,0:T(2,128)S(1)} %get-tuple-element.120.refs_0_), channel_id=1, source_target_pairs={{0,1},{1,0},{2,3},{3,2},{4,5},{5,4},{6,7},{7,6},{8,9},{9,8},{10,11... | collective-permute-start | bytes 6152 | tf_op jit(solution)/shard_map/ppermute | solution.py:84
  31.0 1.6 %collective-permute-start.10 = (f32[4,128,128]{2,1,0:T(8,128)S(1)}, f32[4,128,128]{2,1,0:T(8,128)S(1)}, u32[]{:S(2)}, u32[]{:S(2)}) collective-permute-start(f32[4,128,128]{2,1,0:T(8,128)S(1)} %get-tuple-element.110), channel_id=1, source_target_pairs={{0,2},{2,0},{4,6},{6,4},{8,10},{10,8},{12,14},{14,12},{16,18},{18,... | collective-permute-start | bytes 786440 | tf_op jit(solution)/shard_map/ppermute | solution.py:84
  32.7 6.1 %collective-permute-start.11 = (f32[128,128]{1,0:T(8,128)S(1)}, f32[128,128]{1,0:T(8,128)S(1)}, u32[]{:S(2)}, u32[]{:S(2)}) collective-permute-start(f32[128,128]{1,0:T(8,128)S(1)} %get-tuple-element.182), channel_id=1, source_target_pairs={{0,12},{2,14},{4,8},{6,10},{8,4},{10,6},{12,0},{14,2},{16,28},{18,... | collective-permute-start | bytes 196616 | tf_op jit(solution)/shard_map/ppermute | solution.py:84
  34.4 4.9 %collective-permute-start.12 = (f32[128,128]{1,0:T(8,128)S(1)}, f32[128,128]{1,0:T(8,128)S(1)}, u32[]{:S(2)}, u32[]{:S(2)}) collective-permute-start(f32[128,128]{1,0:T(8,128)S(1)} %get-tuple-element.180), channel_id=1, source_target_pairs={{0,6},{2,4},{4,2},{6,0},{8,14},{10,12},{12,10},{14,8},{16,22},{18,... | collective-permute-start | bytes 196616 | tf_op jit(solution)/shard_map/ppermute | solution.py:84
  34.9 4.4 %collective-permute-start.13 = (f32[128,128]{1,0:T(8,128)S(1)}, f32[128,128]{1,0:T(8,128)S(1)}, u32[]{:S(2)}, u32[]{:S(2)}) collective-permute-start(f32[128,128]{1,0:T(8,128)S(1)} %get-tuple-element.181), channel_id=1, source_target_pairs={{0,10},{2,8},{4,14},{6,12},{8,2},{10,0},{12,6},{14,4},{16,26},{18,... | collective-permute-start | bytes 196616 | tf_op jit(solution)/shard_map/ppermute | solution.py:84
  39.4 6.6 %collective-permute-start.14 = (f32[128,128]{1,0:T(8,128)S(1)}, f32[128,128]{1,0:T(8,128)S(1)}, u32[]{:S(2)}, u32[]{:S(2)}) collective-permute-start(f32[128,128]{1,0:T(8,128)S(1)} %add_add_fusion), channel_id=1, source_target_pairs={{0,16},{2,18},{4,20},{6,22},{8,24},{10,26},{12,28},{14,30},{16,0},... | collective-permute-start | bytes 196616 | tf_op jit(solution)/shard_map/ppermute | solution.py:84
  46.1 5.6 %collective-permute-start.15 = (f32[128,128]{1,0:T(8,128)S(1)}, f32[128,128]{1,0:T(8,128)S(1)}, u32[]{:S(2)}, u32[]{:S(2)}) collective-permute-start(f32[128,128]{1,0:T(8,128)S(1)} %get-tuple-element.173), channel_id=1, source_target_pairs={{0,12},{2,14},{4,8},{6,10},{8,4},{10,6},{12,0},{14,2},{16,28},{18,... | collective-permute-start | bytes 196616 | tf_op jit(solution)/shard_map/ppermute | solution.py:84
  46.8 5.2 %collective-permute-start.16 = (f32[128,128]{1,0:T(8,128)S(1)}, f32[128,128]{1,0:T(8,128)S(1)}, u32[]{:S(2)}, u32[]{:S(2)}) collective-permute-start(f32[128,128]{1,0:T(8,128)S(1)} %get-tuple-element.172), channel_id=1, source_target_pairs={{0,6},{2,4},{4,2},{6,0},{8,14},{10,12},{12,10},{14,8},{16,22},{18,... | collective-permute-start | bytes 196616 | tf_op jit(solution)/shard_map/ppermute | solution.py:84
  46.9 5.2 %collective-permute-start.17 = (f32[128,128]{1,0:T(8,128)S(1)}, f32[128,128]{1,0:T(8,128)S(1)}, u32[]{:S(2)}, u32[]{:S(2)}) collective-permute-start(f32[128,128]{1,0:T(8,128)S(1)} %get-tuple-element.174), channel_id=1, source_target_pairs={{0,10},{2,8},{4,14},{6,12},{8,2},{10,0},{12,6},{14,4},{16,26},{18,... | collective-permute-start | bytes 196616 | tf_op jit(solution)/shard_map/ppermute | solution.py:84
  52.1 1.6 %collective-permute-start.18 = (f32[4,128,128]{2,1,0:T(8,128)S(1)}, f32[4,128,128]{2,1,0:T(8,128)S(1)}, u32[]{:S(2)}, u32[]{:S(2)}) collective-permute-start(f32[4,128,128]{2,1,0:T(8,128)S(1)} %get-tuple-element.165), channel_id=1, source_target_pairs={{0,2},{2,0},{4,6},{6,4},{8,10},{10,8},{12,14},{14,12},{16,18},{18,... | collective-permute-start | bytes 786440 | tf_op jit(solution)/shard_map/ppermute | solution.py:84
